TPU v7x, 512 devices: a whole 4x8x8 slice. The times are simulated.
512 devices in a mesh: slab: 64 (over y_lo, z, core), fsdp: 8 (over x, y_hi).
Axes of the slice: x: 4, y: 8 (y_hi: 2, y_lo: 4; y = y_hi * 4 + y_lo), z: 8, core: 2. Of those that a mesh axis runs over, the one named last changes fastest.
Arguments:
- queries: bfloat16 [14336, 2048], P('slab', 'fsdp'), may hold values from -160 to 160
- key_rows: bfloat16 [14336, 2048], P('slab', 'fsdp'), may hold values from -5 to 5
- value_rows: bfloat16 [14336, 2048], P('slab', 'fsdp'), may hold values from -6 to 6
- extents: int32 [16, 3], P('fsdp'), may hold values from 0 to 1, as said below
- out_weight: bfloat16 [2048, 3072], P('slab', 'fsdp'), may hold values from -6 to 6
- gate_scale: float32 [3072], P('fsdp'), may hold values from 0.5 to 2
Outputs:
- mixed: bfloat16 [14336, 3072], P('slab', 'fsdp')
Inputs may be any that keep to these rules, and one draw needn't show every extreme that they name: `extents`: each entry is 0 or 1, and in every draw some head has 1 in all three.
All inputs are finite; a program needn't handle non-finite values.
Results may differ from a plain program's by a relative error of at most 0.011.
Values may be sent and summed in bfloat16 or wider, within the bound.
No kernel may reach another device: no remote copies, remote signals or barrier semaphores. Data moves between devices by JAX's collectives and lax.ppermute only.
A program may use at most 64 MiB of HBM per device.

v0:
```python
import math

import jax
import jax.numpy as jnp
from jax import lax
from jax.sharding import PartitionSpec as P

HD = 128
ST = 4
SH = 4


def passed_along(value, axis, steps):
    count = lax.axis_size(axis)
    leading, last = (max(0, -steps), min(count, count - steps))
    return lax.ppermute(value, axis, [(source, source + steps) for source in range(leading, last)])


def window_mask(extents, time_step, height_step, width_step, valid):
    head_ok = (
        (abs(time_step) <= extents[:, 0])
        & (abs(height_step) <= extents[:, 1])
        & (abs(width_step) <= extents[:, 2])
        & valid
    )
    return head_ok[:, None, None]


def online_step(state, queries_heads, key_block, value_block, allowed):
    running_max, running_sum, accum = state
    head_count = queries_heads.shape[1]
    key_heads = key_block.reshape(key_block.shape[0], head_count, HD)
    value_heads = value_block.reshape(value_block.shape[0], head_count, HD)
    scores = jnp.einsum(
        "qhd,khd->hqk", queries_heads, key_heads, preferred_element_type=jnp.float32
    ) * (1.0 / math.sqrt(HD))
    scores = jnp.where(allowed, scores, -jnp.inf)
    new_max = jnp.maximum(running_max, jnp.max(scores, axis=2))
    factor = jnp.exp(running_max - new_max)
    weights = jnp.exp(scores - new_max[:, :, None])
    running_sum = running_sum * factor + jnp.sum(weights, axis=2)
    rounded = weights.astype(jnp.bfloat16)
    accum = accum * jnp.transpose(factor)[:, :, None] + jnp.einsum(
        "hqk,khd->qhd", rounded, value_heads, preferred_element_type=jnp.float32
    )
    return (new_max, running_sum, accum)


def local(queries, key_rows, value_rows, extents, out_weight, gate_scale):
    row_count = queries.shape[0]
    head_count = extents.shape[0]
    width_groups = lax.axis_size("slab") // (ST * SH)
    slab_index = lax.axis_index("slab")
    time_pos = slab_index // (SH * width_groups)
    height_pos = slab_index // width_groups % SH
    width_pos = slab_index % width_groups
    queries_heads = queries.reshape(row_count, head_count, HD)
    width_steps = (-1, 0, 1)
    neighbours = {(0, 0, 0): (key_rows, value_rows)}
    others = [
        (ts, hs, ws)
        for ts in (-1, 0, 1)
        for hs in (-1, 0, 1)
        for ws in width_steps
        if ts != 0 or hs != 0 or ws != 0
    ]
    for time_step, height_step, width_step in others:
        offset_tiles = time_step * SH * width_groups + height_step * width_groups + width_step
        neighbours[time_step, height_step, width_step] = passed_along(
            (key_rows, value_rows), "slab", -offset_tiles
        )
    state = (
        jnp.full((head_count, row_count), -jnp.inf, jnp.float32),
        jnp.zeros((head_count, row_count), jnp.float32),
        jnp.zeros((row_count, head_count, HD), jnp.float32),
    )
    for time_step, height_step, width_step in [(0, 0, 0)] + others:
        valid = (
            (time_pos + time_step >= 0)
            & (time_pos + time_step < ST)
            & (height_pos + height_step >= 0)
            & (height_pos + height_step < SH)
            & (width_pos + width_step >= 0)
            & (width_pos + width_step < width_groups)
        )
        allowed = window_mask(extents, time_step, height_step, width_step, valid)
        block_pair = neighbours[time_step, height_step, width_step]
        state = online_step(state, queries_heads, block_pair[0], block_pair[1], allowed)
    attended = (
        (state[2] / jnp.transpose(state[1])[:, :, None])
        .astype(jnp.bfloat16)
        .reshape(row_count, head_count * HD)
    )
    every_head = lax.all_gather(attended, "fsdp", axis=1, tiled=True)
    projection = jnp.dot(
        every_head,
        lax.all_gather(out_weight, "slab", axis=0, tiled=True),
        preferred_element_type=jnp.float32,
    )
    return (projection * gate_scale[None, :]).astype(jnp.bfloat16)


def solution(mesh):
    in_specs = (
        P("slab", "fsdp"),
        P("slab", "fsdp"),
        P("slab", "fsdp"),
        P("fsdp", None),
        P("slab", "fsdp"),
        P("fsdp"),
    )
    out_specs = P("slab", "fsdp")
    return jax.shard_map(local, mesh=mesh, in_specs=in_specs, out_specs=out_specs, check_vma=False)
```

profile of v0, /device:TPU:80, one launch (start us, length us, event | category | flops | bytes accessed | tf_op | source)
XLA Modules:
  0.0 294.6 jit_solution(4534099314262138642)
XLA Ops:
  6.5 3.7 %collective-permute-start.38 = (bf16[224,256]{1,0:T(8,128)(2,1)}, bf16[224,256]{1,0:T(8,128)(2,1)S(1)}, u32[]{:S(2)}, u32[]{:S(2)}) collective-permute-start(bf16[224,256]{1,0:T(8,128)(2,1)} %param.7), channel_id=1, source_target_pairs={{104,0},{112,8},{120,16},{128,24},{136,32},{144,40},{152,48},{160,... | collective-permute-start | bytes 344072 | tf_op jit(solution)/shard_map/ppermute | solution.py:16
  10.3 8.4 %collective-permute-start.34 = (bf16[224,256]{1,0:T(8,128)(2,1)}, bf16[224,256]{1,0:T(8,128)(2,1)S(1)}, u32[]{:S(2)}, u32[]{:S(2)}) collective-permute-start(bf16[224,256]{1,0:T(8,128)(2,1)} %param.7), channel_id=1, source_target_pairs={{88,0},{96,8},{104,16},{112,24},{120,32},{128,40},{136,48},{144,56... | collective-permute-start | bytes 344072 | tf_op jit(solution)/shard_map/ppermute | solution.py:16
  18.7 1.9 collective-permute-start.16
  20.6 4.9 %collective-permute-start.12 = (bf16[224,256]{1,0:T(8,128)(2,1)}, bf16[224,256]{1,0:T(8,128)(2,1)S(1)}, u32[]{:S(2)}, u32[]{:S(2)}) collective-permute-start(bf16[224,256]{1,0:T(8,128)(2,1)} %param.7), channel_id=1, source_target_pairs={{0,104},{8,112},{16,120},{24,128},{32,136},{40,144},{48,152},{56,1... | collective-permute-start | bytes 344072 | tf_op jit(solution)/shard_map/ppermute | solution.py:16
  25.5 1.9 collective-permute-start.4
  27.6 0.9 and_and_fusion
  28.5 0.8 fusion.392
  29.5 1.2 fusion.394
  31.6 1.9 collective-permute-start
  33.8 7.1 %collective-permute-start.36 = (bf16[224,256]{1,0:T(8,128)(2,1)S(1)}, bf16[224,256]{1,0:T(8,128)(2,1)S(1)}, u32[]{:S(2)}, u32[]{:S(2)}) collective-permute-start(bf16[224,256]{1,0:T(8,128)(2,1)S(1)} %copy-done.2), channel_id=1, source_target_pairs={{96,0},{104,8},{112,16},{120,24},{128,32},{136,40},{144,48},{152,5... | collective-permute-start | bytes 344072 | tf_op jit(solution)/shard_map/ppermute | solution.py:16
  41.2 1.9 collective-permute-start.14
  43.4 1.9 collective-permute-start.2
  45.6 4.6 %collective-permute-start.32 = (bf16[224,256]{1,0:T(8,128)(2,1)S(1)}, bf16[224,256]{1,0:T(8,128)(2,1)S(1)}, u32[]{:S(2)}, u32[]{:S(2)}) collective-permute-start(bf16[224,256]{1,0:T(8,128)(2,1)S(1)} %copy-done.2), channel_id=1, source_target_pairs={{40,0},{48,8},{56,16},{64,24},{72,32},{80,40},{88,48},{96,56},{104... | collective-permute-start | bytes 344072 | tf_op jit(solution)/shard_map/ppermute | solution.py:16
  50.5 2.8 collective-permute-done
  53.3 1.9 collective-permute-start.28
  55.5 9.1 %collective-permute-done.36 = bf16[224,256]{1,0:T(8,128)(2,1)S(1)} collective-permute-done((bf16[224,256]{1,0:T(8,128)(2,1)S(1)}, bf16[224,256]{1,0:T(8,128)(2,1)S(1)}, u32[]{:S(2)}, u32[]{:S(2)}) %collective-permute-start.36) | collective-permute-done | bytes 114720 | tf_op jit(solution)/shard_map/ppermute | solution.py:16
  64.5 1.9 collective-permute-start.22
  66.7 1.9 collective-permute-start.18
  68.9 1.9 collective-permute-start.40
  71.1 4.5 %collective-permute-start.10 = (bf16[224,256]{1,0:T(8,128)(2,1)S(1)}, bf16[224,256]{1,0:T(8,128)(2,1)S(1)}, u32[]{:S(2)}, u32[]{:S(2)}) collective-permute-start(bf16[224,256]{1,0:T(8,128)(2,1)S(1)} %copy-done.2), channel_id=1, source_target_pairs={{0,120},{8,128},{16,136},{24,144},{32,152},{40,160},{48,168},{56,1... | collective-permute-start | bytes 344072 | tf_op jit(solution)/shard_map/ppermute | solution.py:16
  76.0 1.9 collective-permute-start.6
  78.2 2.6 collective-permute-start.42
  81.3 6.8 %collective-permute-start.30 = (bf16[224,256]{1,0:T(8,128)(2,1)S(1)}, bf16[224,256]{1,0:T(8,128)(2,1)S(1)}, u32[]{:S(2)}, u32[]{:S(2)}) collective-permute-start(bf16[224,256]{1,0:T(8,128)(2,1)S(1)} %copy-done.2), channel_id=1, source_target_pairs={{32,0},{40,8},{48,16},{56,24},{64,32},{72,40},{80,48},{88,56},{96,... | collective-permute-start | bytes 344072 | tf_op jit(solution)/shard_map/ppermute | solution.py:16
  88.4 3.3 %collective-permute-start.26 = (bf16[224,256]{1,0:T(8,128)(2,1)S(1)}, bf16[224,256]{1,0:T(8,128)(2,1)S(1)}, u32[]{:S(2)}, u32[]{:S(2)}) collective-permute-start(bf16[224,256]{1,0:T(8,128)(2,1)S(1)} %copy-done.2), channel_id=1, source_target_pairs={{8,0},{16,8},{24,16},{32,24},{40,32},{48,40},{56,48},{64,56},{72,6... | collective-permute-start | bytes 344072 | tf_op jit(solution)/shard_map/ppermute | solution.py:16
  92.0 1.9 collective-permute-start.24
  94.2 1.9 collective-permute-start.20
  96.5 1.9 collective-permute-start.8
  98.7 9.1 %collective-permute-start.50 = (bf16[224,256]{1,0:T(8,128)(2,1)S(1)}, bf16[224,256]{1,0:T(8,128)(2,1)S(1)}, u32[]{:S(2)}, u32[]{:S(2)}) collective-permute-start(bf16[224,256]{1,0:T(8,128)(2,1)S(1)} %copy-done.2), channel_id=1, source_target_pairs={{168,0},{176,8},{184,16},{192,24},{200,32},{208,40},{216,48},{224,... | collective-permute-start | bytes 344072 | tf_op jit(solution)/shard_map/ppermute | solution.py:16
  108.1 1.9 collective-permute-start.46
  110.3 1.9 collective-permute-start.48
  112.5 1.9 collective-permute-start.44
  114.7 3.9 %collective-permute-start.1 = (bf16[224,256]{1,0:T(8,128)(2,1)S(1)}, bf16[224,256]{1,0:T(8,128)(2,1)S(1)}, u32[]{:S(2)}, u32[]{:S(2)}) collective-permute-start(bf16[224,256]{1,0:T(8,128)(2,1)S(1)} %copy-done.1), channel_id=1, source_target_pairs={{0,168},{8,176},{16,184},{24,192},{32,200},{40,208},{48,216},{56,2... | collective-permute-start | bytes 344072 | tf_op jit(solution)/shard_map/ppermute | solution.py:16
  119.3 2.1 collective-permute-start.3
  121.7 0.7 collective-permute-done.46
  122.4 1.9 collective-permute-start.5
  124.9 1.9 collective-permute-start.7
  127.1 1.9 collective-permute-start.9
  131.9 3.1 %collective-permute-start.11 = (bf16[224,256]{1,0:T(8,128)(2,1)S(1)}, bf16[224,256]{1,0:T(8,128)(2,1)S(1)}, u32[]{:S(2)}, u32[]{:S(2)}) collective-permute-start(bf16[224,256]{1,0:T(8,128)(2,1)S(1)} %copy-done.1), channel_id=1, source_target_pairs={{0,120},{8,128},{16,136},{24,144},{32,152},{40,160},{48,168},{56,1... | collective-permute-start | bytes 344072 | tf_op jit(solution)/shard_map/ppermute | solution.py:16
  135.4 6.1 %collective-permute-start.13 = (bf16[224,256]{1,0:T(8,128)(2,1)S(1)}, bf16[224,256]{1,0:T(8,128)(2,1)S(1)}, u32[]{:S(2)}, u32[]{:S(2)}) collective-permute-start(bf16[224,256]{1,0:T(8,128)(2,1)S(1)} %copy-done.1), channel_id=1, source_target_pairs={{0,104},{8,112},{16,120},{24,128},{32,136},{40,144},{48,152},{56,1... | collective-permute-start | bytes 344072 | tf_op jit(solution)/shard_map/ppermute | solution.py:16
  141.8 2.6 collective-permute-start.15
  144.8 1.9 collective-permute-start.17
  147.0 5.3 %collective-permute-start.19 = (bf16[224,256]{1,0:T(8,128)(2,1)S(1)}, bf16[224,256]{1,0:T(8,128)(2,1)S(1)}, u32[]{:S(2)}, u32[]{:S(2)}) collective-permute-start(bf16[224,256]{1,0:T(8,128)(2,1)S(1)} %copy-done.1), channel_id=1, source_target_pairs={{0,40},{8,48},{16,56},{24,64},{32,72},{40,80},{48,88},{56,96},{64,... | collective-permute-start | bytes 344072 | tf_op jit(solution)/shard_map/ppermute | solution.py:16
  152.6 2.5 collective-permute-start.21
  155.5 1.9 collective-permute-start.23
  157.7 4.9 %collective-permute-start.25 = (bf16[224,256]{1,0:T(8,128)(2,1)S(1)}, bf16[224,256]{1,0:T(8,128)(2,1)S(1)}, u32[]{:S(2)}, u32[]{:S(2)}) collective-permute-start(bf16[224,256]{1,0:T(8,128)(2,1)S(1)} %copy-done.1), channel_id=1, source_target_pairs={{0,8},{8,16},{16,24},{24,32},{32,40},{40,48},{48,56},{56,64},{64,7... | collective-permute-start | bytes 344072 | tf_op jit(solution)/shard_map/ppermute | solution.py:16
  163.0 3.5 %collective-permute-start.27 = (bf16[224,256]{1,0:T(8,128)(2,1)S(1)}, bf16[224,256]{1,0:T(8,128)(2,1)S(1)}, u32[]{:S(2)}, u32[]{:S(2)}) collective-permute-start(bf16[224,256]{1,0:T(8,128)(2,1)S(1)} %copy-done.1), channel_id=1, source_target_pairs={{8,0},{16,8},{24,16},{32,24},{40,32},{48,40},{56,48},{64,56},{72,6... | collective-permute-start | bytes 344072 | tf_op jit(solution)/shard_map/ppermute | solution.py:16
  166.9 5.2 %collective-permute-start.29 = (bf16[224,256]{1,0:T(8,128)(2,1)S(1)}, bf16[224,256]{1,0:T(8,128)(2,1)S(1)}, u32[]{:S(2)}, u32[]{:S(2)}) collective-permute-start(bf16[224,256]{1,0:T(8,128)(2,1)S(1)} %copy-done.1), channel_id=1, source_target_pairs={{24,0},{32,8},{40,16},{48,24},{56,32},{64,40},{72,48},{80,56},{88,... | collective-permute-start | bytes 344072 | tf_op jit(solution)/shard_map/ppermute | solution.py:16
  172.4 4.5 %collective-permute-start.31 = (bf16[224,256]{1,0:T(8,128)(2,1)S(1)}, bf16[224,256]{1,0:T(8,128)(2,1)S(1)}, u32[]{:S(2)}, u32[]{:S(2)}) collective-permute-start(bf16[224,256]{1,0:T(8,128)(2,1)S(1)} %copy-done.1), channel_id=1, source_target_pairs={{32,0},{40,8},{48,16},{56,24},{64,32},{72,40},{80,48},{88,56},{96,... | collective-permute-start | bytes 344072 | tf_op jit(solution)/shard_map/ppermute | solution.py:16
  177.3 1.9 collective-permute-start.33
  179.5 5.1 %collective-permute-start.35 = (bf16[224,256]{1,0:T(8,128)(2,1)S(1)}, bf16[224,256]{1,0:T(8,128)(2,1)S(1)}, u32[]{:S(2)}, u32[]{:S(2)}) collective-permute-start(bf16[224,256]{1,0:T(8,128)(2,1)S(1)} %copy-done.1), channel_id=1, source_target_pairs={{88,0},{96,8},{104,16},{112,24},{120,32},{128,40},{136,48},{144,56... | collective-permute-start | bytes 344072 | tf_op jit(solution)/shard_map/ppermute | solution.py:16
  184.9 1.9 collective-permute-start.37
  187.2 1.9 collective-permute-start.39
  189.4 1.9 collective-permute-start.41
  191.7 2.6 collective-permute-start.43
  194.6 2.8 collective-permute-start.45
  197.7 0.7 collective-permute-done.37
  198.5 2.6 collective-permute-start.47
  201.9 2.8 collective-permute-start.49
  205.0 1.9 collective-permute-start.51
  208.1 12.2 %collective-permute-done.47 = bf16[224,256]{1,0:T(8,128)(2,1)S(1)} collective-permute-done((bf16[224,256]{1,0:T(8,128)(2,1)S(1)}, bf16[224,256]{1,0:T(8,128)(2,1)S(1)}, u32[]{:S(2)}, u32[]{:S(2)}) %collective-permute-start.47) | collective-permute-done | bytes 114720 | tf_op jit(solution)/shard_map/ppermute | solution.py:16
  220.7 2.1 collective-permute-done.49
  223.1 8.6 %collective-permute-done.51 = bf16[224,256]{1,0:T(8,128)(2,1)S(1)} collective-permute-done((bf16[224,256]{1,0:T(8,128)(2,1)S(1)}, bf16[224,256]{1,0:T(8,128)(2,1)S(1)}, u32[]{:S(2)}, u32[]{:S(2)}) %collective-permute-start.51) | collective-permute-done | bytes 114720 | tf_op jit(solution)/shard_map/ppermute | solution.py:16
  232.1 52.9 %all_gather.6 = bf16[224,2048]{1,0:T(8,128)(2,1)S(1)} all-gather(bf16[224,256]{1,0:T(8,128)(2,1)S(1)} %bitcast.1167), channel_id=1, replica_groups=mesh['slab'=64,'fsdp'=8] {'fsdp'}, dimensions={1}, use_global_device_ids=true | all-gather | bytes 1032192 | tf_op jit(solution)/shard_map/all_gather | solution.py:94
  285.0 2.7 fusion.27
  (133 shorter events, 20.3 us)
Async XLA Ops:
  6.5 23.0 %copy-start = (bf16[224,256]{1,0:T(8,128)(2,1)S(1)}, bf16[224,256]{1,0:T(8,128)(2,1)}, u32[]{:S(2)}) copy-start(bf16[224,256]{1,0:T(8,128)(2,1)} %param.6) | copy-start | bytes 344068
  6.5 27.3 %copy-start.2 = (bf16[224,256]{1,0:T(8,128)(2,1)S(1)}, bf16[224,256]{1,0:T(8,128)(2,1)}, u32[]{:S(2)}) copy-start(bf16[224,256]{1,0:T(8,128)(2,1)} %param.7) | copy-start | bytes 344068
  6.5 278.4 %all-gather.2.cloned.1.call-start = ((), (), s32[]{:S(2)}) async-start(), calls=%async_computation | async-start | bytes 1597440 | tf_op jit(solution)/shard_map/all_gather | solution.py:97
  6.5 25.0 %collective-permute-start.38 = (bf16[224,256]{1,0:T(8,128)(2,1)}, bf16[224,256]{1,0:T(8,128)(2,1)S(1)}, u32[]{:S(2)}, u32[]{:S(2)}) collective-permute-start(bf16[224,256]{1,0:T(8,128)(2,1)} %param.7), channel_id=1, source_target_pairs={{104,0},{112,8},{120,16},{128,24},{136,32},{144,40},{152,48},{160,... | collective-permute-start | bytes 344072 | tf_op jit(solution)/shard_map/ppermute | solution.py:16
  10.3 23.5 %collective-permute-start.34 = (bf16[224,256]{1,0:T(8,128)(2,1)}, bf16[224,256]{1,0:T(8,128)(2,1)S(1)}, u32[]{:S(2)}, u32[]{:S(2)}) collective-permute-start(bf16[224,256]{1,0:T(8,128)(2,1)} %param.7), channel_id=1, source_target_pairs={{88,0},{96,8},{104,16},{112,24},{120,32},{128,40},{136,48},{144,56... | collective-permute-start | bytes 344072 | tf_op jit(solution)/shard_map/ppermute | solution.py:16
  18.7 22.5 %collective-permute-start.16 = (bf16[224,256]{1,0:T(8,128)(2,1)}, bf16[224,256]{1,0:T(8,128)(2,1)S(1)}, u32[]{:S(2)}, u32[]{:S(2)}) collective-permute-start(bf16[224,256]{1,0:T(8,128)(2,1)} %param.7), channel_id=1, source_target_pairs={{0,88},{8,96},{16,104},{24,112},{32,120},{40,128},{48,136},{56,144... | collective-permute-start | bytes 344072 | tf_op jit(solution)/shard_map/ppermute | solution.py:16
  20.6 22.8 %collective-permute-start.12 = (bf16[224,256]{1,0:T(8,128)(2,1)}, bf16[224,256]{1,0:T(8,128)(2,1)S(1)}, u32[]{:S(2)}, u32[]{:S(2)}) collective-permute-start(bf16[224,256]{1,0:T(8,128)(2,1)} %param.7), channel_id=1, source_target_pairs={{0,104},{8,112},{16,120},{24,128},{32,136},{40,144},{48,152},{56,1... | collective-permute-start | bytes 344072 | tf_op jit(solution)/shard_map/ppermute | solution.py:16
  25.5 20.1 %collective-permute-start.4 = (bf16[224,256]{1,0:T(8,128)(2,1)}, bf16[224,256]{1,0:T(8,128)(2,1)S(1)}, u32[]{:S(2)}, u32[]{:S(2)}) collective-permute-start(bf16[224,256]{1,0:T(8,128)(2,1)} %param.7), channel_id=1, source_target_pairs={{0,152},{8,160},{16,168},{24,176},{32,184},{40,192},{48,200},{56,2... | collective-permute-start | bytes 344072 | tf_op jit(solution)/shard_map/ppermute | solution.py:16
  31.6 21.7 %collective-permute-start = (bf16[224,256]{1,0:T(8,128)(2,1)}, bf16[224,256]{1,0:T(8,128)(2,1)S(1)}, u32[]{:S(2)}, u32[]{:S(2)}) collective-permute-start(bf16[224,256]{1,0:T(8,128)(2,1)} %param.7), channel_id=1, source_target_pairs={{0,168},{8,176},{16,184},{24,192},{32,200},{40,208},{48,216},{56,2... | collective-permute-start | bytes 344072 | tf_op jit(solution)/shard_map/ppermute | solution.py:16
  33.8 30.7 %collective-permute-start.36 = (bf16[224,256]{1,0:T(8,128)(2,1)S(1)}, bf16[224,256]{1,0:T(8,128)(2,1)S(1)}, u32[]{:S(2)}, u32[]{:S(2)}) collective-permute-start(bf16[224,256]{1,0:T(8,128)(2,1)S(1)} %copy-done.2), channel_id=1, source_target_pairs={{96,0},{104,8},{112,16},{120,24},{128,32},{136,40},{144,48},{152,5... | collective-permute-start | bytes 344072 | tf_op jit(solution)/shard_map/ppermute | solution.py:16
  41.2 25.5 %collective-permute-start.14 = (bf16[224,256]{1,0:T(8,128)(2,1)S(1)}, bf16[224,256]{1,0:T(8,128)(2,1)S(1)}, u32[]{:S(2)}, u32[]{:S(2)}) collective-permute-start(bf16[224,256]{1,0:T(8,128)(2,1)S(1)} %copy-done.2), channel_id=1, source_target_pairs={{0,96},{8,104},{16,112},{24,120},{32,128},{40,136},{48,144},{56,15... | collective-permute-start | bytes 344072 | tf_op jit(solution)/shard_map/ppermute | solution.py:16
  43.4 25.6 %collective-permute-start.2 = (bf16[224,256]{1,0:T(8,128)(2,1)S(1)}, bf16[224,256]{1,0:T(8,128)(2,1)S(1)}, u32[]{:S(2)}, u32[]{:S(2)}) collective-permute-start(bf16[224,256]{1,0:T(8,128)(2,1)S(1)} %copy-done.2), channel_id=1, source_target_pairs={{0,160},{8,168},{16,176},{24,184},{32,192},{40,200},{48,208},{56,2... | collective-permute-start | bytes 344072 | tf_op jit(solution)/shard_map/ppermute | solution.py:16
  45.6 25.6 %collective-permute-start.32 = (bf16[224,256]{1,0:T(8,128)(2,1)S(1)}, bf16[224,256]{1,0:T(8,128)(2,1)S(1)}, u32[]{:S(2)}, u32[]{:S(2)}) collective-permute-start(bf16[224,256]{1,0:T(8,128)(2,1)S(1)} %copy-done.2), channel_id=1, source_target_pairs={{40,0},{48,8},{56,16},{64,24},{72,32},{80,40},{88,48},{96,56},{104... | collective-permute-start | bytes 344072 | tf_op jit(solution)/shard_map/ppermute | solution.py:16
  53.3 22.7 %collective-permute-start.28 = (bf16[224,256]{1,0:T(8,128)(2,1)S(1)}, bf16[224,256]{1,0:T(8,128)(2,1)S(1)}, u32[]{:S(2)}, u32[]{:S(2)}) collective-permute-start(bf16[224,256]{1,0:T(8,128)(2,1)S(1)} %copy-done.2), channel_id=1, source_target_pairs={{24,0},{32,8},{40,16},{48,24},{56,32},{64,40},{72,48},{80,56},{88,... | collective-permute-start | bytes 344072 | tf_op jit(solution)/shard_map/ppermute | solution.py:16
  64.5 13.6 %collective-permute-start.22 = (bf16[224,256]{1,0:T(8,128)(2,1)S(1)}, bf16[224,256]{1,0:T(8,128)(2,1)S(1)}, u32[]{:S(2)}, u32[]{:S(2)}) collective-permute-start(bf16[224,256]{1,0:T(8,128)(2,1)S(1)} %copy-done.2), channel_id=1, source_target_pairs={{0,24},{8,32},{16,40},{24,48},{32,56},{40,64},{48,72},{56,80},{64,... | collective-permute-start | bytes 344072 | tf_op jit(solution)/shard_map/ppermute | solution.py:16
  66.7 14.6 %collective-permute-start.18 = (bf16[224,256]{1,0:T(8,128)(2,1)S(1)}, bf16[224,256]{1,0:T(8,128)(2,1)S(1)}, u32[]{:S(2)}, u32[]{:S(2)}) collective-permute-start(bf16[224,256]{1,0:T(8,128)(2,1)S(1)} %copy-done.2), channel_id=1, source_target_pairs={{0,40},{8,48},{16,56},{24,64},{32,72},{40,80},{48,88},{56,96},{64,... | collective-permute-start | bytes 344072 | tf_op jit(solution)/shard_map/ppermute | solution.py:16
  68.9 19.5 %collective-permute-start.40 = (bf16[224,256]{1,0:T(8,128)(2,1)S(1)}, bf16[224,256]{1,0:T(8,128)(2,1)S(1)}, u32[]{:S(2)}, u32[]{:S(2)}) collective-permute-start(bf16[224,256]{1,0:T(8,128)(2,1)S(1)} %copy-done.2), channel_id=1, source_target_pairs={{120,0},{128,8},{136,16},{144,24},{152,32},{160,40},{168,48},{176,... | collective-permute-start | bytes 344072 | tf_op jit(solution)/shard_map/ppermute | solution.py:16
  71.1 20.9 %collective-permute-start.10 = (bf16[224,256]{1,0:T(8,128)(2,1)S(1)}, bf16[224,256]{1,0:T(8,128)(2,1)S(1)}, u32[]{:S(2)}, u32[]{:S(2)}) collective-permute-start(bf16[224,256]{1,0:T(8,128)(2,1)S(1)} %copy-done.2), channel_id=1, source_target_pairs={{0,120},{8,128},{16,136},{24,144},{32,152},{40,160},{48,168},{56,1... | collective-permute-start | bytes 344072 | tf_op jit(solution)/shard_map/ppermute | solution.py:16
  76.0 18.3 %collective-permute-start.6 = (bf16[224,256]{1,0:T(8,128)(2,1)S(1)}, bf16[224,256]{1,0:T(8,128)(2,1)S(1)}, u32[]{:S(2)}, u32[]{:S(2)}) collective-permute-start(bf16[224,256]{1,0:T(8,128)(2,1)S(1)} %copy-done.2), channel_id=1, source_target_pairs={{0,136},{8,144},{16,152},{24,160},{32,168},{40,176},{48,184},{56,1... | collective-permute-start | bytes 344072 | tf_op jit(solution)/shard_map/ppermute | solution.py:16
  78.2 18.3 %collective-permute-start.42 = (bf16[224,256]{1,0:T(8,128)(2,1)S(1)}, bf16[224,256]{1,0:T(8,128)(2,1)S(1)}, u32[]{:S(2)}, u32[]{:S(2)}) collective-permute-start(bf16[224,256]{1,0:T(8,128)(2,1)S(1)} %copy-done.2), channel_id=1, source_target_pairs={{128,0},{136,8},{144,16},{152,24},{160,32},{168,40},{176,48},{184,... | collective-permute-start | bytes 344072 | tf_op jit(solution)/shard_map/ppermute | solution.py:16
  81.3 17.4 %collective-permute-start.30 = (bf16[224,256]{1,0:T(8,128)(2,1)S(1)}, bf16[224,256]{1,0:T(8,128)(2,1)S(1)}, u32[]{:S(2)}, u32[]{:S(2)}) collective-permute-start(bf16[224,256]{1,0:T(8,128)(2,1)S(1)} %copy-done.2), channel_id=1, source_target_pairs={{32,0},{40,8},{48,16},{56,24},{64,32},{72,40},{80,48},{88,56},{96,... | collective-permute-start | bytes 344072 | tf_op jit(solution)/shard_map/ppermute | solution.py:16
  88.4 19.7 %collective-permute-start.26 = (bf16[224,256]{1,0:T(8,128)(2,1)S(1)}, bf16[224,256]{1,0:T(8,128)(2,1)S(1)}, u32[]{:S(2)}, u32[]{:S(2)}) collective-permute-start(bf16[224,256]{1,0:T(8,128)(2,1)S(1)} %copy-done.2), channel_id=1, source_target_pairs={{8,0},{16,8},{24,16},{32,24},{40,32},{48,40},{56,48},{64,56},{72,6... | collective-permute-start | bytes 344072 | tf_op jit(solution)/shard_map/ppermute | solution.py:16
  92.0 18.2 %collective-permute-start.24 = (bf16[224,256]{1,0:T(8,128)(2,1)S(1)}, bf16[224,256]{1,0:T(8,128)(2,1)S(1)}, u32[]{:S(2)}, u32[]{:S(2)}) collective-permute-start(bf16[224,256]{1,0:T(8,128)(2,1)S(1)} %copy-done.2), channel_id=1, source_target_pairs={{0,8},{8,16},{16,24},{24,32},{32,40},{40,48},{48,56},{56,64},{64,7... | collective-permute-start | bytes 344072 | tf_op jit(solution)/shard_map/ppermute | solution.py:16
  94.2 18.2 %collective-permute-start.20 = (bf16[224,256]{1,0:T(8,128)(2,1)S(1)}, bf16[224,256]{1,0:T(8,128)(2,1)S(1)}, u32[]{:S(2)}, u32[]{:S(2)}) collective-permute-start(bf16[224,256]{1,0:T(8,128)(2,1)S(1)} %copy-done.2), channel_id=1, source_target_pairs={{0,32},{8,40},{16,48},{24,56},{32,64},{40,72},{48,80},{56,88},{64,... | collective-permute-start | bytes 344072 | tf_op jit(solution)/shard_map/ppermute | solution.py:16
  96.5 18.2 %collective-permute-start.8 = (bf16[224,256]{1,0:T(8,128)(2,1)S(1)}, bf16[224,256]{1,0:T(8,128)(2,1)S(1)}, u32[]{:S(2)}, u32[]{:S(2)}) collective-permute-start(bf16[224,256]{1,0:T(8,128)(2,1)S(1)} %copy-done.2), channel_id=1, source_target_pairs={{0,128},{8,136},{16,144},{24,152},{32,160},{40,168},{48,176},{56,1... | collective-permute-start | bytes 344072 | tf_op jit(solution)/shard_map/ppermute | solution.py:16
  98.6 16.0 %copy-start.1 = (bf16[224,256]{1,0:T(8,128)(2,1)S(1)}, bf16[224,256]{1,0:T(8,128)(2,1)}, u32[]{:S(2)}) copy-start(bf16[224,256]{1,0:T(8,128)(2,1)} %param.8) | copy-start | bytes 344068
  98.7 20.6 %collective-permute-start.50 = (bf16[224,256]{1,0:T(8,128)(2,1)S(1)}, bf16[224,256]{1,0:T(8,128)(2,1)S(1)}, u32[]{:S(2)}, u32[]{:S(2)}) collective-permute-start(bf16[224,256]{1,0:T(8,128)(2,1)S(1)} %copy-done.2), channel_id=1, source_target_pairs={{168,0},{176,8},{184,16},{192,24},{200,32},{208,40},{216,48},{224,... | collective-permute-start | bytes 344072 | tf_op jit(solution)/shard_map/ppermute | solution.py:16
  108.1 14.3 %collective-permute-start.46 = (bf16[224,256]{1,0:T(8,128)(2,1)S(1)}, bf16[224,256]{1,0:T(8,128)(2,1)S(1)}, u32[]{:S(2)}, u32[]{:S(2)}) collective-permute-start(bf16[224,256]{1,0:T(8,128)(2,1)S(1)} %copy-done.2), channel_id=1, source_target_pairs={{152,0},{160,8},{168,16},{176,24},{184,32},{192,40},{200,48},{208,... | collective-permute-start | bytes 344072 | tf_op jit(solution)/shard_map/ppermute | solution.py:16
  110.3 14.6 %collective-permute-start.48 = (bf16[224,256]{1,0:T(8,128)(2,1)S(1)}, bf16[224,256]{1,0:T(8,128)(2,1)S(1)}, u32[]{:S(2)}, u32[]{:S(2)}) collective-permute-start(bf16[224,256]{1,0:T(8,128)(2,1)S(1)} %copy-done.2), channel_id=1, source_target_pairs={{160,0},{168,8},{176,16},{184,24},{192,32},{200,40},{208,48},{216,... | collective-permute-start | bytes 344072 | tf_op jit(solution)/shard_map/ppermute | solution.py:16
  112.5 14.6 %collective-permute-start.44 = (bf16[224,256]{1,0:T(8,128)(2,1)S(1)}, bf16[224,256]{1,0:T(8,128)(2,1)S(1)}, u32[]{:S(2)}, u32[]{:S(2)}) collective-permute-start(bf16[224,256]{1,0:T(8,128)(2,1)S(1)} %copy-done.2), channel_id=1, source_target_pairs={{136,0},{144,8},{152,16},{160,24},{168,32},{176,40},{184,48},{192,... | collective-permute-start | bytes 344072 | tf_op jit(solution)/shard_map/ppermute | solution.py:16
  114.7 17.2 %collective-permute-start.1 = (bf16[224,256]{1,0:T(8,128)(2,1)S(1)}, bf16[224,256]{1,0:T(8,128)(2,1)S(1)}, u32[]{:S(2)}, u32[]{:S(2)}) collective-permute-start(bf16[224,256]{1,0:T(8,128)(2,1)S(1)} %copy-done.1), channel_id=1, source_target_pairs={{0,168},{8,176},{16,184},{24,192},{32,200},{40,208},{48,216},{56,2... | collective-permute-start | bytes 344072 | tf_op jit(solution)/shard_map/ppermute | solution.py:16
  119.3 16.0 %collective-permute-start.3 = (bf16[224,256]{1,0:T(8,128)(2,1)S(1)}, bf16[224,256]{1,0:T(8,128)(2,1)S(1)}, u32[]{:S(2)}, u32[]{:S(2)}) collective-permute-start(bf16[224,256]{1,0:T(8,128)(2,1)S(1)} %copy-done.1), channel_id=1, source_target_pairs={{0,160},{8,168},{16,176},{24,184},{32,192},{40,200},{48,208},{56,2... | collective-permute-start | bytes 344072 | tf_op jit(solution)/shard_map/ppermute | solution.py:16
  122.4 19.4 %collective-permute-start.5 = (bf16[224,256]{1,0:T(8,128)(2,1)S(1)}, bf16[224,256]{1,0:T(8,128)(2,1)S(1)}, u32[]{:S(2)}, u32[]{:S(2)}) collective-permute-start(bf16[224,256]{1,0:T(8,128)(2,1)S(1)} %copy-done.1), channel_id=1, source_target_pairs={{0,152},{8,160},{16,168},{24,176},{32,184},{40,192},{48,200},{56,2... | collective-permute-start | bytes 344072 | tf_op jit(solution)/shard_map/ppermute | solution.py:16
  124.9 19.9 %collective-permute-start.7 = (bf16[224,256]{1,0:T(8,128)(2,1)S(1)}, bf16[224,256]{1,0:T(8,128)(2,1)S(1)}, u32[]{:S(2)}, u32[]{:S(2)}) collective-permute-start(bf16[224,256]{1,0:T(8,128)(2,1)S(1)} %copy-done.1), channel_id=1, source_target_pairs={{0,136},{8,144},{16,152},{24,160},{32,168},{40,176},{48,184},{56,1... | collective-permute-start | bytes 344072 | tf_op jit(solution)/shard_map/ppermute | solution.py:16
  127.1 19.9 %collective-permute-start.9 = (bf16[224,256]{1,0:T(8,128)(2,1)S(1)}, bf16[224,256]{1,0:T(8,128)(2,1)S(1)}, u32[]{:S(2)}, u32[]{:S(2)}) collective-permute-start(bf16[224,256]{1,0:T(8,128)(2,1)S(1)} %copy-done.1), channel_id=1, source_target_pairs={{0,128},{8,136},{16,144},{24,152},{32,160},{40,168},{48,176},{56,1... | collective-permute-start | bytes 344072 | tf_op jit(solution)/shard_map/ppermute | solution.py:16
  131.9 20.7 %collective-permute-start.11 = (bf16[224,256]{1,0:T(8,128)(2,1)S(1)}, bf16[224,256]{1,0:T(8,128)(2,1)S(1)}, u32[]{:S(2)}, u32[]{:S(2)}) collective-permute-start(bf16[224,256]{1,0:T(8,128)(2,1)S(1)} %copy-done.1), channel_id=1, source_target_pairs={{0,120},{8,128},{16,136},{24,144},{32,152},{40,160},{48,168},{56,1... | collective-permute-start | bytes 344072 | tf_op jit(solution)/shard_map/ppermute | solution.py:16
  135.4 20.1 %collective-permute-start.13 = (bf16[224,256]{1,0:T(8,128)(2,1)S(1)}, bf16[224,256]{1,0:T(8,128)(2,1)S(1)}, u32[]{:S(2)}, u32[]{:S(2)}) collective-permute-start(bf16[224,256]{1,0:T(8,128)(2,1)S(1)} %copy-done.1), channel_id=1, source_target_pairs={{0,104},{8,112},{16,120},{24,128},{32,136},{40,144},{48,152},{56,1... | collective-permute-start | bytes 344072 | tf_op jit(solution)/shard_map/ppermute | solution.py:16
  141.8 15.9 %collective-permute-start.15 = (bf16[224,256]{1,0:T(8,128)(2,1)S(1)}, bf16[224,256]{1,0:T(8,128)(2,1)S(1)}, u32[]{:S(2)}, u32[]{:S(2)}) collective-permute-start(bf16[224,256]{1,0:T(8,128)(2,1)S(1)} %copy-done.1), channel_id=1, source_target_pairs={{0,96},{8,104},{16,112},{24,120},{32,128},{40,136},{48,144},{56,15... | collective-permute-start | bytes 344072 | tf_op jit(solution)/shard_map/ppermute | solution.py:16
  144.8 18.2 %collective-permute-start.17 = (bf16[224,256]{1,0:T(8,128)(2,1)S(1)}, bf16[224,256]{1,0:T(8,128)(2,1)S(1)}, u32[]{:S(2)}, u32[]{:S(2)}) collective-permute-start(bf16[224,256]{1,0:T(8,128)(2,1)S(1)} %copy-done.1), channel_id=1, source_target_pairs={{0,88},{8,96},{16,104},{24,112},{32,120},{40,128},{48,136},{56,144... | collective-permute-start | bytes 344072 | tf_op jit(solution)/shard_map/ppermute | solution.py:16
  147.0 19.8 %collective-permute-start.19 = (bf16[224,256]{1,0:T(8,128)(2,1)S(1)}, bf16[224,256]{1,0:T(8,128)(2,1)S(1)}, u32[]{:S(2)}, u32[]{:S(2)}) collective-permute-start(bf16[224,256]{1,0:T(8,128)(2,1)S(1)} %copy-done.1), channel_id=1, source_target_pairs={{0,40},{8,48},{16,56},{24,64},{32,72},{40,80},{48,88},{56,96},{64,... | collective-permute-start | bytes 344072 | tf_op jit(solution)/shard_map/ppermute | solution.py:16
  152.6 19.7 %collective-permute-start.21 = (bf16[224,256]{1,0:T(8,128)(2,1)S(1)}, bf16[224,256]{1,0:T(8,128)(2,1)S(1)}, u32[]{:S(2)}, u32[]{:S(2)}) collective-permute-start(bf16[224,256]{1,0:T(8,128)(2,1)S(1)} %copy-done.1), channel_id=1, source_target_pairs={{0,32},{8,40},{16,48},{24,56},{32,64},{40,72},{48,80},{56,88},{64,... | collective-permute-start | bytes 344072 | tf_op jit(solution)/shard_map/ppermute | solution.py:16
  155.5 21.8 %collective-permute-start.23 = (bf16[224,256]{1,0:T(8,128)(2,1)S(1)}, bf16[224,256]{1,0:T(8,128)(2,1)S(1)}, u32[]{:S(2)}, u32[]{:S(2)}) collective-permute-start(bf16[224,256]{1,0:T(8,128)(2,1)S(1)} %copy-done.1), channel_id=1, source_target_pairs={{0,24},{8,32},{16,40},{24,48},{32,56},{40,64},{48,72},{56,80},{64,... | collective-permute-start | bytes 344072 | tf_op jit(solution)/shard_map/ppermute | solution.py:16
  157.7 21.8 %collective-permute-start.25 = (bf16[224,256]{1,0:T(8,128)(2,1)S(1)}, bf16[224,256]{1,0:T(8,128)(2,1)S(1)}, u32[]{:S(2)}, u32[]{:S(2)}) collective-permute-start(bf16[224,256]{1,0:T(8,128)(2,1)S(1)} %copy-done.1), channel_id=1, source_target_pairs={{0,8},{8,16},{16,24},{24,32},{32,40},{40,48},{48,56},{56,64},{64,7... | collective-permute-start | bytes 344072 | tf_op jit(solution)/shard_map/ppermute | solution.py:16
  163.0 21.9 %collective-permute-start.27 = (bf16[224,256]{1,0:T(8,128)(2,1)S(1)}, bf16[224,256]{1,0:T(8,128)(2,1)S(1)}, u32[]{:S(2)}, u32[]{:S(2)}) collective-permute-start(bf16[224,256]{1,0:T(8,128)(2,1)S(1)} %copy-done.1), channel_id=1, source_target_pairs={{8,0},{16,8},{24,16},{32,24},{40,32},{48,40},{56,48},{64,56},{72,6... | collective-permute-start | bytes 344072 | tf_op jit(solution)/shard_map/ppermute | solution.py:16
  166.9 20.3 %collective-permute-start.29 = (bf16[224,256]{1,0:T(8,128)(2,1)S(1)}, bf16[224,256]{1,0:T(8,128)(2,1)S(1)}, u32[]{:S(2)}, u32[]{:S(2)}) collective-permute-start(bf16[224,256]{1,0:T(8,128)(2,1)S(1)} %copy-done.1), channel_id=1, source_target_pairs={{24,0},{32,8},{40,16},{48,24},{56,32},{64,40},{72,48},{80,56},{88,... | collective-permute-start | bytes 344072 | tf_op jit(solution)/shard_map/ppermute | solution.py:16
  172.4 17.0 %collective-permute-start.31 = (bf16[224,256]{1,0:T(8,128)(2,1)S(1)}, bf16[224,256]{1,0:T(8,128)(2,1)S(1)}, u32[]{:S(2)}, u32[]{:S(2)}) collective-permute-start(bf16[224,256]{1,0:T(8,128)(2,1)S(1)} %copy-done.1), channel_id=1, source_target_pairs={{32,0},{40,8},{48,16},{56,24},{64,32},{72,40},{80,48},{88,56},{96,... | collective-permute-start | bytes 344072 | tf_op jit(solution)/shard_map/ppermute | solution.py:16
  177.3 14.4 %collective-permute-start.33 = (bf16[224,256]{1,0:T(8,128)(2,1)S(1)}, bf16[224,256]{1,0:T(8,128)(2,1)S(1)}, u32[]{:S(2)}, u32[]{:S(2)}) collective-permute-start(bf16[224,256]{1,0:T(8,128)(2,1)S(1)} %copy-done.1), channel_id=1, source_target_pairs={{40,0},{48,8},{56,16},{64,24},{72,32},{80,40},{88,48},{96,56},{104... | collective-permute-start | bytes 344072 | tf_op jit(solution)/shard_map/ppermute | solution.py:16
  179.5 15.1 %collective-permute-start.35 = (bf16[224,256]{1,0:T(8,128)(2,1)S(1)}, bf16[224,256]{1,0:T(8,128)(2,1)S(1)}, u32[]{:S(2)}, u32[]{:S(2)}) collective-permute-start(bf16[224,256]{1,0:T(8,128)(2,1)S(1)} %copy-done.1), channel_id=1, source_target_pairs={{88,0},{96,8},{104,16},{112,24},{120,32},{128,40},{136,48},{144,56... | collective-permute-start | bytes 344072 | tf_op jit(solution)/shard_map/ppermute | solution.py:16
  184.9 13.5 %collective-permute-start.37 = (bf16[224,256]{1,0:T(8,128)(2,1)S(1)}, bf16[224,256]{1,0:T(8,128)(2,1)S(1)}, u32[]{:S(2)}, u32[]{:S(2)}) collective-permute-start(bf16[224,256]{1,0:T(8,128)(2,1)S(1)} %copy-done.1), channel_id=1, source_target_pairs={{96,0},{104,8},{112,16},{120,24},{128,32},{136,40},{144,48},{152,5... | collective-permute-start | bytes 344072 | tf_op jit(solution)/shard_map/ppermute | solution.py:16
  187.2 14.7 %collective-permute-start.39 = (bf16[224,256]{1,0:T(8,128)(2,1)S(1)}, bf16[224,256]{1,0:T(8,128)(2,1)S(1)}, u32[]{:S(2)}, u32[]{:S(2)}) collective-permute-start(bf16[224,256]{1,0:T(8,128)(2,1)S(1)} %copy-done.1), channel_id=1, source_target_pairs={{104,0},{112,8},{120,16},{128,24},{136,32},{144,40},{152,48},{160,... | collective-permute-start | bytes 344072 | tf_op jit(solution)/shard_map/ppermute | solution.py:16
  189.4 15.5 %collective-permute-start.41 = (bf16[224,256]{1,0:T(8,128)(2,1)S(1)}, bf16[224,256]{1,0:T(8,128)(2,1)S(1)}, u32[]{:S(2)}, u32[]{:S(2)}) collective-permute-start(bf16[224,256]{1,0:T(8,128)(2,1)S(1)} %copy-done.1), channel_id=1, source_target_pairs={{120,0},{128,8},{136,16},{144,24},{152,32},{160,40},{168,48},{176,... | collective-permute-start | bytes 344072 | tf_op jit(solution)/shard_map/ppermute | solution.py:16
  191.7 15.5 %collective-permute-start.43 = (bf16[224,256]{1,0:T(8,128)(2,1)S(1)}, bf16[224,256]{1,0:T(8,128)(2,1)S(1)}, u32[]{:S(2)}, u32[]{:S(2)}) collective-permute-start(bf16[224,256]{1,0:T(8,128)(2,1)S(1)} %copy-done.1), channel_id=1, source_target_pairs={{128,0},{136,8},{144,16},{152,24},{160,32},{168,40},{176,48},{184,... | collective-permute-start | bytes 344072 | tf_op jit(solution)/shard_map/ppermute | solution.py:16
  194.6 13.2 %collective-permute-start.45 = (bf16[224,256]{1,0:T(8,128)(2,1)S(1)}, bf16[224,256]{1,0:T(8,128)(2,1)S(1)}, u32[]{:S(2)}, u32[]{:S(2)}) collective-permute-start(bf16[224,256]{1,0:T(8,128)(2,1)S(1)} %copy-done.1), channel_id=1, source_target_pairs={{136,0},{144,8},{152,16},{160,24},{168,32},{176,40},{184,48},{192,... | collective-permute-start | bytes 344072 | tf_op jit(solution)/shard_map/ppermute | solution.py:16
  198.5 21.9 %collective-permute-start.47 = (bf16[224,256]{1,0:T(8,128)(2,1)S(1)}, bf16[224,256]{1,0:T(8,128)(2,1)S(1)}, u32[]{:S(2)}, u32[]{:S(2)}) collective-permute-start(bf16[224,256]{1,0:T(8,128)(2,1)S(1)} %copy-done.1), channel_id=1, source_target_pairs={{152,0},{160,8},{168,16},{176,24},{184,32},{192,40},{200,48},{208,... | collective-permute-start | bytes 344072 | tf_op jit(solution)/shard_map/ppermute | solution.py:16
  201.9 20.9 %collective-permute-start.49 = (bf16[224,256]{1,0:T(8,128)(2,1)S(1)}, bf16[224,256]{1,0:T(8,128)(2,1)S(1)}, u32[]{:S(2)}, u32[]{:S(2)}) collective-permute-start(bf16[224,256]{1,0:T(8,128)(2,1)S(1)} %copy-done.1), channel_id=1, source_target_pairs={{160,0},{168,8},{176,16},{184,24},{192,32},{200,40},{208,48},{216,... | collective-permute-start | bytes 344072 | tf_op jit(solution)/shard_map/ppermute | solution.py:16
  205.0 26.8 %collective-permute-start.51 = (bf16[224,256]{1,0:T(8,128)(2,1)S(1)}, bf16[224,256]{1,0:T(8,128)(2,1)S(1)}, u32[]{:S(2)}, u32[]{:S(2)}) collective-permute-start(bf16[224,256]{1,0:T(8,128)(2,1)S(1)} %copy-done.1), channel_id=1, source_target_pairs={{168,0},{176,8},{184,16},{192,24},{200,32},{208,40},{216,48},{224,... | collective-permute-start | bytes 344072 | tf_op jit(solution)/shard_map/ppermute | solution.py:16
  222.8 62.2 %copy-start.3 = (f32[384]{0:T(512)S(1)}, f32[384]{0:T(512)}, u32[]{:S(2)}) copy-start(f32[384]{0:T(512)} %param.11) | copy-start | bytes 4612
Sparse Core Ops, SparseCore 0:
  27.5 154.7 all-gather.1
where the time goes:
time: 296 us; the launch traced here: 295 us
  starting transfers between devices  165 us (56%)
  blocking collectives  52.9 us (18%)
  waiting for transfers between devices  38.2 us (13%)
  matrix products  19 us (6%)
  between operations  14.6 us (5%)
  other arithmetic  5.06 us (2%)
    ppermute x52, starting transfers between devices, passed_along(): lax.ppermute(value, axis, [(source, source + steps) for source in range(l...  165 us
    all_gather x1, blocking collectives, local(): every_head = lax.all_gather(attended, 'fsdp', axis=1, tiled=True)  52.9 us
    ppermute x52, waiting for transfers between devices, passed_along(): lax.ppermute(value, axis, [(source, source + steps) for source in range(l...  38.1 us
    dot_general x27, matrix products, online_step(): jnp.einsum('hqk,khd->qhd', rounded, value_heads, preferred_element_type=j...  8.25 us
    dot_general x27, matrix products, online_step(): jnp.einsum('qhd,khd->hqk', queries_heads, key_heads, preferred_element_ty...  8 us
  transfers between devices with their start and end apart: 53, of which 12 were waited for; matrix products, arithmetic and copies ran while one was open for 7% of the time, Pallas kernels for 0%

commit v1 on v0

v1 whole, which is shorter than its diff:
```python
import functools
import math

import jax
import jax.numpy as jnp
from jax import lax
from jax.experimental import pallas as pl
from jax.experimental.pallas import tpu as pltpu
from jax.sharding import Mesh
from jax.sharding import PartitionSpec as P

HD = 128
ROWS = 224
STATE = HD + 8
SCALE = math.log2(math.e) / math.sqrt(HD)
ROW_AXES = ("t", "u", "w", "c")
COL_AXES = ("x", "h")
VMEM_LIMIT = 32 * 1024 * 1024


def passed_along(value, axis, steps):
    count = lax.axis_size(axis)
    return lax.ppermute(
        value, axis, [(i, i + steps) for i in range(count) if 0 <= i + steps < count]
    )


def exchanged(value, axis):
    return lax.ppermute(value, axis, [(0, 1), (1, 0)])


def online_update(state_ref, tile, queries, keys, values):
    scores = lax.dot_general(
        keys, queries, (((1,), (1,)), ((), ())), preferred_element_type=jnp.float32
    )
    old_max = state_ref[tile, HD : HD + 1, :]
    new_max = jnp.maximum(old_max, jnp.max(scores, axis=0, keepdims=True))
    factor = jnp.exp2((old_max - new_max) * SCALE)
    weights = jnp.exp2((scores - new_max) * SCALE)
    total = state_ref[tile, HD + 1 : HD + 2, :] * factor + jnp.sum(weights, axis=0, keepdims=True)
    added = lax.dot_general(
        values,
        weights.astype(jnp.bfloat16),
        (((0,), (0,)), ((), ())),
        preferred_element_type=jnp.float32,
    )
    state_ref[tile, 0:HD, :] = state_ref[tile, 0:HD, :] * factor + added
    state_ref[tile, HD : HD + 1, :] = new_max
    state_ref[tile, HD + 1 : HD + 2, :] = total


def attend_kernel(blocks, tiles, first, *refs):
    flags_ref, q_ref = refs[0], refs[1]
    kv_refs = refs[2 : 2 + blocks]
    state_ref = refs[-1]
    if first:
        state_ref[...] = jnp.zeros(state_ref.shape, jnp.float32)
        state_ref[:, HD : HD + 1, :] = jnp.full((len(tiles), 1, ROWS), -jnp.inf, jnp.float32)
    else:
        state_ref[...] = refs[2 + blocks][...]
    wide = flags_ref[0] > 0
    facing = flags_ref[1]
    for b in range(blocks):
        kv_ref = kv_refs[b]
        valid = flags_ref[2 + b] > 0

        @pl.when(valid & wide)
        def _():
            for at, tile in enumerate(tiles):
                if tile < 2:
                    online_update(
                        state_ref, at, q_ref[tile], kv_ref[:, 0:HD], kv_ref[:, HD : 2 * HD]
                    )
                else:
                    rows = pl.ds(pl.multiple_of(facing * ROWS, 16), ROWS)
                    online_update(
                        state_ref, at, q_ref[tile], kv_ref[rows, 0:HD], kv_ref[rows, HD : 2 * HD]
                    )

        @pl.when(valid & jnp.logical_not(wide))
        def _():
            for at, tile in enumerate(tiles):
                if tile < 2:
                    rows = pl.ds(tile * ROWS, ROWS)
                    online_update(
                        state_ref, at, q_ref[tile], kv_ref[rows, 0:HD], kv_ref[rows, HD : 2 * HD]
                    )


def attend(flags, queries, key_values, tiles, state=None):
    blocks = len(key_values)
    vmem = pl.BlockSpec(memory_space=pltpu.VMEM)
    operands = [flags, queries, *key_values]
    if state is not None:
        operands.append(state)
    pairs = blocks * sum(2 if tile < 2 else 1 for tile in tiles)
    return pl.pallas_call(
        functools.partial(attend_kernel, blocks, tiles, state is None),
        out_shape=jax.ShapeDtypeStruct((len(tiles), STATE, ROWS), jnp.float32),
        in_specs=[pl.BlockSpec(memory_space=pltpu.SMEM)] + [vmem] * (len(operands) - 1),
        out_specs=vmem,
        compiler_params=pltpu.CompilerParams(vmem_limit_bytes=VMEM_LIMIT),
        cost_estimate=pl.CostEstimate(
            flops=pairs * ROWS * ROWS * HD * 4,
            bytes_accessed=blocks * 4 * ROWS * HD * 2,
            transcendentals=pairs * ROWS * ROWS,
        ),
    )(*operands)


def finish_kernel(flags_ref, own_ref, part_ref, out_ref):
    facing = flags_ref[1]
    for tile in range(2):
        own_max = own_ref[tile, HD : HD + 1, :]
        own_sum = own_ref[tile, HD + 1 : HD + 2, :]
        own = own_ref[tile, 0:HD, :]

        @pl.when(facing == tile)
        def _():
            part_max = part_ref[0, HD : HD + 1, :]
            both_max = jnp.maximum(own_max, part_max)
            own_factor = jnp.exp2((own_max - both_max) * SCALE)
            part_factor = jnp.exp2((part_max - both_max) * SCALE)
            both_sum = own_sum * own_factor + part_ref[0, HD + 1 : HD + 2, :] * part_factor
            both = own * own_factor + part_ref[0, 0:HD, :] * part_factor
            out_ref[tile] = jnp.transpose(both / both_sum).astype(jnp.bfloat16)

        @pl.when(facing != tile)
        def _():
            out_ref[tile] = jnp.transpose(own / own_sum).astype(jnp.bfloat16)


def finish(flags, own, part):
    vmem = pl.BlockSpec(memory_space=pltpu.VMEM)
    return pl.pallas_call(
        finish_kernel,
        out_shape=jax.ShapeDtypeStruct((2, ROWS, HD), jnp.bfloat16),
        in_specs=[pl.BlockSpec(memory_space=pltpu.SMEM), vmem, vmem],
        out_specs=vmem,
        compiler_params=pltpu.CompilerParams(vmem_limit_bytes=VMEM_LIMIT),
    )(flags, own, part)


def project_kernel(groups, order_ref, rows_ref, weight_ref, gate_ref, out_ref):
    total = jnp.zeros(out_ref.shape, jnp.float32)
    for x in range(groups):
        for slot in range(4):
            head = x * 4 + (slot ^ order_ref[0])
            weight = weight_ref[pl.ds(pl.multiple_of(head * HD, HD), HD), :]
            total += jnp.dot(
                rows_ref[x, slot], weight, preferred_element_type=jnp.float32
            )
    out_ref[...] = (total * gate_ref[...]).astype(jnp.bfloat16)


def project(order, rows, weight, gate):
    vmem = pl.BlockSpec(memory_space=pltpu.VMEM)
    return pl.pallas_call(
        functools.partial(project_kernel, rows.shape[0]),
        out_shape=jax.ShapeDtypeStruct((rows.shape[2], weight.shape[1]), jnp.bfloat16),
        in_specs=[pl.BlockSpec(memory_space=pltpu.SMEM), vmem, vmem, vmem],
        out_specs=vmem,
        compiler_params=pltpu.CompilerParams(vmem_limit_bytes=VMEM_LIMIT),
    )(order, rows, weight, gate)


def gathered_weight(out_weight, core):
    mine = lax.all_gather(out_weight, ("u", "w"), axis=0, tiled=False)
    mine = lax.all_gather(mine, "t", axis=0, tiled=False)
    other = exchanged(mine, "c")
    first = jnp.where(core == 0, mine, other)
    second = jnp.where(core == 0, other, mine)
    return jnp.stack([first, second], axis=2).reshape(-1, out_weight.shape[1])


def local(queries, key_rows, value_rows, extents, out_weight, gate_scale):
    time_pos, height_pos, width_pair = (lax.axis_index(a) for a in ("t", "u", "w"))
    core, high = lax.axis_index("c"), lax.axis_index("h")

    def split(value):
        kept = jnp.where(core == 0, value[:, :HD], value[:, HD:])
        given = jnp.where(core == 0, value[:, HD:], value[:, :HD])
        return kept, given

    parts = [split(v) for v in (key_rows, value_rows, queries)]
    kept = jnp.concatenate([p[0] for p in parts], axis=1)
    given = jnp.concatenate([p[1] for p in parts], axis=1)
    taken = exchanged(given, "c")
    both = jnp.stack([kept, taken])
    own_kv = both[:, :, : 2 * HD].reshape(2 * ROWS, 2 * HD)
    own_q = both[:, :, 2 * HD :]

    reach = jnp.where(core == 0, extents[0], extents[1])
    facing = (1 - width_pair) ^ core

    def flags(steps):
        ok = [
            (abs(ts) <= reach[0])
            & (abs(us) <= reach[1])
            & (time_pos + ts >= 0)
            & (time_pos + ts < 4)
            & (height_pos + us >= 0)
            & (height_pos + us < 4)
            for ts, us in steps
        ]
        return jnp.stack([(reach[2] > 0).astype(jnp.int32), facing] + [o.astype(jnp.int32) for o in ok])

    up = {us: passed_along(own_kv, "u", -us) for us in (-1, 1)}
    along = {ts: passed_along(own_kv, "t", -ts) for ts in (-1, 1)}
    facing_q = exchanged(lax.dynamic_index_in_dim(own_q, facing, 0, keepdims=True), "w")
    all_q = jnp.concatenate([own_q, facing_q])
    corners = {(ts, us): passed_along(up[us], "t", -ts) for us in (-1, 1) for ts in (-1, 1)}

    state = attend(flags([(0, 0)]), all_q, [own_kv], (0, 1, 2))
    state = attend(
        flags([(0, -1), (0, 1), (-1, 0), (1, 0)]),
        all_q,
        [up[-1], up[1], along[-1], along[1]],
        (0, 1, 2),
        state,
    )
    steps = [(ts, us) for us in (-1, 1) for ts in (-1, 1)]
    last = [corners[s] for s in steps]
    part = attend(flags(steps), all_q, last, (2,), state[2:])
    back = exchanged(part, "w")
    own = attend(flags(steps), all_q, last, (0, 1), state[:2])
    attended = finish(flags([]), own, back)

    swapped = exchanged(attended[1], "c")
    across = exchanged(attended[0], "h")
    crossed = lax.ppermute(attended[1], ("c", "h"), [(0, 3), (3, 0), (1, 2), (2, 1)])
    four = jnp.stack([attended[0], swapped, across, crossed])
    rows = lax.all_gather(four, "x", axis=0, tiled=False)
    weight = gathered_weight(out_weight, core)
    order = (2 * high + core).reshape(1).astype(jnp.int32)
    return project(order, rows, weight, gate_scale[None, :])


def solution(mesh):
    fine = Mesh(mesh.devices.reshape(4, 4, 2, 2, 4, 2), ROW_AXES + COL_AXES)
    in_specs = (
        P(ROW_AXES, COL_AXES),
        P(ROW_AXES, COL_AXES),
        P(ROW_AXES, COL_AXES),
        P(COL_AXES, None),
        P(ROW_AXES, COL_AXES),
        P(COL_AXES),
    )
    return jax.shard_map(
        local, mesh=fine, in_specs=in_specs, out_specs=P(ROW_AXES, COL_AXES), check_vma=False
    )
```

time: 296 us -> 134 us (0.45)
  the two profiles are of different devices: /device:TPU:80 before, /device:TPU:136 now
where the time goes in v1:
time: 134 us
  blocking collectives  59.5 us (44%)
  starting transfers between devices  45.7 us (34%)
  waiting for transfers between devices  13.9 us (10%)
  Pallas kernels  7.78 us (6%)
  between operations  3.56 us (3%)
  other arithmetic  2.47 us (2%)
    all_gather x1, blocking collectives, gathered_weight(): mine = lax.all_gather(out_weight, ('u', 'w'), axis=0, tiled=False)  27.7 us
    ppermute x8, starting transfers between devices, passed_along(): lax.ppermute(value, axis, [(i, i + steps) for i in range(count) if 0 <= i...  24.3 us
    all_gather x1, blocking collectives, gathered_weight(): mine = lax.all_gather(mine, 't', axis=0, tiled=False)  17.1 us
    ppermute x6, starting transfers between devices, exchanged(): return lax.ppermute(value, axis, [(0, 1), (1, 0)])  14.9 us
    all_gather x1, blocking collectives, local(): rows = lax.all_gather(four, 'x', axis=0, tiled=False)  14.7 us
    ppermute x6, waiting for transfers between devices, exchanged(): return lax.ppermute(value, axis, [(0, 1), (1, 0)])  11.7 us
    ppermute x1, starting transfers between devices, local(): lax.ppermute(attended[1], ('c', 'h'), [(0, 3), (3, 0), (1, 2), (2, 1)])  6.59 us
    pallas_call x4, Pallas kernels, attend(): pl.pallas_call(functools.partial(attend_kernel, blocks, tiles, state is N...  5.47 us
  transfers between devices with their start and end apart: 15, of which 3 were waited for; matrix products, arithmetic and copies ran while one was open for 1% of the time, Pallas kernels for 5%

profile of v1, /device:TPU:136, one launch (start us, length us, event | category | flops | bytes accessed | tf_op | source)
XLA Modules:
  0.0 133.8 jit_solution(14306467101589011302)
XLA Ops:
  0.0 0.0 copy-start.1
  0.0 0.9 broadcast_select_fusion.2
  0.9 0.9 broadcast_select_fusion
  1.8 0.0 copy-start
  1.9 1.9 %collective-permute-start = (bf16[224,384]{1,0:T(8,128)(2,1)S(1)}, bf16[224,384]{1,0:T(8,128)(2,1)S(1)}, u32[]{:S(2)}, u32[]{:S(2)}) collective-permute-start(bf16[224,384]{1,0:T(8,128)(2,1)S(1)} %pad_maximum_fusion.3), channel_id=1, source_target_pairs={{0,8},{8,0},{1,9},{9,1},{2,10},{10,2},{3,11},{11,3},{4,12},{12,4},... | collective-permute-start | bytes 516104 | tf_op jit(solution)/shard_map/ppermute | solution.py:29
  3.8 27.7 %all-gather.1 = bf16[256,384]{1,0:T(8,128)(2,1)S(1)} all-gather(bf16[32,384]{1,0:T(8,128)(2,1)} %param.10), channel_id=3, replica_groups=mesh['t'=4,'u'=4,'w'=2,'c'=2,'x'=4,'h'=2] {'u','w'}, dimensions={0}, use_global_device_ids=true | all-gather | bytes 221184 | tf_op jit(solution)/shard_map/all_gather | solution.py:168
  31.5 17.1 %all-gather.2 = bf16[32,32,384]{2,1,0:T(8,128)(2,1)S(1)} all-gather(bf16[8,32,384]{2,1,0:T(8,128)(2,1)S(1)} %bitcast.49), channel_id=4, replica_groups=mesh['t'=4,'u'=4,'w'=2,'c'=2,'x'=4,'h'=2] {'t'}, dimensions={0}, use_global_device_ids=true | all-gather | bytes 983040 | tf_op jit(solution)/shard_map/all_gather | solution.py:169
  48.6 0.0 copy-done.1
  48.6 0.0 collective-permute-done
  48.7 4.6 %collective-permute-start.2 = (bf16[448,256]{1,0:T(8,128)(2,1)S(1)}, bf16[448,256]{1,0:T(8,128)(2,1)S(1)}, u32[]{:S(2)}, u32[]{:S(2)}) collective-permute-start(bf16[448,256]{1,0:T(8,128)(2,1)S(1)} %bitcast.39), channel_id=1, source_target_pairs={{0,32},{32,64},{64,96},{1,33},{33,65},{65,97},{2,34},{34,66},{66,9... | collective-permute-start | bytes 688136 | tf_op jit(solution)/shard_map/ppermute | solution.py:23
  53.3 2.2 %collective-permute-start.5 = (bf16[448,256]{1,0:T(8,128)(2,1)S(1)}, bf16[448,256]{1,0:T(8,128)(2,1)S(1)}, u32[]{:S(2)}, u32[]{:S(2)}) collective-permute-start(bf16[448,256]{1,0:T(8,128)(2,1)S(1)} %bitcast.40), channel_id=1, source_target_pairs={{32,0},{64,32},{96,64},{33,1},{65,33},{97,65},{34,2},{66,34},{98,6... | collective-permute-start | bytes 688136 | tf_op jit(solution)/shard_map/ppermute | solution.py:23
  55.5 2.3 %collective-permute-start.8 = (bf16[448,256]{1,0:T(8,128)(2,1)S(1)}, bf16[448,256]{1,0:T(8,128)(2,1)S(1)}, u32[]{:S(2)}, u32[]{:S(2)}) collective-permute-start(bf16[448,256]{1,0:T(8,128)(2,1)S(1)} %bitcast.41), channel_id=1, source_target_pairs={{0,128},{128,256},{256,384},{1,129},{129,257},{257,385},{2,130},{1... | collective-permute-start | bytes 688136 | tf_op jit(solution)/shard_map/ppermute | solution.py:23
  57.8 3.6 %collective-permute-start.9 = (bf16[448,256]{1,0:T(8,128)(2,1)S(1)}, bf16[448,256]{1,0:T(8,128)(2,1)S(1)}, u32[]{:S(2)}, u32[]{:S(2)}) collective-permute-start(bf16[448,256]{1,0:T(8,128)(2,1)S(1)} %bitcast.42), channel_id=1, source_target_pairs={{128,0},{256,128},{384,256},{129,1},{257,129},{385,257},{130,2},{2... | collective-permute-start | bytes 688136 | tf_op jit(solution)/shard_map/ppermute | solution.py:23
  61.4 3.7 %collective-permute-start.1 = (bf16[1,224,128]{2,1,0:T(8,128)(2,1)S(1)}, bf16[1,224,128]{2,1,0:T(8,128)(2,1)S(1)}, u32[]{:S(2)}, u32[]{:S(2)}) collective-permute-start(bf16[1,224,128]{2,1,0:T(8,128)(2,1)S(1)} %fusion), channel_id=1, source_target_pairs={{0,16},{16,0},{1,17},{17,1},{2,18},{18,2},{3,19},{19,3},{4,20},{20... | collective-permute-start | bytes 172040 | tf_op jit(solution)/shard_map/ppermute | solution.py:29
  65.1 0.6 fusion.2
  68.9 0.0 copy-done
  68.9 0.1 stack.123.refs_0_
  69.0 0.1 stack.135.refs_0_
  69.1 0.0 collective-permute-done.1
  69.1 1.9 %collective-permute-start.14 = (bf16[4,8,32,384]{3,2,1,0:T(8,128)(2,1)S(1)}, bf16[4,8,32,384]{3,2,1,0:T(8,128)(2,1)S(1)}, u32[]{:S(2)}, u32[]{:S(2)}) collective-permute-start(bf16[4,8,32,384]{3,2,1,0:T(8,128)(2,1)S(1)} %bitcast.44), channel_id=1, source_target_pairs={{0,8},{8,0},{1,9},{9,1},{2,10},{10,2},{3,11},{11,3},{4,12},{12,4},... | collective-permute-start | bytes 2359304 | tf_op jit(solution)/shard_map/ppermute | solution.py:29
  71.0 0.1 pad_add_fusion.1.refs_0_
  71.1 0.0 collective-permute-done.2.refs_2_
  71.1 3.1 %collective-permute-start.3 = (bf16[448,256]{1,0:T(8,128)(2,1)S(1)}, bf16[448,256]{1,0:T(8,128)(2,1)S(1)}, u32[]{:S(2)}, u32[]{:S(2)}) collective-permute-start(bf16[448,256]{1,0:T(8,128)(2,1)S(1)} %collective-permute-done.2.refs_2_), channel_id=1, source_target_pairs={{0,128},{128,256},{256,384},{1,129},{129,257},{257,385},{2,130},{1... | collective-permute-start | bytes 688136 | tf_op jit(solution)/shard_map/ppermute | solution.py:23
  74.2 0.0 collective-permute-done.5.refs_3_
  74.2 2.8 %collective-permute-start.4 = (bf16[448,256]{1,0:T(8,128)(2,1)S(1)}, bf16[448,256]{1,0:T(8,128)(2,1)S(1)}, u32[]{:S(2)}, u32[]{:S(2)}) collective-permute-start(bf16[448,256]{1,0:T(8,128)(2,1)S(1)} %collective-permute-done.2.refs_2_), channel_id=1, source_target_pairs={{128,0},{256,128},{384,256},{129,1},{257,129},{385,257},{130,2},{2... | collective-permute-start | bytes 688136 | tf_op jit(solution)/shard_map/ppermute | solution.py:23
  77.0 0.0 collective-permute-done.8.refs_4_
  77.0 3.1 %collective-permute-start.6 = (bf16[448,256]{1,0:T(8,128)(2,1)S(1)}, bf16[448,256]{1,0:T(8,128)(2,1)S(1)}, u32[]{:S(2)}, u32[]{:S(2)}) collective-permute-start(bf16[448,256]{1,0:T(8,128)(2,1)S(1)} %collective-permute-done.5.refs_3_), channel_id=1, source_target_pairs={{0,128},{128,256},{256,384},{1,129},{129,257},{257,385},{2,130},{1... | collective-permute-start | bytes 688136 | tf_op jit(solution)/shard_map/ppermute | solution.py:23
  80.0 0.0 collective-permute-done.9.refs_5_
  80.1 2.8 %collective-permute-start.7 = (bf16[448,256]{1,0:T(8,128)(2,1)S(1)}, bf16[448,256]{1,0:T(8,128)(2,1)S(1)}, u32[]{:S(2)}, u32[]{:S(2)}) collective-permute-start(bf16[448,256]{1,0:T(8,128)(2,1)S(1)} %collective-permute-done.5.refs_3_), channel_id=1, source_target_pairs={{128,0},{256,128},{384,256},{129,1},{257,129},{385,257},{130,2},{2... | collective-permute-start | bytes 688136 | tf_op jit(solution)/shard_map/ppermute | solution.py:23
  82.9 1.6 %shard_map.64.refs_6_ = f32[3,136,224]{2,1,0:T(8,128)S(1)} custom-call(s32[3]{0:T(128)S(1)} %pad_add_fusion.1.refs_0_, bf16[3,224,128]{2,1,0:T(8,128)(2,1)S(1)} %pad_maximum_fusion.4.refs_1_, bf16[448,256]{1,0:T(8,128)(2,1)S(1)} %bitcast.43), custom_call_target="tpu_custom_call" | custom-call | flops 128450560 | bytes 229376 | tf_op jit(solution)/shard_map/pallas_call | solution.py:97
  84.5 2.7 %shard_map.65 = f32[3,136,224]{2,1,0:T(8,128)S(1)} custom-call(s32[6]{0:T(128)S(1)} %stack.135.refs_0_, bf16[3,224,128]{2,1,0:T(8,128)(2,1)S(1)} %pad_maximum_fusion.4.refs_1_, bf16[448,256]{1,0:T(8,128)(2,1)S(1)} %collective-permute-done.2.refs_2_, bf16[448,256]{1,0:T(8,128)(2,1)S(1)} %collective-permute-done.5.refs_3_, ...), custom_call_target="tpu_custom_call" | custom-call | flops 513802240 | bytes 917504 | tf_op jit(solution)/shard_map/pallas_call | solution.py:97
  87.2 0.0 collective-permute-done.3.refs_2_
  87.2 0.0 collective-permute-done.4.refs_3_
  87.2 0.0 collective-permute-done.6.refs_4_
  87.2 2.2 %collective-permute-done.7.refs_5_ = bf16[448,256]{1,0:T(8,128)(2,1)S(1)} collective-permute-done((bf16[448,256]{1,0:T(8,128)(2,1)S(1)}, bf16[448,256]{1,0:T(8,128)(2,1)S(1)}, u32[]{:S(2)}, u32[]{:S(2)}) %collective-permute-start.7) | collective-permute-done | bytes 229408 | tf_op jit(solution)/shard_map/ppermute | solution.py:23
  89.4 0.6 shard_map.67
  90.0 2.1 %collective-permute-start.10 = (f32[1,136,224]{2,1,0:T(8,128)S(1)}, f32[1,136,224]{2,1,0:T(8,128)S(1)}, u32[]{:S(2)}, u32[]{:S(2)}) collective-permute-start(f32[1,136,224]{2,1,0:T(8,128)S(1)} %shard_map.67), channel_id=1, source_target_pairs={{0,16},{16,0},{1,17},{17,1},{2,18},{18,2},{3,19},{19,3},{4,20},{20... | collective-permute-start | bytes 365576 | tf_op jit(solution)/shard_map/ppermute | solution.py:29
  92.1 0.1 pad_add_fusion.flags_ref
  92.2 0.6 shard_map.66.own_ref
  92.9 4.1 %collective-permute-done.10.part_ref = f32[1,136,224]{2,1,0:T(8,128)S(1)} collective-permute-done((f32[1,136,224]{2,1,0:T(8,128)S(1)}, f32[1,136,224]{2,1,0:T(8,128)S(1)}, u32[]{:S(2)}, u32[]{:S(2)}) %collective-permute-start.10) | collective-permute-done | bytes 121888 | tf_op jit(solution)/shard_map/ppermute | solution.py:29
  96.9 0.8 shard_map.68
  97.8 6.6 %collective-permute-start.13 = (bf16[224,128]{1,0:T(8,128)(2,1)S(1)}, bf16[224,128]{1,0:T(8,128)(2,1)S(1)}, u32[]{:S(2)}, u32[]{:S(2)}) collective-permute-start(bf16[224,128]{1,0:T(8,128)(2,1)S(1)} %get-tuple-element.9), channel_id=1, source_target_pairs={{0,9},{9,0},{1,8},{8,1},{2,11},{11,2},{3,10},{10,3},{4,13},{13,4},... | collective-permute-start | bytes 172040 | tf_op jit(solution)/shard_map/ppermute | solution.py:231
  104.4 2.5 %collective-permute-start.11 = (bf16[224,128]{1,0:T(8,128)(2,1)S(1)}, bf16[224,128]{1,0:T(8,128)(2,1)S(1)}, u32[]{:S(2)}, u32[]{:S(2)}) collective-permute-start(bf16[224,128]{1,0:T(8,128)(2,1)S(1)} %get-tuple-element.9), channel_id=1, source_target_pairs={{0,8},{8,0},{1,9},{9,1},{2,10},{10,2},{3,11},{11,3},{4,12},{12,4},... | collective-permute-start | bytes 172040 | tf_op jit(solution)/shard_map/ppermute | solution.py:29
  106.9 2.7 %collective-permute-start.12 = (bf16[224,128]{1,0:T(8,128)(2,1)S(1)}, bf16[224,128]{1,0:T(8,128)(2,1)S(1)}, u32[]{:S(2)}, u32[]{:S(2)}) collective-permute-start(bf16[224,128]{1,0:T(8,128)(2,1)S(1)} %get-tuple-element.8), channel_id=1, source_target_pairs={{0,1},{1,0},{2,3},{3,2},{4,5},{5,4},{6,7},{7,6},{8,9},{9,8},{10,11... | collective-permute-start | bytes 172040 | tf_op jit(solution)/shard_map/ppermute | solution.py:29
  109.6 0.0 collective-permute-done.14
  109.6 0.2 select_bitcast_fusion.1
  109.7 0.2 pad_maximum_fusion
  109.9 0.0 collective-permute-done.13
  109.9 7.6 %collective-permute-done.12 = bf16[224,128]{1,0:T(8,128)(2,1)S(1)} collective-permute-done((bf16[224,128]{1,0:T(8,128)(2,1)S(1)}, bf16[224,128]{1,0:T(8,128)(2,1)S(1)}, u32[]{:S(2)}, u32[]{:S(2)}) %collective-permute-start.12) | collective-permute-done | bytes 57376 | tf_op jit(solution)/shard_map/ppermute | solution.py:29
  117.5 0.0 collective-permute-done.11
  117.6 14.7 %all-gather = bf16[16,224,128]{2,1,0:T(8,128)(2,1)S(1)} all-gather(bf16[4,224,128]{2,1,0:T(8,128)(2,1)S(1)} %pad_maximum_fusion.2), channel_id=2, replica_groups=mesh['t'=4,'u'=4,'w'=2,'c'=2,'x'=4,'h'=2] {'x'}, dimensions={0}, use_global_device_ids=true | all-gather | bytes 1146880 | tf_op jit(solution)/shard_map/all_gather | solution.py:233
  132.3 1.5 %shard_map.69 = bf16[224,384]{1,0:T(8,128)(2,1)} custom-call(s32[1]{0:T(128)} %bitcast.order_ref, bf16[4,4,224,128]{3,2,1,0:T(8,128)(2,1)S(1)} %bitcast.38, bf16[2048,384]{1,0:T(8,128)(2,1)S(1)} %bitcast.37, f32[1,384]{1,0:T(1,128)S(1)} %broadcast_in_dim.3.gate_ref), custom_call_target="tpu_custom_call" | custom-call | tf_op jit(solution)/shard_map/pallas_call | solution.py:158
  (12 shorter events, 0.2 us)
Async XLA Ops:
  0.0 48.6 %copy-start.1 = (s32[2,3]{1,0:T(2,128)S(1)}, s32[2,3]{1,0:T(2,128)}, u32[]{:S(2)}) copy-start(s32[2,3]{1,0:T(2,128)} %param.9) | copy-start | bytes 76
  1.8 67.1 %copy-start = (f32[384]{0:T(512)S(1)}, f32[384]{0:T(512)}, u32[]{:S(2)}) copy-start(f32[384]{0:T(512)} %param.11) | copy-start | bytes 4612
  1.9 46.8 %collective-permute-start = (bf16[224,384]{1,0:T(8,128)(2,1)S(1)}, bf16[224,384]{1,0:T(8,128)(2,1)S(1)}, u32[]{:S(2)}, u32[]{:S(2)}) collective-permute-start(bf16[224,384]{1,0:T(8,128)(2,1)S(1)} %pad_maximum_fusion.3), channel_id=1, source_target_pairs={{0,8},{8,0},{1,9},{9,1},{2,10},{10,2},{3,11},{11,3},{4,12},{12,4},... | collective-permute-start | bytes 516104 | tf_op jit(solution)/shard_map/ppermute | solution.py:29
  48.7 22.4 %collective-permute-start.2 = (bf16[448,256]{1,0:T(8,128)(2,1)S(1)}, bf16[448,256]{1,0:T(8,128)(2,1)S(1)}, u32[]{:S(2)}, u32[]{:S(2)}) collective-permute-start(bf16[448,256]{1,0:T(8,128)(2,1)S(1)} %bitcast.39), channel_id=1, source_target_pairs={{0,32},{32,64},{64,96},{1,33},{33,65},{65,97},{2,34},{34,66},{66,9... | collective-permute-start | bytes 688136 | tf_op jit(solution)/shard_map/ppermute | solution.py:23
  53.3 20.9 %collective-permute-start.5 = (bf16[448,256]{1,0:T(8,128)(2,1)S(1)}, bf16[448,256]{1,0:T(8,128)(2,1)S(1)}, u32[]{:S(2)}, u32[]{:S(2)}) collective-permute-start(bf16[448,256]{1,0:T(8,128)(2,1)S(1)} %bitcast.40), channel_id=1, source_target_pairs={{32,0},{64,32},{96,64},{33,1},{65,33},{97,65},{34,2},{66,34},{98,6... | collective-permute-start | bytes 688136 | tf_op jit(solution)/shard_map/ppermute | solution.py:23
  55.5 21.5 %collective-permute-start.8 = (bf16[448,256]{1,0:T(8,128)(2,1)S(1)}, bf16[448,256]{1,0:T(8,128)(2,1)S(1)}, u32[]{:S(2)}, u32[]{:S(2)}) collective-permute-start(bf16[448,256]{1,0:T(8,128)(2,1)S(1)} %bitcast.41), channel_id=1, source_target_pairs={{0,128},{128,256},{256,384},{1,129},{129,257},{257,385},{2,130},{1... | collective-permute-start | bytes 688136 | tf_op jit(solution)/shard_map/ppermute | solution.py:23
  57.8 22.3 %collective-permute-start.9 = (bf16[448,256]{1,0:T(8,128)(2,1)S(1)}, bf16[448,256]{1,0:T(8,128)(2,1)S(1)}, u32[]{:S(2)}, u32[]{:S(2)}) collective-permute-start(bf16[448,256]{1,0:T(8,128)(2,1)S(1)} %bitcast.42), channel_id=1, source_target_pairs={{128,0},{256,128},{384,256},{129,1},{257,129},{385,257},{130,2},{2... | collective-permute-start | bytes 688136 | tf_op jit(solution)/shard_map/ppermute | solution.py:23
  61.4 7.7 %collective-permute-start.1 = (bf16[1,224,128]{2,1,0:T(8,128)(2,1)S(1)}, bf16[1,224,128]{2,1,0:T(8,128)(2,1)S(1)}, u32[]{:S(2)}, u32[]{:S(2)}) collective-permute-start(bf16[1,224,128]{2,1,0:T(8,128)(2,1)S(1)} %fusion), channel_id=1, source_target_pairs={{0,16},{16,0},{1,17},{17,1},{2,18},{18,2},{3,19},{19,3},{4,20},{20... | collective-permute-start | bytes 172040 | tf_op jit(solution)/shard_map/ppermute | solution.py:29
  69.1 40.5 %collective-permute-start.14 = (bf16[4,8,32,384]{3,2,1,0:T(8,128)(2,1)S(1)}, bf16[4,8,32,384]{3,2,1,0:T(8,128)(2,1)S(1)}, u32[]{:S(2)}, u32[]{:S(2)}) collective-permute-start(bf16[4,8,32,384]{3,2,1,0:T(8,128)(2,1)S(1)} %bitcast.44), channel_id=1, source_target_pairs={{0,8},{8,0},{1,9},{9,1},{2,10},{10,2},{3,11},{11,3},{4,12},{12,4},... | collective-permute-start | bytes 2359304 | tf_op jit(solution)/shard_map/ppermute | solution.py:29
  71.1 16.1 %collective-permute-start.3 = (bf16[448,256]{1,0:T(8,128)(2,1)S(1)}, bf16[448,256]{1,0:T(8,128)(2,1)S(1)}, u32[]{:S(2)}, u32[]{:S(2)}) collective-permute-start(bf16[448,256]{1,0:T(8,128)(2,1)S(1)} %collective-permute-done.2.refs_2_), channel_id=1, source_target_pairs={{0,128},{128,256},{256,384},{1,129},{129,257},{257,385},{2,130},{1... | collective-permute-start | bytes 688136 | tf_op jit(solution)/shard_map/ppermute | solution.py:23
  74.2 13.1 %collective-permute-start.4 = (bf16[448,256]{1,0:T(8,128)(2,1)S(1)}, bf16[448,256]{1,0:T(8,128)(2,1)S(1)}, u32[]{:S(2)}, u32[]{:S(2)}) collective-permute-start(bf16[448,256]{1,0:T(8,128)(2,1)S(1)} %collective-permute-done.2.refs_2_), channel_id=1, source_target_pairs={{128,0},{256,128},{384,256},{129,1},{257,129},{385,257},{130,2},{2... | collective-permute-start | bytes 688136 | tf_op jit(solution)/shard_map/ppermute | solution.py:23
  77.0 10.3 %collective-permute-start.6 = (bf16[448,256]{1,0:T(8,128)(2,1)S(1)}, bf16[448,256]{1,0:T(8,128)(2,1)S(1)}, u32[]{:S(2)}, u32[]{:S(2)}) collective-permute-start(bf16[448,256]{1,0:T(8,128)(2,1)S(1)} %collective-permute-done.5.refs_3_), channel_id=1, source_target_pairs={{0,128},{128,256},{256,384},{1,129},{129,257},{257,385},{2,130},{1... | collective-permute-start | bytes 688136 | tf_op jit(solution)/shard_map/ppermute | solution.py:23
  80.1 9.3 %collective-permute-start.7 = (bf16[448,256]{1,0:T(8,128)(2,1)S(1)}, bf16[448,256]{1,0:T(8,128)(2,1)S(1)}, u32[]{:S(2)}, u32[]{:S(2)}) collective-permute-start(bf16[448,256]{1,0:T(8,128)(2,1)S(1)} %collective-permute-done.5.refs_3_), channel_id=1, source_target_pairs={{128,0},{256,128},{384,256},{129,1},{257,129},{385,257},{130,2},{2... | collective-permute-start | bytes 688136 | tf_op jit(solution)/shard_map/ppermute | solution.py:23
  90.0 6.9 %collective-permute-start.10 = (f32[1,136,224]{2,1,0:T(8,128)S(1)}, f32[1,136,224]{2,1,0:T(8,128)S(1)}, u32[]{:S(2)}, u32[]{:S(2)}) collective-permute-start(f32[1,136,224]{2,1,0:T(8,128)S(1)} %shard_map.67), channel_id=1, source_target_pairs={{0,16},{16,0},{1,17},{17,1},{2,18},{18,2},{3,19},{19,3},{4,20},{20... | collective-permute-start | bytes 365576 | tf_op jit(solution)/shard_map/ppermute | solution.py:29
  97.8 12.2 %collective-permute-start.13 = (bf16[224,128]{1,0:T(8,128)(2,1)S(1)}, bf16[224,128]{1,0:T(8,128)(2,1)S(1)}, u32[]{:S(2)}, u32[]{:S(2)}) collective-permute-start(bf16[224,128]{1,0:T(8,128)(2,1)S(1)} %get-tuple-element.9), channel_id=1, source_target_pairs={{0,9},{9,0},{1,8},{8,1},{2,11},{11,2},{3,10},{10,3},{4,13},{13,4},... | collective-permute-start | bytes 172040 | tf_op jit(solution)/shard_map/ppermute | solution.py:231
  104.4 13.2 %collective-permute-start.11 = (bf16[224,128]{1,0:T(8,128)(2,1)S(1)}, bf16[224,128]{1,0:T(8,128)(2,1)S(1)}, u32[]{:S(2)}, u32[]{:S(2)}) collective-permute-start(bf16[224,128]{1,0:T(8,128)(2,1)S(1)} %get-tuple-element.9), channel_id=1, source_target_pairs={{0,8},{8,0},{1,9},{9,1},{2,10},{10,2},{3,11},{11,3},{4,12},{12,4},... | collective-permute-start | bytes 172040 | tf_op jit(solution)/shard_map/ppermute | solution.py:29
  106.9 10.7 %collective-permute-start.12 = (bf16[224,128]{1,0:T(8,128)(2,1)S(1)}, bf16[224,128]{1,0:T(8,128)(2,1)S(1)}, u32[]{:S(2)}, u32[]{:S(2)}) collective-permute-start(bf16[224,128]{1,0:T(8,128)(2,1)S(1)} %get-tuple-element.8), channel_id=1, source_target_pairs={{0,1},{1,0},{2,3},{3,2},{4,5},{5,4},{6,7},{7,6},{8,9},{9,8},{10,11... | collective-permute-start | bytes 172040 | tf_op jit(solution)/shard_map/ppermute | solution.py:29

commit v2 on v0

v2 whole, which is shorter than its diff:
```python
import functools
import math

import jax
import jax.numpy as jnp
from jax import lax
from jax.experimental import pallas as pl
from jax.experimental.pallas import tpu as pltpu
from jax.sharding import Mesh
from jax.sharding import PartitionSpec as P

HD = 128
ROWS = 224
LANES = 256
STATE = HD + 8
SCALE = math.log2(math.e) / math.sqrt(HD)
ROW_AXES = ("t", "u", "w", "c")
COL_AXES = ("x", "h")
VMEM_LIMIT = 32 * 1024 * 1024


def swapped(value, axis, flip):
    count = lax.axis_size(axis)
    return lax.ppermute(value, axis, [(i, i ^ flip) for i in range(count)])


def middle_swapped(value, axis):
    return lax.ppermute(value, axis, [(1, 2), (2, 1)])


def joined_kernel(*refs):
    start = 0
    for ref in refs[:-1]:
        refs[-1][start : start + ref.shape[0]] = ref[...]
        start += ref.shape[0]


def joined(*parts):
    vmem = pl.BlockSpec(memory_space=pltpu.VMEM)
    first = parts[0]
    rows = sum(p.shape[0] for p in parts)
    return pl.pallas_call(
        joined_kernel,
        out_shape=jax.ShapeDtypeStruct((rows, *first.shape[1:]), first.dtype),
        in_specs=[vmem] * len(parts),
        out_specs=vmem,
        compiler_params=pltpu.CompilerParams(vmem_limit_bytes=VMEM_LIMIT),
    )(*parts)


def beside_kernel(left_ref, right_ref, out_ref, sems):
    width = left_ref.shape[1]
    copies = [
        pltpu.make_async_copy(ref, out_ref.at[:, pl.ds(at * width, width)], sems.at[at])
        for at, ref in enumerate((left_ref, right_ref))
    ]
    for copy in copies:
        copy.start()
    for copy in copies:
        copy.wait()


def beside(left, right):
    return pl.pallas_call(
        beside_kernel,
        out_shape=jax.ShapeDtypeStruct((left.shape[0], 2 * left.shape[1]), left.dtype),
        in_specs=[pl.BlockSpec(memory_space=pl.ANY)] * 2,
        out_specs=pl.BlockSpec(memory_space=pltpu.VMEM),
        scratch_shapes=[pltpu.SemaphoreType.DMA((2,))],
    )(left, right)


def online_update(state_ref, head, lanes, queries, keys, values, first, last_ok):
    scores = lax.dot_general(
        keys, queries, (((1,), (1,)), ((), ())), preferred_element_type=jnp.float32
    )
    if last_ok is not None:
        spare = 2 * ROWS
        scores = jnp.concatenate(
            [scores[:spare], scores[spare:] + jnp.where(last_ok, 0.0, -jnp.inf)]
        )
    new_max = jnp.max(scores, axis=0, keepdims=True)
    if not first:
        old_max = state_ref[head, HD : HD + 1, lanes]
        new_max = jnp.maximum(old_max, new_max)
        factor = jnp.exp2((old_max - new_max) * SCALE)
    weights = jnp.exp2((scores - new_max) * SCALE)
    total = jnp.sum(weights, axis=0, keepdims=True)
    added = lax.dot_general(
        values,
        weights.astype(jnp.bfloat16),
        (((0,), (0,)), ((), ())),
        preferred_element_type=jnp.float32,
    )
    if not first:
        added = state_ref[head, 0:HD, lanes] * factor + added
        total = state_ref[head, HD + 1 : HD + 2, lanes] * factor + total
    state_ref[head, 0:HD, lanes] = added
    state_ref[head, HD : HD + 1, lanes] = new_max
    state_ref[head, HD + 1 : HD + 2, lanes] = total


def attend_kernel(low, high, stage, pos_ref, ext_ref, *refs):
    tiles = high - low
    first = stage == 0
    if first:
        q_refs, (kv_ref, state_ref, q_ref) = refs[:tiles], refs[tiles:]
        for tile in range(tiles):
            q_ref[tile * LANES : tile * LANES + ROWS, :] = q_refs[tile][...]
            q_ref[tile * LANES + ROWS : (tile + 1) * LANES, :] = jnp.zeros(
                (LANES - ROWS, 2 * HD), jnp.bfloat16
            )
        state_ref[...] = jnp.zeros(state_ref.shape, jnp.float32)
        state_ref[:, HD : HD + 1, :] = jnp.full((2, 1, tiles * LANES), -jnp.inf, jnp.float32)
    else:
        q_ref, kv_ref, old_ref, state_ref = refs
        state_ref[...] = old_ref[:, :, low * LANES : high * LANES]
    time_pos, height_pos = pos_ref[0], pos_ref[1]
    inner_t = ((time_pos == 1) | (time_pos == 2)).astype(jnp.int32)
    inner_u = (height_pos == 1) | (height_pos == 2)

    def one_head(head, _):
        reach_t, reach_u, reach_w = (ext_ref[head, i] for i in range(3))
        gate = (1, reach_t, reach_t * inner_t)[stage]
        head_lanes = pl.ds(pl.multiple_of(head * HD, HD), HD)
        value_lanes = pl.ds(pl.multiple_of((head + 2) * HD, HD), HD)
        for tall in (0, 1):
            for wide in (0, 1):
                if (low > 0 and not wide) or (high == 1 and wide):
                    continue
                right = high if wide else 1
                chosen = (reach_u == tall) & (gate > 0)
                if high > 1:
                    chosen &= reach_w == wide

                @pl.when(chosen)
                def _(tall=tall, right=right):
                    rows = slice(0, 3 * ROWS if tall else ROWS)
                    online_update(
                        state_ref,
                        head,
                        slice(0, (right - low) * LANES),
                        q_ref[low * LANES : right * LANES, head_lanes],
                        kv_ref[rows, head_lanes],
                        kv_ref[rows, value_lanes],
                        first,
                        inner_u if tall else None,
                    )

        return 0

    lax.fori_loop(0, 2, one_head, 0)


def attend(pos, extents, queries, low, high, stage, key_values, state=None):
    tiles = high - low
    smem = pl.BlockSpec(memory_space=pltpu.SMEM)
    vmem = pl.BlockSpec(memory_space=pltpu.VMEM)
    out = jax.ShapeDtypeStruct((2, STATE, tiles * LANES), jnp.float32)
    if stage == 0:
        operands = [*queries, key_values]
        out = (out, jax.ShapeDtypeStruct((tiles * LANES, 2 * HD), jnp.bfloat16))
    else:
        operands = [queries, key_values, state]
    pairs = 3 * tiles * 2
    return pl.pallas_call(
        functools.partial(attend_kernel, low, high, stage),
        out_shape=out,
        in_specs=[smem, smem] + [vmem] * len(operands),
        out_specs=(vmem, vmem) if stage == 0 else vmem,
        compiler_params=pltpu.CompilerParams(vmem_limit_bytes=VMEM_LIMIT),
        cost_estimate=pl.CostEstimate(
            flops=pairs * ROWS * ROWS * HD * 4,
            bytes_accessed=12 * ROWS * HD * 2,
            transcendentals=pairs * ROWS * ROWS,
        ),
    )(pos, extents, *operands)


def finish_kernel(pos_ref, own_ref, core_ref, face_ref, out_ref):
    faces = pos_ref[2] != pos_ref[3]
    for head in range(2):
        maxes = [r[head, HD : HD + 1, :] for r in (own_ref, core_ref, face_ref)]
        maxes[2] = jnp.where(faces, maxes[2], -jnp.inf)
        top = jnp.maximum(jnp.maximum(maxes[0], maxes[1]), maxes[2])
        factors = [jnp.exp2((m - top) * SCALE) for m in maxes]
        total = sum(
            r[head, HD + 1 : HD + 2, :] * f for r, f in zip((own_ref, core_ref, face_ref), factors)
        )
        summed = sum(r[head, 0:HD, :] * f for r, f in zip((own_ref, core_ref, face_ref), factors))
        rows = jnp.transpose(summed / total)
        out_ref[:, head * HD : (head + 1) * HD] = rows[:ROWS].astype(jnp.bfloat16)


def finish(pos, own, from_core, from_face):
    vmem = pl.BlockSpec(memory_space=pltpu.VMEM)
    return pl.pallas_call(
        finish_kernel,
        out_shape=jax.ShapeDtypeStruct((ROWS, 2 * HD), jnp.bfloat16),
        in_specs=[pl.BlockSpec(memory_space=pltpu.SMEM), vmem, vmem, vmem],
        out_specs=vmem,
        compiler_params=pltpu.CompilerParams(vmem_limit_bytes=VMEM_LIMIT),
    )(pos, own, from_core, from_face)


def arrange_kernel(pos_ref, mine_ref, other_ref, out_ref):
    time_pos, height_pos, width_pair, core = (pos_ref[i] for i in range(4))
    depth = mine_ref.shape[1]
    for flip_c, ref in enumerate((mine_ref, other_ref)):

        def one_block(at, _, ref=ref, flip_c=flip_c):
            t = time_pos ^ (2 * (at & 1)) ^ ((at >> 3) & 1)
            u = height_pos ^ ((at >> 1) & 1) ^ (3 * ((at >> 2) & 1))
            w = width_pair ^ ((at >> 4) & 1)
            to = ((t * 4 + u) * 2 + w) * 2 + (core ^ flip_c)
            out_ref[pl.ds(pl.multiple_of(to * depth, depth), depth), :] = ref[at]
            return 0

        lax.fori_loop(0, mine_ref.shape[0], one_block, 0, unroll=4)


def arranged_weight(pos, mine, other):
    vmem = pl.BlockSpec(memory_space=pltpu.VMEM)
    return pl.pallas_call(
        arrange_kernel,
        out_shape=jax.ShapeDtypeStruct(
            (2 * mine.shape[0] * mine.shape[1], mine.shape[2]), mine.dtype
        ),
        in_specs=[pl.BlockSpec(memory_space=pltpu.SMEM), vmem, vmem],
        out_specs=vmem,
        compiler_params=pltpu.CompilerParams(vmem_limit_bytes=VMEM_LIMIT),
    )(pos, mine, other)


def project_kernel(groups, pos_ref, rows_ref, weight_ref, gate_ref, out_ref):
    depth = rows_ref.shape[3]
    total = jnp.zeros(out_ref.shape, jnp.float32)
    for x in range(groups):
        for slot in range(2):
            start = (x * 2 + (slot ^ pos_ref[4])) * depth
            weight = weight_ref[pl.ds(pl.multiple_of(start, depth), depth), :]
            total += jnp.dot(rows_ref[x, slot], weight, preferred_element_type=jnp.float32)
    out_ref[...] = (total * gate_ref[...]).astype(jnp.bfloat16)


def project(pos, rows, weight, gate):
    vmem = pl.BlockSpec(memory_space=pltpu.VMEM)
    return pl.pallas_call(
        functools.partial(project_kernel, rows.shape[0]),
        out_shape=jax.ShapeDtypeStruct((rows.shape[2], weight.shape[1]), jnp.bfloat16),
        in_specs=[pl.BlockSpec(memory_space=pltpu.SMEM), vmem, vmem, vmem],
        out_specs=vmem,
        compiler_params=pltpu.CompilerParams(vmem_limit_bytes=VMEM_LIMIT),
    )(pos, rows, weight, gate)


def after(value, other):
    return lax.optimization_barrier((value, other))[0]


def local(queries, key_rows, value_rows, extents, out_weight, gate_scale):
    pos = jnp.stack([lax.axis_index(a) for a in ("t", "u", "w", "c", "h")])

    own_kv = beside(key_rows, value_rows)
    up = swapped(own_kv, "u", 1)
    down = middle_swapped(own_kv, "u")
    facing = [(1, 2), (2, 1)]
    tiles_q = [
        queries,
        swapped(queries, "c", 1),
        lax.ppermute(queries, ("w", "c"), facing),
    ]
    weight = out_weight[None]
    weight_t = swapped(weight, "t", 2)

    up, tiles_q, weight_t = lax.optimization_barrier((up, tiles_q, weight_t))
    near = joined(own_kv, up, down)
    early = swapped(near, "t", 1)
    late = middle_swapped(near, "t")
    weight, weight_t, near = lax.optimization_barrier((weight, weight_t, near))
    weight = joined(weight, weight_t)
    weight_u = swapped(weight, "u", 1)
    state, all_q = attend(pos, extents, tiles_q, 0, 3, 0, near)
    weight = joined(weight, after(weight_u, state))
    state, weight = lax.optimization_barrier((state, weight))
    weight_u = swapped(weight, "u", 3)

    state = attend(pos, extents, all_q, 0, 3, 1, early, state)
    given = attend(pos, extents, all_q, 1, 3, 2, late, state)
    state, given, weight_u = lax.optimization_barrier((state, given, weight_u))
    from_core = swapped(given[:, :, :LANES], "c", 1)
    from_face = lax.ppermute(given[:, :, LANES:], ("w", "c"), facing)
    weight = joined(weight, weight_u)
    weight_t = swapped(weight, "t", 1)
    own = attend(pos, extents, all_q, 0, 1, 2, late, state)
    attended = finish(pos, own, from_core, from_face)

    across = swapped(attended, "h", 1)
    weight = joined(weight, after(weight_t, attended))
    weight_w = swapped(weight, "w", 1)
    rows = lax.all_gather(joined(attended[None], across[None]), "x", axis=0, tiled=False)
    weight = joined(weight, after(weight_w, rows))
    weight = arranged_weight(pos, weight, swapped(weight, "c", 1))
    return project(pos, rows, weight, gate_scale[None, :])


def solution(mesh):
    fine = Mesh(mesh.devices.reshape(4, 4, 2, 2, 4, 2), ROW_AXES + COL_AXES)
    in_specs = (
        P(ROW_AXES, COL_AXES),
        P(ROW_AXES, COL_AXES),
        P(ROW_AXES, COL_AXES),
        P(COL_AXES, None),
        P(ROW_AXES, COL_AXES),
        P(COL_AXES),
    )
    return jax.shard_map(
        local, mesh=fine, in_specs=in_specs, out_specs=P(ROW_AXES, COL_AXES), check_vma=False
    )
```

time: 296 us -> 95.4 us (0.32)
  the two profiles are of different devices: /device:TPU:80 before, /device:TPU:1 now
where the time goes in v2:
time: 95.4 us; the launch traced here: 94.9 us
  starting transfers between devices  63.2 us (66%)
  blocking collectives  10.9 us (11%)
  Pallas kernels  10.1 us (11%)
  waiting for transfers between devices  9.36 us (10%)
  local copies, waits for them, and re-layouts  1.08 us (1%)
    ppermute x11, starting transfers between devices, swapped(): return lax.ppermute(value, axis, [(i, i ^ flip) for i in range(count)])  54.4 us
    all_gather x1, blocking collectives, local(): lax.all_gather(joined(attended[None], across[None]), 'x', axis=0, tiled=F...  10.9 us
    ppermute x11, waiting for transfers between devices, swapped(): return lax.ppermute(value, axis, [(i, i ^ flip) for i in range(count)])  9.35 us
    ppermute x1, starting transfers between devices, local(): from_face = lax.ppermute(given[:, :, LANES:], ('w', 'c'), facing)  4.7 us
    pallas_call x4, Pallas kernels, attend(): pl.pallas_call(functools.partial(attend_kernel, low, high, stage), out_sh...  4.51 us
    ppermute x1, starting transfers between devices, local(): lax.ppermute(queries, ('w', 'c'), facing)  2.69 us
  transfers between devices with their start and end apart: 15, of which 5 were waited for; matrix products, arithmetic and copies ran while one was open for 0% of the time, Pallas kernels for 6%

profile of v2, /device:TPU:1, one launch (start us, length us, event | category | flops | bytes accessed | tf_op | source)
XLA Modules:
  0.0 94.9 jit_solution(6120176160615517851)
XLA Ops:
  0.0 0.0 copy-start.3
  0.0 0.0 copy-start.1
  0.0 0.0 copy-start.2
  0.0 1.7 %shard_map.64.refs_0_ = bf16[224,512]{1,0:T(8,128)(2,1)} custom-call(bf16[224,256]{1,0:T(8,128)(2,1)} %left_ref.1, bf16[224,256]{1,0:T(8,128)(2,1)} %right_ref.1), custom_call_target="tpu_custom_call" | custom-call | tf_op jit(solution)/shard_map/pallas_call | solution.py:64
  1.7 6.6 %collective-permute-start = (bf16[224,512]{1,0:T(8,128)(2,1)}, bf16[224,512]{1,0:T(8,128)(2,1)S(1)}, u32[]{:S(2)}, u32[]{:S(2)}) collective-permute-start(bf16[224,512]{1,0:T(8,128)(2,1)} %shard_map.64.refs_0_), channel_id=1, source_target_pairs={{0,32},{32,0},{64,96},{96,64},{1,33},{33,1},{65,97},{97,65},{2,34}... | collective-permute-start | bytes 688136 | tf_op jit(solution)/shard_map/ppermute | solution.py:24
  8.4 0.7 collective-permute-start.4
  9.0 4.1 %collective-permute-start.1 = (bf16[224,256]{1,0:T(8,128)(2,1)}, bf16[224,256]{1,0:T(8,128)(2,1)S(1)}, u32[]{:S(2)}, u32[]{:S(2)}) collective-permute-start(bf16[224,256]{1,0:T(8,128)(2,1)} %refs_0_), channel_id=1, source_target_pairs={{0,8},{8,0},{1,9},{9,1},{2,10},{10,2},{3,11},{11,3},{4,12},{12,4},... | collective-permute-start | bytes 344072 | tf_op jit(solution)/shard_map/ppermute | solution.py:24
  13.1 2.7 %collective-permute-start.2 = (bf16[224,256]{1,0:T(8,128)(2,1)}, bf16[224,256]{1,0:T(8,128)(2,1)S(1)}, u32[]{:S(2)}, u32[]{:S(2)}) collective-permute-start(bf16[224,256]{1,0:T(8,128)(2,1)} %refs_0_), channel_id=1, source_target_pairs={{8,16},{16,8},{9,17},{17,9},{10,18},{18,10},{11,19},{19,11},{12,20... | collective-permute-start | bytes 344072 | tf_op jit(solution)/shard_map/ppermute | solution.py:271
  15.8 4.2 %collective-permute-start.3 = (bf16[1,32,384]{2,1,0:T(8,128)(2,1)}, bf16[1,32,384]{2,1,0:T(8,128)(2,1)S(1)}, u32[]{:S(2)}, u32[]{:S(2)}) collective-permute-start(bf16[1,32,384]{2,1,0:T(8,128)(2,1)} %bitcast.12), channel_id=1, source_target_pairs={{0,256},{128,384},{256,0},{384,128},{1,257},{129,385},{257,1},{385... | collective-permute-start | bytes 73736 | tf_op jit(solution)/shard_map/ppermute | solution.py:24
  20.0 1.5 %collective-permute-done.3.refs_1_ = bf16[1,32,384]{2,1,0:T(8,128)(2,1)S(1)} collective-permute-done((bf16[1,32,384]{2,1,0:T(8,128)(2,1)}, bf16[1,32,384]{2,1,0:T(8,128)(2,1)S(1)}, u32[]{:S(2)}, u32[]{:S(2)}) %collective-permute-start.3) | collective-permute-done | bytes 24608 | tf_op jit(solution)/shard_map/ppermute | solution.py:24
  21.5 0.0 collective-permute-done.1.refs_1_
  21.5 0.0 collective-permute-done.2.refs_2_
  21.5 0.0 collective-permute-done.refs_1_
  21.5 0.0 collective-permute-done.4.refs_2_
  21.5 0.0 copy-start
  21.5 0.9 copy-done
  22.5 3.2 %collective-permute-start.6 = (bf16[672,512]{1,0:T(8,128)(2,1)S(1)}, bf16[672,512]{1,0:T(8,128)(2,1)S(1)}, u32[]{:S(2)}, u32[]{:S(2)}) collective-permute-start(bf16[672,512]{1,0:T(8,128)(2,1)S(1)} %shard_map.65.refs_3_), channel_id=1, source_target_pairs={{0,128},{128,0},{256,384},{384,256},{1,129},{129,1},{257,385},{385... | collective-permute-start | bytes 2064392 | tf_op jit(solution)/shard_map/ppermute | solution.py:24
  25.7 0.7 collective-permute-start.5
  26.4 0.0 copy-done.1
  26.5 9.7 %collective-permute-start.7 = (bf16[2,32,384]{2,1,0:T(8,128)(2,1)S(1)}, bf16[2,32,384]{2,1,0:T(8,128)(2,1)S(1)}, u32[]{:S(2)}, u32[]{:S(2)}) collective-permute-start(bf16[2,32,384]{2,1,0:T(8,128)(2,1)S(1)} %shard_map.67.refs_0_), channel_id=1, source_target_pairs={{0,32},{32,0},{64,96},{96,64},{1,33},{33,1},{65,97},{97,65},{2,34}... | collective-permute-start | bytes 147464 | tf_op jit(solution)/shard_map/ppermute | solution.py:24
  36.2 0.1 stack.23.pos_ref
  36.3 0.0 copy-done.3
  36.3 0.0 copy-done.2
  36.3 1.6 %shard_map.66 = (f32[2,136,768]{2,1,0:T(8,128)S(1)}, bf16[768,256]{1,0:T(8,128)(2,1)S(1)}) custom-call(s32[5]{0:T(128)S(1)} %stack.23.pos_ref, s32[2,3]{1,0:T(2,128)S(1)} %copy-done.2, bf16[224,256]{1,0:T(8,128)(2,1)S(1)} %copy-done.3, bf16[224,256]{1,0:T(8,128)(2,1)S(1)} %collective-permute-done.1.refs_1_, ...), custom_call_target="tpu_custom_call" | custom-call | flops 462422016 | bytes 688128 | tf_op jit(solution)/shard_map/pallas_call | solution.py:166
  37.9 0.0 collective-permute-done.7.refs_1_
  38.0 2.8 %collective-permute-start.8 = (bf16[4,32,384]{2,1,0:T(8,128)(2,1)S(1)}, bf16[4,32,384]{2,1,0:T(8,128)(2,1)S(1)}, u32[]{:S(2)}, u32[]{:S(2)}) collective-permute-start(bf16[4,32,384]{2,1,0:T(8,128)(2,1)S(1)} %shard_map.68.refs_0_), channel_id=1, source_target_pairs={{0,96},{32,64},{64,32},{96,0},{1,97},{33,65},{65,33},{97,1},{2,98}... | collective-permute-start | bytes 294920 | tf_op jit(solution)/shard_map/ppermute | solution.py:24
  40.7 0.5 collective-permute-done.6.refs_1_
  41.2 1.7 %shard_map.69.refs_2_ = f32[2,136,768]{2,1,0:T(8,128)S(1)} custom-call(s32[5]{0:T(128)S(1)} %stack.23.pos_ref, s32[2,3]{1,0:T(2,128)S(1)} %copy-done.2, bf16[768,256]{1,0:T(8,128)(2,1)S(1)} %get-tuple-element.29.refs_0_, bf16[672,512]{1,0:T(8,128)(2,1)S(1)} %collective-permute-done.6.refs_1_, f32[2,136,768]{2,1,0:T(8,128)S(1)} %get-tuple-element.34.refs_2_), custom_call_target="tpu_custom_call" | custom-call | flops 462422016 | bytes 688128 | tf_op jit(solution)/shard_map/pallas_call | solution.py:166
  42.9 0.0 collective-permute-done.5.refs_1_
  42.9 0.6 shard_map.70
  43.6 2.9 %collective-permute-done.8.refs_1_ = bf16[4,32,384]{2,1,0:T(8,128)(2,1)S(1)} collective-permute-done((bf16[4,32,384]{2,1,0:T(8,128)(2,1)S(1)}, bf16[4,32,384]{2,1,0:T(8,128)(2,1)S(1)}, u32[]{:S(2)}, u32[]{:S(2)}) %collective-permute-start.8) | collective-permute-done | bytes 98336 | tf_op jit(solution)/shard_map/ppermute | solution.py:24
  46.5 4.7 %collective-permute-start.10 = (f32[2,136,256]{2,1,0:T(8,128)S(1)}, f32[2,136,256]{2,1,0:T(8,128)S(1)}, u32[]{:S(2)}, u32[]{:S(2)}) collective-permute-start(f32[2,136,256]{2,1,0:T(8,128)S(1)} %get-tuple-element.41), channel_id=1, source_target_pairs={{8,16},{16,8},{9,17},{17,9},{10,18},{18,10},{11,19},{19,11},{12,20... | collective-permute-start | bytes 835592 | tf_op jit(solution)/shard_map/ppermute | solution.py:292
  51.3 1.9 %collective-permute-start.9 = (f32[2,136,256]{2,1,0:T(8,128)S(1)}, f32[2,136,256]{2,1,0:T(8,128)S(1)}, u32[]{:S(2)}, u32[]{:S(2)}) collective-permute-start(f32[2,136,256]{2,1,0:T(8,128)S(1)} %get-tuple-element.42), channel_id=1, source_target_pairs={{0,8},{8,0},{1,9},{9,1},{2,10},{10,2},{3,11},{11,3},{4,12},{12,4},... | collective-permute-start | bytes 835592 | tf_op jit(solution)/shard_map/ppermute | solution.py:24
  53.2 6.1 %collective-permute-start.12 = (bf16[8,32,384]{2,1,0:T(8,128)(2,1)S(1)}, bf16[8,32,384]{2,1,0:T(8,128)(2,1)S(1)}, u32[]{:S(2)}, u32[]{:S(2)}) collective-permute-start(bf16[8,32,384]{2,1,0:T(8,128)(2,1)S(1)} %shard_map.74.refs_0_), channel_id=1, source_target_pairs={{0,128},{128,0},{256,384},{384,256},{1,129},{129,1},{257,385},{385... | collective-permute-start | bytes 589832 | tf_op jit(solution)/shard_map/ppermute | solution.py:24
  59.3 0.6 shard_map.71.own_ref
  59.9 0.0 collective-permute-done.10.face_ref
  60.0 0.0 collective-permute-done.9.core_ref
  60.0 0.7 shard_map.72
  60.7 5.2 %collective-permute-start.11 = (bf16[224,256]{1,0:T(8,128)(2,1)S(1)}, bf16[224,256]{1,0:T(8,128)(2,1)S(1)}, u32[]{:S(2)}, u32[]{:S(2)}) collective-permute-start(bf16[224,256]{1,0:T(8,128)(2,1)S(1)} %shard_map.72), channel_id=1, source_target_pairs={{0,1},{1,0},{2,3},{3,2},{4,5},{5,4},{6,7},{7,6},{8,9},{9,8},{10,11... | collective-permute-start | bytes 344072 | tf_op jit(solution)/shard_map/ppermute | solution.py:24
  65.9 0.0 collective-permute-done.12.refs_1_
  65.9 2.0 %collective-permute-start.13 = (bf16[16,32,384]{2,1,0:T(8,128)(2,1)S(1)}, bf16[16,32,384]{2,1,0:T(8,128)(2,1)S(1)}, u32[]{:S(2)}, u32[]{:S(2)}) collective-permute-start(bf16[16,32,384]{2,1,0:T(8,128)(2,1)S(1)} %shard_map.75.refs_0_), channel_id=1, source_target_pairs={{0,16},{16,0},{1,17},{17,1},{2,18},{18,2},{3,19},{19,3},{4,20},{20... | collective-permute-start | bytes 1179656 | tf_op jit(solution)/shard_map/ppermute | solution.py:24
  68.0 2.6 %collective-permute-done.11 = bf16[224,256]{1,0:T(8,128)(2,1)S(1)} collective-permute-done((bf16[224,256]{1,0:T(8,128)(2,1)S(1)}, bf16[224,256]{1,0:T(8,128)(2,1)S(1)}, u32[]{:S(2)}, u32[]{:S(2)}) %collective-permute-start.11) | collective-permute-done | bytes 114720 | tf_op jit(solution)/shard_map/ppermute | solution.py:24
  70.5 0.0 copy-start.4
  70.6 10.9 %all-gather = bf16[8,224,256]{2,1,0:T(8,128)(2,1)S(1)} all-gather(bf16[2,224,256]{2,1,0:T(8,128)(2,1)S(1)} %shard_map.73), channel_id=2, replica_groups=mesh['t'=4,'u'=4,'w'=2,'c'=2,'x'=4,'h'=2] {'x'}, dimensions={0}, use_global_device_ids=true | all-gather | bytes 1146880 | tf_op jit(solution)/shard_map/all_gather | solution.py:301
  81.5 0.0 collective-permute-done.13.refs_1_
  81.5 0.1 shard_map.76.mine_ref
  81.5 8.5 %collective-permute-start.14 = (bf16[32,32,384]{2,1,0:T(8,128)(2,1)S(1)}, bf16[32,32,384]{2,1,0:T(8,128)(2,1)S(1)}, u32[]{:S(2)}, u32[]{:S(2)}) collective-permute-start(bf16[32,32,384]{2,1,0:T(8,128)(2,1)S(1)} %shard_map.76.mine_ref), channel_id=1, source_target_pairs={{0,8},{8,0},{1,9},{9,1},{2,10},{10,2},{3,11},{11,3},{4,12},{12,4},... | collective-permute-start | bytes 2359304 | tf_op jit(solution)/shard_map/ppermute | solution.py:24
  90.0 0.0 copy-done.4
  90.0 1.9 %collective-permute-done.14.other_ref = bf16[32,32,384]{2,1,0:T(8,128)(2,1)S(1)} collective-permute-done((bf16[32,32,384]{2,1,0:T(8,128)(2,1)S(1)}, bf16[32,32,384]{2,1,0:T(8,128)(2,1)S(1)}, u32[]{:S(2)}, u32[]{:S(2)}) %collective-permute-start.14) | collective-permute-done | bytes 786464 | tf_op jit(solution)/shard_map/ppermute | solution.py:24
  91.9 1.1 %shard_map.77.weight_ref = bf16[2048,384]{1,0:T(8,128)(2,1)S(1)} custom-call(s32[5]{0:T(128)S(1)} %stack.23.pos_ref, bf16[32,32,384]{2,1,0:T(8,128)(2,1)S(1)} %shard_map.76.mine_ref, bf16[32,32,384]{2,1,0:T(8,128)(2,1)S(1)} %collective-permute-done.14.other_ref), custom_call_target="tpu_custom_call" | custom-call | tf_op jit(solution)/shard_map/pallas_call | solution.py:224
  93.0 1.9 %shard_map.78 = bf16[224,384]{1,0:T(8,128)(2,1)} custom-call(s32[5]{0:T(128)S(1)} %stack.23.pos_ref, bf16[4,2,224,256]{3,2,1,0:T(8,128)(2,1)S(1)} %bitcast.9, bf16[2048,384]{1,0:T(8,128)(2,1)S(1)} %shard_map.77.weight_ref, f32[1,384]{1,0:T(1,128)S(1)} %broadcast_in_dim.15.gate_ref), custom_call_target="tpu_custom_call" | custom-call | tf_op jit(solution)/shard_map/pallas_call | solution.py:248
  (8 shorter events, 0.2 us)
Async XLA Ops:
  0.0 36.3 %copy-start.3 = (bf16[224,256]{1,0:T(8,128)(2,1)S(1)}, bf16[224,256]{1,0:T(8,128)(2,1)}, u32[]{:S(2)}) copy-start(bf16[224,256]{1,0:T(8,128)(2,1)} %refs_0_) | copy-start | bytes 344068
  0.0 26.4 %copy-start.1 = (bf16[32,384]{1,0:T(8,128)(2,1)S(1)}, bf16[32,384]{1,0:T(8,128)(2,1)}, u32[]{:S(2)}) copy-start(bf16[32,384]{1,0:T(8,128)(2,1)} %param.10) | copy-start | bytes 73732
  0.0 36.3 %copy-start.2 = (s32[2,3]{1,0:T(2,128)S(1)}, s32[2,3]{1,0:T(2,128)}, u32[]{:S(2)}) copy-start(s32[2,3]{1,0:T(2,128)} %ext_ref.7) | copy-start | bytes 76
  1.7 19.8 %collective-permute-start = (bf16[224,512]{1,0:T(8,128)(2,1)}, bf16[224,512]{1,0:T(8,128)(2,1)S(1)}, u32[]{:S(2)}, u32[]{:S(2)}) collective-permute-start(bf16[224,512]{1,0:T(8,128)(2,1)} %shard_map.64.refs_0_), channel_id=1, source_target_pairs={{0,32},{32,0},{64,96},{96,64},{1,33},{33,1},{65,97},{97,65},{2,34}... | collective-permute-start | bytes 688136 | tf_op jit(solution)/shard_map/ppermute | solution.py:24
  8.4 13.2 %collective-permute-start.4 = (bf16[224,512]{1,0:T(8,128)(2,1)}, bf16[224,512]{1,0:T(8,128)(2,1)S(1)}, u32[]{:S(2)}, u32[]{:S(2)}) collective-permute-start(bf16[224,512]{1,0:T(8,128)(2,1)} %shard_map.64.refs_0_), channel_id=1, source_target_pairs={{32,64},{64,32},{33,65},{65,33},{34,66},{66,34},{35,67},{67,35},{3... | collective-permute-start | bytes 688136 | tf_op jit(solution)/shard_map/ppermute | solution.py:28
  9.0 12.5 %collective-permute-start.1 = (bf16[224,256]{1,0:T(8,128)(2,1)}, bf16[224,256]{1,0:T(8,128)(2,1)S(1)}, u32[]{:S(2)}, u32[]{:S(2)}) collective-permute-start(bf16[224,256]{1,0:T(8,128)(2,1)} %refs_0_), channel_id=1, source_target_pairs={{0,8},{8,0},{1,9},{9,1},{2,10},{10,2},{3,11},{11,3},{4,12},{12,4},... | collective-permute-start | bytes 344072 | tf_op jit(solution)/shard_map/ppermute | solution.py:24
  13.1 8.4 %collective-permute-start.2 = (bf16[224,256]{1,0:T(8,128)(2,1)}, bf16[224,256]{1,0:T(8,128)(2,1)S(1)}, u32[]{:S(2)}, u32[]{:S(2)}) collective-permute-start(bf16[224,256]{1,0:T(8,128)(2,1)} %refs_0_), channel_id=1, source_target_pairs={{8,16},{16,8},{9,17},{17,9},{10,18},{18,10},{11,19},{19,11},{12,20... | collective-permute-start | bytes 344072 | tf_op jit(solution)/shard_map/ppermute | solution.py:271
  15.8 5.7 %collective-permute-start.3 = (bf16[1,32,384]{2,1,0:T(8,128)(2,1)}, bf16[1,32,384]{2,1,0:T(8,128)(2,1)S(1)}, u32[]{:S(2)}, u32[]{:S(2)}) collective-permute-start(bf16[1,32,384]{2,1,0:T(8,128)(2,1)} %bitcast.12), channel_id=1, source_target_pairs={{0,256},{128,384},{256,0},{384,128},{1,257},{129,385},{257,1},{385... | collective-permute-start | bytes 73736 | tf_op jit(solution)/shard_map/ppermute | solution.py:24
  21.5 0.9 copy-start
  22.5 18.7 %collective-permute-start.6 = (bf16[672,512]{1,0:T(8,128)(2,1)S(1)}, bf16[672,512]{1,0:T(8,128)(2,1)S(1)}, u32[]{:S(2)}, u32[]{:S(2)}) collective-permute-start(bf16[672,512]{1,0:T(8,128)(2,1)S(1)} %shard_map.65.refs_3_), channel_id=1, source_target_pairs={{0,128},{128,0},{256,384},{384,256},{1,129},{129,1},{257,385},{385... | collective-permute-start | bytes 2064392 | tf_op jit(solution)/shard_map/ppermute | solution.py:24
  25.7 17.2 %collective-permute-start.5 = (bf16[672,512]{1,0:T(8,128)(2,1)S(1)}, bf16[672,512]{1,0:T(8,128)(2,1)S(1)}, u32[]{:S(2)}, u32[]{:S(2)}) collective-permute-start(bf16[672,512]{1,0:T(8,128)(2,1)S(1)} %shard_map.65.refs_3_), channel_id=1, source_target_pairs={{128,256},{256,128},{129,257},{257,129},{130,258},{258,130},{131,2... | collective-permute-start | bytes 2064392 | tf_op jit(solution)/shard_map/ppermute | solution.py:28
  26.5 11.5 %collective-permute-start.7 = (bf16[2,32,384]{2,1,0:T(8,128)(2,1)S(1)}, bf16[2,32,384]{2,1,0:T(8,128)(2,1)S(1)}, u32[]{:S(2)}, u32[]{:S(2)}) collective-permute-start(bf16[2,32,384]{2,1,0:T(8,128)(2,1)S(1)} %shard_map.67.refs_0_), channel_id=1, source_target_pairs={{0,32},{32,0},{64,96},{96,64},{1,33},{33,1},{65,97},{97,65},{2,34}... | collective-permute-start | bytes 147464 | tf_op jit(solution)/shard_map/ppermute | solution.py:24
  38.0 8.5 %collective-permute-start.8 = (bf16[4,32,384]{2,1,0:T(8,128)(2,1)S(1)}, bf16[4,32,384]{2,1,0:T(8,128)(2,1)S(1)}, u32[]{:S(2)}, u32[]{:S(2)}) collective-permute-start(bf16[4,32,384]{2,1,0:T(8,128)(2,1)S(1)} %shard_map.68.refs_0_), channel_id=1, source_target_pairs={{0,96},{32,64},{64,32},{96,0},{1,97},{33,65},{65,33},{97,1},{2,98}... | collective-permute-start | bytes 294920 | tf_op jit(solution)/shard_map/ppermute | solution.py:24
  46.5 13.4 %collective-permute-start.10 = (f32[2,136,256]{2,1,0:T(8,128)S(1)}, f32[2,136,256]{2,1,0:T(8,128)S(1)}, u32[]{:S(2)}, u32[]{:S(2)}) collective-permute-start(f32[2,136,256]{2,1,0:T(8,128)S(1)} %get-tuple-element.41), channel_id=1, source_target_pairs={{8,16},{16,8},{9,17},{17,9},{10,18},{18,10},{11,19},{19,11},{12,20... | collective-permute-start | bytes 835592 | tf_op jit(solution)/shard_map/ppermute | solution.py:292
  51.3 8.7 %collective-permute-start.9 = (f32[2,136,256]{2,1,0:T(8,128)S(1)}, f32[2,136,256]{2,1,0:T(8,128)S(1)}, u32[]{:S(2)}, u32[]{:S(2)}) collective-permute-start(f32[2,136,256]{2,1,0:T(8,128)S(1)} %get-tuple-element.42), channel_id=1, source_target_pairs={{0,8},{8,0},{1,9},{9,1},{2,10},{10,2},{3,11},{11,3},{4,12},{12,4},... | collective-permute-start | bytes 835592 | tf_op jit(solution)/shard_map/ppermute | solution.py:24
  53.2 12.7 %collective-permute-start.12 = (bf16[8,32,384]{2,1,0:T(8,128)(2,1)S(1)}, bf16[8,32,384]{2,1,0:T(8,128)(2,1)S(1)}, u32[]{:S(2)}, u32[]{:S(2)}) collective-permute-start(bf16[8,32,384]{2,1,0:T(8,128)(2,1)S(1)} %shard_map.74.refs_0_), channel_id=1, source_target_pairs={{0,128},{128,0},{256,384},{384,256},{1,129},{129,1},{257,385},{385... | collective-permute-start | bytes 589832 | tf_op jit(solution)/shard_map/ppermute | solution.py:24
  60.7 9.9 %collective-permute-start.11 = (bf16[224,256]{1,0:T(8,128)(2,1)S(1)}, bf16[224,256]{1,0:T(8,128)(2,1)S(1)}, u32[]{:S(2)}, u32[]{:S(2)}) collective-permute-start(bf16[224,256]{1,0:T(8,128)(2,1)S(1)} %shard_map.72), channel_id=1, source_target_pairs={{0,1},{1,0},{2,3},{3,2},{4,5},{5,4},{6,7},{7,6},{8,9},{9,8},{10,11... | collective-permute-start | bytes 344072 | tf_op jit(solution)/shard_map/ppermute | solution.py:24
  65.9 15.5 %collective-permute-start.13 = (bf16[16,32,384]{2,1,0:T(8,128)(2,1)S(1)}, bf16[16,32,384]{2,1,0:T(8,128)(2,1)S(1)}, u32[]{:S(2)}, u32[]{:S(2)}) collective-permute-start(bf16[16,32,384]{2,1,0:T(8,128)(2,1)S(1)} %shard_map.75.refs_0_), channel_id=1, source_target_pairs={{0,16},{16,0},{1,17},{17,1},{2,18},{18,2},{3,19},{19,3},{4,20},{20... | collective-permute-start | bytes 1179656 | tf_op jit(solution)/shard_map/ppermute | solution.py:24
  70.5 19.5 %copy-start.4 = (f32[384]{0:T(512)S(1)}, f32[384]{0:T(512)}, u32[]{:S(2)}) copy-start(f32[384]{0:T(512)} %param.11) | copy-start | bytes 4612
  81.5 10.4 %collective-permute-start.14 = (bf16[32,32,384]{2,1,0:T(8,128)(2,1)S(1)}, bf16[32,32,384]{2,1,0:T(8,128)(2,1)S(1)}, u32[]{:S(2)}, u32[]{:S(2)}) collective-permute-start(bf16[32,32,384]{2,1,0:T(8,128)(2,1)S(1)} %shard_map.76.mine_ref), channel_id=1, source_target_pairs={{0,8},{8,0},{1,9},{9,1},{2,10},{10,2},{3,11},{11,3},{4,12},{12,4},... | collective-permute-start | bytes 2359304 | tf_op jit(solution)/shard_map/ppermute | solution.py:24

commit v3 on v2

--- a/solution.py
+++ b/solution.py
@@ -271,14 +271,13 @@
         lax.ppermute(queries, ("w", "c"), facing),
     ]
     weight = out_weight[None]
-    weight_t = swapped(weight, "t", 2)
-
-    up, tiles_q, weight_t = lax.optimization_barrier((up, tiles_q, weight_t))
+    weight = joined(weight, swapped(weight, "t", 2))
+
+    down, tiles_q, weight = lax.optimization_barrier((down, tiles_q, weight))
     near = joined(own_kv, up, down)
     early = swapped(near, "t", 1)
     late = middle_swapped(near, "t")
-    weight, weight_t, near = lax.optimization_barrier((weight, weight_t, near))
-    weight = joined(weight, weight_t)
+    weight, near = lax.optimization_barrier((weight, near))
     weight_u = swapped(weight, "u", 1)
     state, all_q = attend(pos, extents, tiles_q, 0, 3, 0, near)
     weight = joined(weight, after(weight_u, state))
@@ -293,7 +292,7 @@
     weight = joined(weight, weight_u)
     weight_t = swapped(weight, "t", 1)
     own = attend(pos, extents, all_q, 0, 1, 2, late, state)
-    attended = finish(pos, own, from_core, from_face)
+    attended = finish(pos, own, after(from_core, own), from_face)
 
     across = swapped(attended, "h", 1)
     weight = joined(weight, after(weight_t, attended))

time: 95.4 us -> 95.5 us (level); the launches traced: 94.9 us -> 93.9 us
  starting transfers between devices: 63.2 us -> 53.6 us
  waiting for transfers between devices: 9.36 us -> 15.6 us
  blocking collectives: 10.9 us -> 12.7 us
    ppermute x11, starting transfers between devices: 54.4 us -> 46.4 us  [swapped(): return lax.ppermute(value, axis, [(i, i ^ flip) for i in range(count)])]
    ppermute x11, waiting for transfers between devices: 9.35 us -> 15.6 us  [swapped(): return lax.ppermute(value, axis, [(i, i ^ flip) for i in range(count)])]
    ppermute x1, starting transfers between devices: 4.7 us -> 2.86 us  [local(): from_face = lax.ppermute(given[:, :, LANES:], ('w', 'c'), facing)]
    all_gather x1, blocking collectives: 10.9 us -> 12.7 us  [local(): lax.all_gather(joined(attended[None], across[None]), 'x', axis=0, tiled=F...]
  transfers between devices with their start and end apart: 15 -> 15, of which waited for: 5 -> 5; matrix products, arithmetic and copies ran while one was open for 0% -> 0% of each run, Pallas kernels for 6% -> 5%
where the time goes in v3:
time: 95.5 us; the launch traced here: 93.9 us
  starting transfers between devices  53.6 us (56%)
  waiting for transfers between devices  15.6 us (16%)
  blocking collectives  12.7 us (13%)
  Pallas kernels  9.79 us (10%)
  local copies, waits for them, and re-layouts  1.81 us (2%)
    ppermute x11, starting transfers between devices, swapped(): return lax.ppermute(value, axis, [(i, i ^ flip) for i in range(count)])  46.4 us
    ppermute x11, waiting for transfers between devices, swapped(): return lax.ppermute(value, axis, [(i, i ^ flip) for i in range(count)])  15.6 us
    all_gather x1, blocking collectives, local(): lax.all_gather(joined(attended[None], across[None]), 'x', axis=0, tiled=F...  12.7 us
    pallas_call x4, Pallas kernels, attend(): pl.pallas_call(functools.partial(attend_kernel, low, high, stage), out_sh...  4.25 us
    ppermute x1, starting transfers between devices, local(): lax.ppermute(queries, ('w', 'c'), facing)  3 us
    ppermute x1, starting transfers between devices, local(): from_face = lax.ppermute(given[:, :, LANES:], ('w', 'c'), facing)  2.86 us
  transfers between devices with their start and end apart: 15, of which 5 were waited for; matrix products, arithmetic and copies ran while one was open for 0% of the time, Pallas kernels for 5%

profile of v3, /device:TPU:1, one launch (start us, length us, event | category | flops | bytes accessed | tf_op | source)
XLA Modules:
  0.0 93.9 jit_solution(5928577557882562225)
XLA Ops:
  0.0 0.0 copy-start.3
  0.0 0.0 copy-start.2
  0.0 1.7 %shard_map.64.refs_0_ = bf16[224,512]{1,0:T(8,128)(2,1)} custom-call(bf16[224,256]{1,0:T(8,128)(2,1)} %left_ref.1, bf16[224,256]{1,0:T(8,128)(2,1)} %right_ref.1), custom_call_target="tpu_custom_call" | custom-call | tf_op jit(solution)/shard_map/pallas_call | solution.py:64
  1.7 0.7 collective-permute-start
  2.4 13.0 %collective-permute-start.4 = (bf16[224,512]{1,0:T(8,128)(2,1)}, bf16[224,512]{1,0:T(8,128)(2,1)S(1)}, u32[]{:S(2)}, u32[]{:S(2)}) collective-permute-start(bf16[224,512]{1,0:T(8,128)(2,1)} %shard_map.64.refs_0_), channel_id=1, source_target_pairs={{0,32},{32,0},{64,96},{96,64},{1,33},{33,1},{65,97},{97,65},{2,34}... | collective-permute-start | bytes 688136 | tf_op jit(solution)/shard_map/ppermute | solution.py:24
  15.4 3.1 %collective-permute-start.1 = (bf16[224,256]{1,0:T(8,128)(2,1)}, bf16[224,256]{1,0:T(8,128)(2,1)S(1)}, u32[]{:S(2)}, u32[]{:S(2)}) collective-permute-start(bf16[224,256]{1,0:T(8,128)(2,1)} %refs_0_), channel_id=1, source_target_pairs={{0,8},{8,0},{1,9},{9,1},{2,10},{10,2},{3,11},{11,3},{4,12},{12,4},... | collective-permute-start | bytes 344072 | tf_op jit(solution)/shard_map/ppermute | solution.py:24
  18.5 3.0 %collective-permute-start.2 = (bf16[224,256]{1,0:T(8,128)(2,1)}, bf16[224,256]{1,0:T(8,128)(2,1)S(1)}, u32[]{:S(2)}, u32[]{:S(2)}) collective-permute-start(bf16[224,256]{1,0:T(8,128)(2,1)} %refs_0_), channel_id=1, source_target_pairs={{8,16},{16,8},{9,17},{17,9},{10,18},{18,10},{11,19},{19,11},{12,20... | collective-permute-start | bytes 344072 | tf_op jit(solution)/shard_map/ppermute | solution.py:271
  21.5 4.2 %collective-permute-start.3 = (bf16[1,32,384]{2,1,0:T(8,128)(2,1)}, bf16[1,32,384]{2,1,0:T(8,128)(2,1)S(1)}, u32[]{:S(2)}, u32[]{:S(2)}) collective-permute-start(bf16[1,32,384]{2,1,0:T(8,128)(2,1)} %bitcast.12), channel_id=1, source_target_pairs={{0,256},{128,384},{256,0},{384,128},{1,257},{129,385},{257,1},{385... | collective-permute-start | bytes 73736 | tf_op jit(solution)/shard_map/ppermute | solution.py:24
  25.8 1.5 %collective-permute-done.3.refs_1_ = bf16[1,32,384]{2,1,0:T(8,128)(2,1)S(1)} collective-permute-done((bf16[1,32,384]{2,1,0:T(8,128)(2,1)}, bf16[1,32,384]{2,1,0:T(8,128)(2,1)S(1)}, u32[]{:S(2)}, u32[]{:S(2)}) %collective-permute-start.3) | collective-permute-done | bytes 24608 | tf_op jit(solution)/shard_map/ppermute | solution.py:24
  27.2 0.0 copy-start.1
  27.2 0.7 copy-done.1
  28.0 0.0 collective-permute-done.1.refs_1_
  28.0 0.0 collective-permute-done.2.refs_2_
  28.0 0.0 collective-permute-done.refs_2_
  28.0 0.0 collective-permute-done.4.refs_1_
  28.0 0.0 copy-start
  28.0 0.9 copy-done
  29.0 3.2 %collective-permute-start.6 = (bf16[672,512]{1,0:T(8,128)(2,1)S(1)}, bf16[672,512]{1,0:T(8,128)(2,1)S(1)}, u32[]{:S(2)}, u32[]{:S(2)}) collective-permute-start(bf16[672,512]{1,0:T(8,128)(2,1)S(1)} %shard_map.66.refs_3_), channel_id=1, source_target_pairs={{0,128},{128,0},{256,384},{384,256},{1,129},{129,1},{257,385},{385... | collective-permute-start | bytes 2064392 | tf_op jit(solution)/shard_map/ppermute | solution.py:24
  32.2 0.7 collective-permute-start.5
  32.9 1.9 %collective-permute-start.7 = (bf16[2,32,384]{2,1,0:T(8,128)(2,1)S(1)}, bf16[2,32,384]{2,1,0:T(8,128)(2,1)S(1)}, u32[]{:S(2)}, u32[]{:S(2)}) collective-permute-start(bf16[2,32,384]{2,1,0:T(8,128)(2,1)S(1)} %shard_map.65.refs_0_), channel_id=1, source_target_pairs={{0,32},{32,0},{64,96},{96,64},{1,33},{33,1},{65,97},{97,65},{2,34}... | collective-permute-start | bytes 147464 | tf_op jit(solution)/shard_map/ppermute | solution.py:24
  34.8 0.1 stack.23.pos_ref
  34.9 0.0 copy-done.3
  34.9 0.0 copy-done.2
  34.9 1.5 %shard_map.67 = (f32[2,136,768]{2,1,0:T(8,128)S(1)}, bf16[768,256]{1,0:T(8,128)(2,1)S(1)}) custom-call(s32[5]{0:T(128)S(1)} %stack.23.pos_ref, s32[2,3]{1,0:T(2,128)S(1)} %copy-done.2, bf16[224,256]{1,0:T(8,128)(2,1)S(1)} %copy-done.3, bf16[224,256]{1,0:T(8,128)(2,1)S(1)} %collective-permute-done.1.refs_1_, ...), custom_call_target="tpu_custom_call" | custom-call | flops 462422016 | bytes 688128 | tf_op jit(solution)/shard_map/pallas_call | solution.py:166
  36.4 3.0 %collective-permute-done.7.refs_1_ = bf16[2,32,384]{2,1,0:T(8,128)(2,1)S(1)} collective-permute-done((bf16[2,32,384]{2,1,0:T(8,128)(2,1)S(1)}, bf16[2,32,384]{2,1,0:T(8,128)(2,1)S(1)}, u32[]{:S(2)}, u32[]{:S(2)}) %collective-permute-start.7) | collective-permute-done | bytes 49184 | tf_op jit(solution)/shard_map/ppermute | solution.py:24
  39.4 1.9 %collective-permute-start.8 = (bf16[4,32,384]{2,1,0:T(8,128)(2,1)S(1)}, bf16[4,32,384]{2,1,0:T(8,128)(2,1)S(1)}, u32[]{:S(2)}, u32[]{:S(2)}) collective-permute-start(bf16[4,32,384]{2,1,0:T(8,128)(2,1)S(1)} %shard_map.68.refs_0_), channel_id=1, source_target_pairs={{0,96},{32,64},{64,32},{96,0},{1,97},{33,65},{65,33},{97,1},{2,98}... | collective-permute-start | bytes 294920 | tf_op jit(solution)/shard_map/ppermute | solution.py:24
  41.3 6.3 %collective-permute-done.6.refs_1_ = bf16[672,512]{1,0:T(8,128)(2,1)S(1)} collective-permute-done((bf16[672,512]{1,0:T(8,128)(2,1)S(1)}, bf16[672,512]{1,0:T(8,128)(2,1)S(1)}, u32[]{:S(2)}, u32[]{:S(2)}) %collective-permute-start.6) | collective-permute-done | bytes 688160 | tf_op jit(solution)/shard_map/ppermute | solution.py:24
  47.6 1.5 %shard_map.69.refs_2_ = f32[2,136,768]{2,1,0:T(8,128)S(1)} custom-call(s32[5]{0:T(128)S(1)} %stack.23.pos_ref, s32[2,3]{1,0:T(2,128)S(1)} %copy-done.2, bf16[768,256]{1,0:T(8,128)(2,1)S(1)} %get-tuple-element.29.refs_0_, bf16[672,512]{1,0:T(8,128)(2,1)S(1)} %collective-permute-done.6.refs_1_, f32[2,136,768]{2,1,0:T(8,128)S(1)} %get-tuple-element.33.refs_2_), custom_call_target="tpu_custom_call" | custom-call | flops 462422016 | bytes 688128 | tf_op jit(solution)/shard_map/pallas_call | solution.py:166
  49.1 0.0 collective-permute-done.5.refs_1_
  49.1 0.6 shard_map.70
  49.8 0.0 collective-permute-done.8.refs_1_
  49.8 1.9 %collective-permute-start.9 = (f32[2,136,256]{2,1,0:T(8,128)S(1)}, f32[2,136,256]{2,1,0:T(8,128)S(1)}, u32[]{:S(2)}, u32[]{:S(2)}) collective-permute-start(f32[2,136,256]{2,1,0:T(8,128)S(1)} %get-tuple-element.42), channel_id=1, source_target_pairs={{0,8},{8,0},{1,9},{9,1},{2,10},{10,2},{3,11},{11,3},{4,12},{12,4},... | collective-permute-start | bytes 835592 | tf_op jit(solution)/shard_map/ppermute | solution.py:24
  51.8 2.9 %collective-permute-start.10 = (f32[2,136,256]{2,1,0:T(8,128)S(1)}, f32[2,136,256]{2,1,0:T(8,128)S(1)}, u32[]{:S(2)}, u32[]{:S(2)}) collective-permute-start(f32[2,136,256]{2,1,0:T(8,128)S(1)} %get-tuple-element.41), channel_id=1, source_target_pairs={{8,16},{16,8},{9,17},{17,9},{10,18},{18,10},{11,19},{19,11},{12,20... | collective-permute-start | bytes 835592 | tf_op jit(solution)/shard_map/ppermute | solution.py:291
  54.7 5.9 %collective-permute-start.12 = (bf16[8,32,384]{2,1,0:T(8,128)(2,1)S(1)}, bf16[8,32,384]{2,1,0:T(8,128)(2,1)S(1)}, u32[]{:S(2)}, u32[]{:S(2)}) collective-permute-start(bf16[8,32,384]{2,1,0:T(8,128)(2,1)S(1)} %shard_map.74.refs_0_), channel_id=1, source_target_pairs={{0,128},{128,0},{256,384},{384,256},{1,129},{129,1},{257,385},{385... | collective-permute-start | bytes 589832 | tf_op jit(solution)/shard_map/ppermute | solution.py:24
  60.6 0.6 shard_map.71.own_ref
  61.2 0.0 collective-permute-done.9.core_ref
  61.2 0.0 collective-permute-done.10.face_ref
  61.2 0.7 shard_map.72
  61.9 5.7 %collective-permute-start.11 = (bf16[224,256]{1,0:T(8,128)(2,1)S(1)}, bf16[224,256]{1,0:T(8,128)(2,1)S(1)}, u32[]{:S(2)}, u32[]{:S(2)}) collective-permute-start(bf16[224,256]{1,0:T(8,128)(2,1)S(1)} %shard_map.72), channel_id=1, source_target_pairs={{0,1},{1,0},{2,3},{3,2},{4,5},{5,4},{6,7},{7,6},{8,9},{9,8},{10,11... | collective-permute-start | bytes 344072 | tf_op jit(solution)/shard_map/ppermute | solution.py:24
  67.6 0.0 collective-permute-done.12.refs_1_
  67.7 1.9 %collective-permute-start.13 = (bf16[16,32,384]{2,1,0:T(8,128)(2,1)S(1)}, bf16[16,32,384]{2,1,0:T(8,128)(2,1)S(1)}, u32[]{:S(2)}, u32[]{:S(2)}) collective-permute-start(bf16[16,32,384]{2,1,0:T(8,128)(2,1)S(1)} %shard_map.75.refs_0_), channel_id=1, source_target_pairs={{0,16},{16,0},{1,17},{17,1},{2,18},{18,2},{3,19},{19,3},{4,20},{20... | collective-permute-start | bytes 1179656 | tf_op jit(solution)/shard_map/ppermute | solution.py:24
  69.6 3.0 %collective-permute-done.11 = bf16[224,256]{1,0:T(8,128)(2,1)S(1)} collective-permute-done((bf16[224,256]{1,0:T(8,128)(2,1)S(1)}, bf16[224,256]{1,0:T(8,128)(2,1)S(1)}, u32[]{:S(2)}, u32[]{:S(2)}) %collective-permute-start.11) | collective-permute-done | bytes 114720 | tf_op jit(solution)/shard_map/ppermute | solution.py:24
  72.7 0.0 copy-start.4
  72.7 12.7 %all-gather = bf16[8,224,256]{2,1,0:T(8,128)(2,1)S(1)} all-gather(bf16[2,224,256]{2,1,0:T(8,128)(2,1)S(1)} %shard_map.73), channel_id=2, replica_groups=mesh['t'=4,'u'=4,'w'=2,'c'=2,'x'=4,'h'=2] {'x'}, dimensions={0}, use_global_device_ids=true | all-gather | bytes 1146880 | tf_op jit(solution)/shard_map/all_gather | solution.py:300
  85.4 0.0 collective-permute-done.13.refs_1_
  85.4 0.1 shard_map.76.mine_ref
  85.5 3.5 %collective-permute-start.14 = (bf16[32,32,384]{2,1,0:T(8,128)(2,1)S(1)}, bf16[32,32,384]{2,1,0:T(8,128)(2,1)S(1)}, u32[]{:S(2)}, u32[]{:S(2)}) collective-permute-start(bf16[32,32,384]{2,1,0:T(8,128)(2,1)S(1)} %shard_map.76.mine_ref), channel_id=1, source_target_pairs={{0,8},{8,0},{1,9},{9,1},{2,10},{10,2},{3,11},{11,3},{4,12},{12,4},... | collective-permute-start | bytes 2359304 | tf_op jit(solution)/shard_map/ppermute | solution.py:24
  89.0 0.0 copy-done.4
  89.1 1.9 %collective-permute-done.14.other_ref = bf16[32,32,384]{2,1,0:T(8,128)(2,1)S(1)} collective-permute-done((bf16[32,32,384]{2,1,0:T(8,128)(2,1)S(1)}, bf16[32,32,384]{2,1,0:T(8,128)(2,1)S(1)}, u32[]{:S(2)}, u32[]{:S(2)}) %collective-permute-start.14) | collective-permute-done | bytes 786464 | tf_op jit(solution)/shard_map/ppermute | solution.py:24
  90.9 1.1 %shard_map.77.weight_ref = bf16[2048,384]{1,0:T(8,128)(2,1)S(1)} custom-call(s32[5]{0:T(128)S(1)} %stack.23.pos_ref, bf16[32,32,384]{2,1,0:T(8,128)(2,1)S(1)} %shard_map.76.mine_ref, bf16[32,32,384]{2,1,0:T(8,128)(2,1)S(1)} %collective-permute-done.14.other_ref), custom_call_target="tpu_custom_call" | custom-call | tf_op jit(solution)/shard_map/pallas_call | solution.py:224
  92.0 1.9 %shard_map.78 = bf16[224,384]{1,0:T(8,128)(2,1)} custom-call(s32[5]{0:T(128)S(1)} %stack.23.pos_ref, bf16[4,2,224,256]{3,2,1,0:T(8,128)(2,1)S(1)} %bitcast.9, bf16[2048,384]{1,0:T(8,128)(2,1)S(1)} %shard_map.77.weight_ref, f32[1,384]{1,0:T(1,128)S(1)} %broadcast_in_dim.15.gate_ref), custom_call_target="tpu_custom_call" | custom-call | tf_op jit(solution)/shard_map/pallas_call | solution.py:248
  (8 shorter events, 0.2 us)
Async XLA Ops:
  0.0 34.9 %copy-start.3 = (bf16[224,256]{1,0:T(8,128)(2,1)S(1)}, bf16[224,256]{1,0:T(8,128)(2,1)}, u32[]{:S(2)}) copy-start(bf16[224,256]{1,0:T(8,128)(2,1)} %refs_0_) | copy-start | bytes 344068
  0.0 34.9 %copy-start.2 = (s32[2,3]{1,0:T(2,128)S(1)}, s32[2,3]{1,0:T(2,128)}, u32[]{:S(2)}) copy-start(s32[2,3]{1,0:T(2,128)} %ext_ref.7) | copy-start | bytes 76
  1.7 26.3 %collective-permute-start = (bf16[224,512]{1,0:T(8,128)(2,1)}, bf16[224,512]{1,0:T(8,128)(2,1)S(1)}, u32[]{:S(2)}, u32[]{:S(2)}) collective-permute-start(bf16[224,512]{1,0:T(8,128)(2,1)} %shard_map.64.refs_0_), channel_id=1, source_target_pairs={{32,64},{64,32},{33,65},{65,33},{34,66},{66,34},{35,67},{67,35},{3... | collective-permute-start | bytes 688136 | tf_op jit(solution)/shard_map/ppermute | solution.py:28
  2.4 25.6 %collective-permute-start.4 = (bf16[224,512]{1,0:T(8,128)(2,1)}, bf16[224,512]{1,0:T(8,128)(2,1)S(1)}, u32[]{:S(2)}, u32[]{:S(2)}) collective-permute-start(bf16[224,512]{1,0:T(8,128)(2,1)} %shard_map.64.refs_0_), channel_id=1, source_target_pairs={{0,32},{32,0},{64,96},{96,64},{1,33},{33,1},{65,97},{97,65},{2,34}... | collective-permute-start | bytes 688136 | tf_op jit(solution)/shard_map/ppermute | solution.py:24
  15.4 12.6 %collective-permute-start.1 = (bf16[224,256]{1,0:T(8,128)(2,1)}, bf16[224,256]{1,0:T(8,128)(2,1)S(1)}, u32[]{:S(2)}, u32[]{:S(2)}) collective-permute-start(bf16[224,256]{1,0:T(8,128)(2,1)} %refs_0_), channel_id=1, source_target_pairs={{0,8},{8,0},{1,9},{9,1},{2,10},{10,2},{3,11},{11,3},{4,12},{12,4},... | collective-permute-start | bytes 344072 | tf_op jit(solution)/shard_map/ppermute | solution.py:24
  18.5 9.4 %collective-permute-start.2 = (bf16[224,256]{1,0:T(8,128)(2,1)}, bf16[224,256]{1,0:T(8,128)(2,1)S(1)}, u32[]{:S(2)}, u32[]{:S(2)}) collective-permute-start(bf16[224,256]{1,0:T(8,128)(2,1)} %refs_0_), channel_id=1, source_target_pairs={{8,16},{16,8},{9,17},{17,9},{10,18},{18,10},{11,19},{19,11},{12,20... | collective-permute-start | bytes 344072 | tf_op jit(solution)/shard_map/ppermute | solution.py:271
  21.5 5.7 %collective-permute-start.3 = (bf16[1,32,384]{2,1,0:T(8,128)(2,1)}, bf16[1,32,384]{2,1,0:T(8,128)(2,1)S(1)}, u32[]{:S(2)}, u32[]{:S(2)}) collective-permute-start(bf16[1,32,384]{2,1,0:T(8,128)(2,1)} %bitcast.12), channel_id=1, source_target_pairs={{0,256},{128,384},{256,0},{384,128},{1,257},{129,385},{257,1},{385... | collective-permute-start | bytes 73736 | tf_op jit(solution)/shard_map/ppermute | solution.py:24
  27.2 0.7 copy-start.1
  28.0 0.9 %copy-start = (bf16[224,512]{1,0:T(8,128)(2,1)S(1)}, bf16[224,512]{1,0:T(8,128)(2,1)}, u32[]{:S(2)}) copy-start(bf16[224,512]{1,0:T(8,128)(2,1)} %shard_map.64.refs_0_) | copy-start | bytes 688132
  29.0 18.6 %collective-permute-start.6 = (bf16[672,512]{1,0:T(8,128)(2,1)S(1)}, bf16[672,512]{1,0:T(8,128)(2,1)S(1)}, u32[]{:S(2)}, u32[]{:S(2)}) collective-permute-start(bf16[672,512]{1,0:T(8,128)(2,1)S(1)} %shard_map.66.refs_3_), channel_id=1, source_target_pairs={{0,128},{128,0},{256,384},{384,256},{1,129},{129,1},{257,385},{385... | collective-permute-start | bytes 2064392 | tf_op jit(solution)/shard_map/ppermute | solution.py:24
  32.2 16.9 %collective-permute-start.5 = (bf16[672,512]{1,0:T(8,128)(2,1)S(1)}, bf16[672,512]{1,0:T(8,128)(2,1)S(1)}, u32[]{:S(2)}, u32[]{:S(2)}) collective-permute-start(bf16[672,512]{1,0:T(8,128)(2,1)S(1)} %shard_map.66.refs_3_), channel_id=1, source_target_pairs={{128,256},{256,128},{129,257},{257,129},{130,258},{258,130},{131,2... | collective-permute-start | bytes 2064392 | tf_op jit(solution)/shard_map/ppermute | solution.py:28
  32.9 6.5 %collective-permute-start.7 = (bf16[2,32,384]{2,1,0:T(8,128)(2,1)S(1)}, bf16[2,32,384]{2,1,0:T(8,128)(2,1)S(1)}, u32[]{:S(2)}, u32[]{:S(2)}) collective-permute-start(bf16[2,32,384]{2,1,0:T(8,128)(2,1)S(1)} %shard_map.65.refs_0_), channel_id=1, source_target_pairs={{0,32},{32,0},{64,96},{96,64},{1,33},{33,1},{65,97},{97,65},{2,34}... | collective-permute-start | bytes 147464 | tf_op jit(solution)/shard_map/ppermute | solution.py:24
  39.4 10.4 %collective-permute-start.8 = (bf16[4,32,384]{2,1,0:T(8,128)(2,1)S(1)}, bf16[4,32,384]{2,1,0:T(8,128)(2,1)S(1)}, u32[]{:S(2)}, u32[]{:S(2)}) collective-permute-start(bf16[4,32,384]{2,1,0:T(8,128)(2,1)S(1)} %shard_map.68.refs_0_), channel_id=1, source_target_pairs={{0,96},{32,64},{64,32},{96,0},{1,97},{33,65},{65,33},{97,1},{2,98}... | collective-permute-start | bytes 294920 | tf_op jit(solution)/shard_map/ppermute | solution.py:24
  49.8 11.3 %collective-permute-start.9 = (f32[2,136,256]{2,1,0:T(8,128)S(1)}, f32[2,136,256]{2,1,0:T(8,128)S(1)}, u32[]{:S(2)}, u32[]{:S(2)}) collective-permute-start(f32[2,136,256]{2,1,0:T(8,128)S(1)} %get-tuple-element.42), channel_id=1, source_target_pairs={{0,8},{8,0},{1,9},{9,1},{2,10},{10,2},{3,11},{11,3},{4,12},{12,4},... | collective-permute-start | bytes 835592 | tf_op jit(solution)/shard_map/ppermute | solution.py:24
  51.8 9.4 %collective-permute-start.10 = (f32[2,136,256]{2,1,0:T(8,128)S(1)}, f32[2,136,256]{2,1,0:T(8,128)S(1)}, u32[]{:S(2)}, u32[]{:S(2)}) collective-permute-start(f32[2,136,256]{2,1,0:T(8,128)S(1)} %get-tuple-element.41), channel_id=1, source_target_pairs={{8,16},{16,8},{9,17},{17,9},{10,18},{18,10},{11,19},{19,11},{12,20... | collective-permute-start | bytes 835592 | tf_op jit(solution)/shard_map/ppermute | solution.py:291
  54.7 13.0 %collective-permute-start.12 = (bf16[8,32,384]{2,1,0:T(8,128)(2,1)S(1)}, bf16[8,32,384]{2,1,0:T(8,128)(2,1)S(1)}, u32[]{:S(2)}, u32[]{:S(2)}) collective-permute-start(bf16[8,32,384]{2,1,0:T(8,128)(2,1)S(1)} %shard_map.74.refs_0_), channel_id=1, source_target_pairs={{0,128},{128,0},{256,384},{384,256},{1,129},{129,1},{257,385},{385... | collective-permute-start | bytes 589832 | tf_op jit(solution)/shard_map/ppermute | solution.py:24
  61.9 10.8 %collective-permute-start.11 = (bf16[224,256]{1,0:T(8,128)(2,1)S(1)}, bf16[224,256]{1,0:T(8,128)(2,1)S(1)}, u32[]{:S(2)}, u32[]{:S(2)}) collective-permute-start(bf16[224,256]{1,0:T(8,128)(2,1)S(1)} %shard_map.72), channel_id=1, source_target_pairs={{0,1},{1,0},{2,3},{3,2},{4,5},{5,4},{6,7},{7,6},{8,9},{9,8},{10,11... | collective-permute-start | bytes 344072 | tf_op jit(solution)/shard_map/ppermute | solution.py:24
  67.7 17.7 %collective-permute-start.13 = (bf16[16,32,384]{2,1,0:T(8,128)(2,1)S(1)}, bf16[16,32,384]{2,1,0:T(8,128)(2,1)S(1)}, u32[]{:S(2)}, u32[]{:S(2)}) collective-permute-start(bf16[16,32,384]{2,1,0:T(8,128)(2,1)S(1)} %shard_map.75.refs_0_), channel_id=1, source_target_pairs={{0,16},{16,0},{1,17},{17,1},{2,18},{18,2},{3,19},{19,3},{4,20},{20... | collective-permute-start | bytes 1179656 | tf_op jit(solution)/shard_map/ppermute | solution.py:24
  72.7 16.4 %copy-start.4 = (f32[384]{0:T(512)S(1)}, f32[384]{0:T(512)}, u32[]{:S(2)}) copy-start(f32[384]{0:T(512)} %param.11) | copy-start | bytes 4612
  85.5 5.4 %collective-permute-start.14 = (bf16[32,32,384]{2,1,0:T(8,128)(2,1)S(1)}, bf16[32,32,384]{2,1,0:T(8,128)(2,1)S(1)}, u32[]{:S(2)}, u32[]{:S(2)}) collective-permute-start(bf16[32,32,384]{2,1,0:T(8,128)(2,1)S(1)} %shard_map.76.mine_ref), channel_id=1, source_target_pairs={{0,8},{8,0},{1,9},{9,1},{2,10},{10,2},{3,11},{11,3},{4,12},{12,4},... | collective-permute-start | bytes 2359304 | tf_op jit(solution)/shard_map/ppermute | solution.py:24

commit v4 on v3

--- a/solution.py
+++ b/solution.py
@@ -48,11 +48,16 @@
     )(*parts)
 
 
-def beside_kernel(left_ref, right_ref, out_ref, sems):
-    width = left_ref.shape[1]
+def staged_kernel(key_ref, value_ref, q_ref, weight_ref, kv_out, q_out, weight_out, sems):
+    width = key_ref.shape[1]
+    pairs = [
+        (key_ref, kv_out.at[:, pl.ds(0, width)]),
+        (value_ref, kv_out.at[:, pl.ds(width, width)]),
+        (weight_ref, weight_out.at[0]),
+        (q_ref, q_out),
+    ]
     copies = [
-        pltpu.make_async_copy(ref, out_ref.at[:, pl.ds(at * width, width)], sems.at[at])
-        for at, ref in enumerate((left_ref, right_ref))
+        pltpu.make_async_copy(src, dst, sems.at[at]) for at, (src, dst) in enumerate(pairs)
     ]
     for copy in copies:
         copy.start()
@@ -60,14 +65,20 @@
         copy.wait()
 
 
-def beside(left, right):
-    return pl.pallas_call(
-        beside_kernel,
-        out_shape=jax.ShapeDtypeStruct((left.shape[0], 2 * left.shape[1]), left.dtype),
-        in_specs=[pl.BlockSpec(memory_space=pl.ANY)] * 2,
-        out_specs=pl.BlockSpec(memory_space=pltpu.VMEM),
-        scratch_shapes=[pltpu.SemaphoreType.DMA((2,))],
-    )(left, right)
+def staged(keys, values, queries, weight):
+    vmem = pl.BlockSpec(memory_space=pltpu.VMEM)
+    rows, width = keys.shape
+    return pl.pallas_call(
+        staged_kernel,
+        out_shape=(
+            jax.ShapeDtypeStruct((rows, 2 * width), keys.dtype),
+            jax.ShapeDtypeStruct(queries.shape, queries.dtype),
+            jax.ShapeDtypeStruct((1, *weight.shape), weight.dtype),
+        ),
+        in_specs=[pl.BlockSpec(memory_space=pl.ANY)] * 4,
+        out_specs=(vmem, vmem, vmem),
+        scratch_shapes=[pltpu.SemaphoreType.DMA((4,))],
+    )(keys, values, queries, weight)
 
 
 def online_update(state_ref, head, lanes, queries, keys, values, first, last_ok):
@@ -261,7 +272,7 @@
 def local(queries, key_rows, value_rows, extents, out_weight, gate_scale):
     pos = jnp.stack([lax.axis_index(a) for a in ("t", "u", "w", "c", "h")])
 
-    own_kv = beside(key_rows, value_rows)
+    own_kv, queries, weight = staged(key_rows, value_rows, queries, out_weight)
     up = swapped(own_kv, "u", 1)
     down = middle_swapped(own_kv, "u")
     facing = [(1, 2), (2, 1)]
@@ -270,7 +281,6 @@
         swapped(queries, "c", 1),
         lax.ppermute(queries, ("w", "c"), facing),
     ]
-    weight = out_weight[None]
     weight = joined(weight, swapped(weight, "t", 2))
 
     down, tiles_q, weight = lax.optimization_barrier((down, tiles_q, weight))

time: 95.5 us -> 94.9 us (level)
    ppermute x11, starting transfers between devices: 46.4 us -> 45.1 us  [swapped(): return lax.ppermute(value, axis, [(i, i ^ flip) for i in range(count)])]
  transfers between devices with their start and end apart: 15 -> 15, of which waited for: 5 -> 5; matrix products, arithmetic and copies ran while one was open for 0% -> 0% of each run, Pallas kernels for 5% -> 4%
where the time goes in v4:
time: 94.9 us; the launch traced here: 93.7 us
  starting transfers between devices  53.2 us (56%)
  waiting for transfers between devices  14.8 us (16%)
  blocking collectives  13.6 us (14%)
  Pallas kernels  9.07 us (10%)
  local copies, waits for them, and re-layouts  2.7 us (3%)
    ppermute x11, starting transfers between devices, swapped(): return lax.ppermute(value, axis, [(i, i ^ flip) for i in range(count)])  45.1 us
    ppermute x11, waiting for transfers between devices, swapped(): return lax.ppermute(value, axis, [(i, i ^ flip) for i in range(count)])  14.8 us
    all_gather x1, blocking collectives, local(): lax.all_gather(joined(attended[None], across[None]), 'x', axis=0, tiled=F...  13.6 us
    ppermute x1, starting transfers between devices, local(): from_face = lax.ppermute(given[:, :, LANES:], ('w', 'c'), facing)  3.69 us
    pallas_call x4, Pallas kernels, attend(): pl.pallas_call(functools.partial(attend_kernel, low, high, stage), out_sh...  3.42 us
    ppermute x1, starting transfers between devices, local(): lax.ppermute(queries, ('w', 'c'), facing)  3 us
    unnamed x10, local copies, waits for them, and re-layouts  2.58 us
  transfers between devices with their start and end apart: 15, of which 5 were waited for; matrix products, arithmetic and copies ran while one was open for 0% of the time, Pallas kernels for 4%

profile of v4, /device:TPU:1, one launch (start us, length us, event | category | flops | bytes accessed | tf_op | source)
XLA Modules:
  0.0 93.7 jit_solution(15647334466832014737)
XLA Ops:
  0.0 0.0 copy-start.2
  0.0 1.8 %shard_map.64 = (bf16[224,512]{1,0:T(8,128)(2,1)}, bf16[224,256]{1,0:T(8,128)(2,1)}, bf16[1,32,384]{2,1,0:T(8,128)(2,1)}) custom-call(bf16[224,256]{1,0:T(8,128)(2,1)} %key_ref.1, bf16[224,256]{1,0:T(8,128)(2,1)} %value_ref.1, bf16[224,256]{1,0:T(8,128)(2,1)} %q_ref.1, bf16[32,384]{1,0:T(8,128)(2,1)} %weight_ref.1), custom_call_target="tpu_custom_call" | custom-call | tf_op jit(solution)/shard_map/pallas_call | solution.py:71
  1.8 0.7 collective-permute-start
  2.5 13.0 %collective-permute-start.4 = (bf16[224,512]{1,0:T(8,128)(2,1)}, bf16[224,512]{1,0:T(8,128)(2,1)S(1)}, u32[]{:S(2)}, u32[]{:S(2)}) collective-permute-start(bf16[224,512]{1,0:T(8,128)(2,1)} %get-tuple-element.26.refs_0_), channel_id=1, source_target_pairs={{0,32},{32,0},{64,96},{96,64},{1,33},{33,1},{65,97},{97,65},{2,34}... | collective-permute-start | bytes 688136 | tf_op jit(solution)/shard_map/ppermute | solution.py:24
  15.5 3.1 %collective-permute-start.1 = (bf16[224,256]{1,0:T(8,128)(2,1)}, bf16[224,256]{1,0:T(8,128)(2,1)S(1)}, u32[]{:S(2)}, u32[]{:S(2)}) collective-permute-start(bf16[224,256]{1,0:T(8,128)(2,1)} %get-tuple-element.29.refs_0_), channel_id=1, source_target_pairs={{0,8},{8,0},{1,9},{9,1},{2,10},{10,2},{3,11},{11,3},{4,12},{12,4},... | collective-permute-start | bytes 344072 | tf_op jit(solution)/shard_map/ppermute | solution.py:24
  18.6 3.0 %collective-permute-start.2 = (bf16[224,256]{1,0:T(8,128)(2,1)}, bf16[224,256]{1,0:T(8,128)(2,1)S(1)}, u32[]{:S(2)}, u32[]{:S(2)}) collective-permute-start(bf16[224,256]{1,0:T(8,128)(2,1)} %get-tuple-element.29.refs_0_), channel_id=1, source_target_pairs={{8,16},{16,8},{9,17},{17,9},{10,18},{18,10},{11,19},{19,11},{12,20... | collective-permute-start | bytes 344072 | tf_op jit(solution)/shard_map/ppermute | solution.py:282
  21.6 4.2 %collective-permute-start.3 = (bf16[1,32,384]{2,1,0:T(8,128)(2,1)}, bf16[1,32,384]{2,1,0:T(8,128)(2,1)S(1)}, u32[]{:S(2)}, u32[]{:S(2)}) collective-permute-start(bf16[1,32,384]{2,1,0:T(8,128)(2,1)} %get-tuple-element.28.refs_0_), channel_id=1, source_target_pairs={{0,256},{128,384},{256,0},{384,128},{1,257},{129,385},{257,1},{385... | collective-permute-start | bytes 73736 | tf_op jit(solution)/shard_map/ppermute | solution.py:24
  25.9 1.5 %collective-permute-done.3.refs_1_ = bf16[1,32,384]{2,1,0:T(8,128)(2,1)S(1)} collective-permute-done((bf16[1,32,384]{2,1,0:T(8,128)(2,1)}, bf16[1,32,384]{2,1,0:T(8,128)(2,1)S(1)}, u32[]{:S(2)}, u32[]{:S(2)}) %collective-permute-start.3) | collective-permute-done | bytes 24608 | tf_op jit(solution)/shard_map/ppermute | solution.py:24
  27.3 0.0 copy-start.1
  27.3 0.7 copy-done.1
  28.1 0.0 collective-permute-done.1.refs_1_
  28.1 0.0 collective-permute-done.2.refs_2_
  28.1 0.0 collective-permute-done.refs_2_
  28.1 0.0 collective-permute-done.4.refs_1_
  28.1 0.0 copy-start
  28.1 0.9 copy-done
  29.1 3.2 %collective-permute-start.6 = (bf16[672,512]{1,0:T(8,128)(2,1)S(1)}, bf16[672,512]{1,0:T(8,128)(2,1)S(1)}, u32[]{:S(2)}, u32[]{:S(2)}) collective-permute-start(bf16[672,512]{1,0:T(8,128)(2,1)S(1)} %shard_map.66.refs_3_), channel_id=1, source_target_pairs={{0,128},{128,0},{256,384},{384,256},{1,129},{129,1},{257,385},{385... | collective-permute-start | bytes 2064392 | tf_op jit(solution)/shard_map/ppermute | solution.py:24
  32.3 0.7 collective-permute-start.5
  33.0 1.9 %collective-permute-start.7 = (bf16[2,32,384]{2,1,0:T(8,128)(2,1)S(1)}, bf16[2,32,384]{2,1,0:T(8,128)(2,1)S(1)}, u32[]{:S(2)}, u32[]{:S(2)}) collective-permute-start(bf16[2,32,384]{2,1,0:T(8,128)(2,1)S(1)} %shard_map.65.refs_0_), channel_id=1, source_target_pairs={{0,32},{32,0},{64,96},{96,64},{1,33},{33,1},{65,97},{97,65},{2,34}... | collective-permute-start | bytes 147464 | tf_op jit(solution)/shard_map/ppermute | solution.py:24
  35.0 0.1 stack.23.pos_ref
  35.0 0.0 copy-done.2
  35.0 0.0 copy-start.3
  35.0 0.9 copy-done.3
  35.9 1.5 %shard_map.67 = (f32[2,136,768]{2,1,0:T(8,128)S(1)}, bf16[768,256]{1,0:T(8,128)(2,1)S(1)}) custom-call(s32[5]{0:T(128)S(1)} %stack.23.pos_ref, s32[2,3]{1,0:T(2,128)S(1)} %copy-done.2, bf16[224,256]{1,0:T(8,128)(2,1)S(1)} %copy-done.3, bf16[224,256]{1,0:T(8,128)(2,1)S(1)} %collective-permute-done.1.refs_1_, ...), custom_call_target="tpu_custom_call" | custom-call | flops 462422016 | bytes 688128 | tf_op jit(solution)/shard_map/pallas_call | solution.py:177
  37.5 2.1 %collective-permute-done.7.refs_1_ = bf16[2,32,384]{2,1,0:T(8,128)(2,1)S(1)} collective-permute-done((bf16[2,32,384]{2,1,0:T(8,128)(2,1)S(1)}, bf16[2,32,384]{2,1,0:T(8,128)(2,1)S(1)}, u32[]{:S(2)}, u32[]{:S(2)}) %collective-permute-start.7) | collective-permute-done | bytes 49184 | tf_op jit(solution)/shard_map/ppermute | solution.py:24
  39.5 1.9 %collective-permute-start.8 = (bf16[4,32,384]{2,1,0:T(8,128)(2,1)S(1)}, bf16[4,32,384]{2,1,0:T(8,128)(2,1)S(1)}, u32[]{:S(2)}, u32[]{:S(2)}) collective-permute-start(bf16[4,32,384]{2,1,0:T(8,128)(2,1)S(1)} %shard_map.68.refs_0_), channel_id=1, source_target_pairs={{0,96},{32,64},{64,32},{96,0},{1,97},{33,65},{65,33},{97,1},{2,98}... | collective-permute-start | bytes 294920 | tf_op jit(solution)/shard_map/ppermute | solution.py:24
  41.5 6.3 %collective-permute-done.6.refs_1_ = bf16[672,512]{1,0:T(8,128)(2,1)S(1)} collective-permute-done((bf16[672,512]{1,0:T(8,128)(2,1)S(1)}, bf16[672,512]{1,0:T(8,128)(2,1)S(1)}, u32[]{:S(2)}, u32[]{:S(2)}) %collective-permute-start.6) | collective-permute-done | bytes 688160 | tf_op jit(solution)/shard_map/ppermute | solution.py:24
  47.7 0.7 shard_map.69.refs_2_
  48.4 0.0 collective-permute-done.5.refs_1_
  48.4 0.6 shard_map.70
  49.1 0.0 collective-permute-done.8.refs_1_
  49.1 1.9 %collective-permute-start.9 = (f32[2,136,256]{2,1,0:T(8,128)S(1)}, f32[2,136,256]{2,1,0:T(8,128)S(1)}, u32[]{:S(2)}, u32[]{:S(2)}) collective-permute-start(f32[2,136,256]{2,1,0:T(8,128)S(1)} %get-tuple-element.48), channel_id=1, source_target_pairs={{0,8},{8,0},{1,9},{9,1},{2,10},{10,2},{3,11},{11,3},{4,12},{12,4},... | collective-permute-start | bytes 835592 | tf_op jit(solution)/shard_map/ppermute | solution.py:24
  51.0 3.7 %collective-permute-start.10 = (f32[2,136,256]{2,1,0:T(8,128)S(1)}, f32[2,136,256]{2,1,0:T(8,128)S(1)}, u32[]{:S(2)}, u32[]{:S(2)}) collective-permute-start(f32[2,136,256]{2,1,0:T(8,128)S(1)} %get-tuple-element.47), channel_id=1, source_target_pairs={{8,16},{16,8},{9,17},{17,9},{10,18},{18,10},{11,19},{19,11},{12,20... | collective-permute-start | bytes 835592 | tf_op jit(solution)/shard_map/ppermute | solution.py:301
  54.8 5.9 %collective-permute-start.12 = (bf16[8,32,384]{2,1,0:T(8,128)(2,1)S(1)}, bf16[8,32,384]{2,1,0:T(8,128)(2,1)S(1)}, u32[]{:S(2)}, u32[]{:S(2)}) collective-permute-start(bf16[8,32,384]{2,1,0:T(8,128)(2,1)S(1)} %shard_map.74.refs_0_), channel_id=1, source_target_pairs={{0,128},{128,0},{256,384},{384,256},{1,129},{129,1},{257,385},{385... | collective-permute-start | bytes 589832 | tf_op jit(solution)/shard_map/ppermute | solution.py:24
  60.7 0.6 shard_map.71.own_ref
  61.3 0.0 collective-permute-done.9.core_ref
  61.3 0.0 collective-permute-done.10.face_ref
  61.3 0.7 shard_map.72
  62.0 5.3 %collective-permute-start.11 = (bf16[224,256]{1,0:T(8,128)(2,1)S(1)}, bf16[224,256]{1,0:T(8,128)(2,1)S(1)}, u32[]{:S(2)}, u32[]{:S(2)}) collective-permute-start(bf16[224,256]{1,0:T(8,128)(2,1)S(1)} %shard_map.72), channel_id=1, source_target_pairs={{0,1},{1,0},{2,3},{3,2},{4,5},{5,4},{6,7},{7,6},{8,9},{9,8},{10,11... | collective-permute-start | bytes 344072 | tf_op jit(solution)/shard_map/ppermute | solution.py:24
  67.3 0.0 collective-permute-done.12.refs_1_
  67.4 1.9 %collective-permute-start.13 = (bf16[16,32,384]{2,1,0:T(8,128)(2,1)S(1)}, bf16[16,32,384]{2,1,0:T(8,128)(2,1)S(1)}, u32[]{:S(2)}, u32[]{:S(2)}) collective-permute-start(bf16[16,32,384]{2,1,0:T(8,128)(2,1)S(1)} %shard_map.75.refs_0_), channel_id=1, source_target_pairs={{0,16},{16,0},{1,17},{17,1},{2,18},{18,2},{3,19},{19,3},{4,20},{20... | collective-permute-start | bytes 1179656 | tf_op jit(solution)/shard_map/ppermute | solution.py:24
  69.3 3.1 %collective-permute-done.11 = bf16[224,256]{1,0:T(8,128)(2,1)S(1)} collective-permute-done((bf16[224,256]{1,0:T(8,128)(2,1)S(1)}, bf16[224,256]{1,0:T(8,128)(2,1)S(1)}, u32[]{:S(2)}, u32[]{:S(2)}) %collective-permute-start.11) | collective-permute-done | bytes 114720 | tf_op jit(solution)/shard_map/ppermute | solution.py:24
  72.5 0.0 copy-start.4
  72.5 13.6 %all-gather = bf16[8,224,256]{2,1,0:T(8,128)(2,1)S(1)} all-gather(bf16[2,224,256]{2,1,0:T(8,128)(2,1)S(1)} %shard_map.73), channel_id=2, replica_groups=mesh['t'=4,'u'=4,'w'=2,'c'=2,'x'=4,'h'=2] {'x'}, dimensions={0}, use_global_device_ids=true | all-gather | bytes 1146880 | tf_op jit(solution)/shard_map/all_gather | solution.py:310
  86.1 0.0 collective-permute-done.13.refs_1_
  86.1 0.1 shard_map.76.mine_ref
  86.2 2.7 %collective-permute-start.14 = (bf16[32,32,384]{2,1,0:T(8,128)(2,1)S(1)}, bf16[32,32,384]{2,1,0:T(8,128)(2,1)S(1)}, u32[]{:S(2)}, u32[]{:S(2)}) collective-permute-start(bf16[32,32,384]{2,1,0:T(8,128)(2,1)S(1)} %shard_map.76.mine_ref), channel_id=1, source_target_pairs={{0,8},{8,0},{1,9},{9,1},{2,10},{10,2},{3,11},{11,3},{4,12},{12,4},... | collective-permute-start | bytes 2359304 | tf_op jit(solution)/shard_map/ppermute | solution.py:24
  88.8 0.0 copy-done.4
  88.8 1.9 %collective-permute-done.14.other_ref = bf16[32,32,384]{2,1,0:T(8,128)(2,1)S(1)} collective-permute-done((bf16[32,32,384]{2,1,0:T(8,128)(2,1)S(1)}, bf16[32,32,384]{2,1,0:T(8,128)(2,1)S(1)}, u32[]{:S(2)}, u32[]{:S(2)}) %collective-permute-start.14) | collective-permute-done | bytes 786464 | tf_op jit(solution)/shard_map/ppermute | solution.py:24
  90.7 1.1 %shard_map.77.weight_ref = bf16[2048,384]{1,0:T(8,128)(2,1)S(1)} custom-call(s32[5]{0:T(128)S(1)} %stack.23.pos_ref, bf16[32,32,384]{2,1,0:T(8,128)(2,1)S(1)} %shard_map.76.mine_ref, bf16[32,32,384]{2,1,0:T(8,128)(2,1)S(1)} %collective-permute-done.14.other_ref), custom_call_target="tpu_custom_call" | custom-call | tf_op jit(solution)/shard_map/pallas_call | solution.py:235
  91.8 1.9 %shard_map.78 = bf16[224,384]{1,0:T(8,128)(2,1)} custom-call(s32[5]{0:T(128)S(1)} %stack.23.pos_ref, bf16[4,2,224,256]{3,2,1,0:T(8,128)(2,1)S(1)} %bitcast.8, bf16[2048,384]{1,0:T(8,128)(2,1)S(1)} %shard_map.77.weight_ref, f32[1,384]{1,0:T(1,128)S(1)} %broadcast_in_dim.11.gate_ref), custom_call_target="tpu_custom_call" | custom-call | tf_op jit(solution)/shard_map/pallas_call | solution.py:259
  (8 shorter events, 0.2 us)
Async XLA Ops:
  0.0 35.0 %copy-start.2 = (s32[2,3]{1,0:T(2,128)S(1)}, s32[2,3]{1,0:T(2,128)}, u32[]{:S(2)}) copy-start(s32[2,3]{1,0:T(2,128)} %ext_ref.7) | copy-start | bytes 76
  1.8 26.3 %collective-permute-start = (bf16[224,512]{1,0:T(8,128)(2,1)}, bf16[224,512]{1,0:T(8,128)(2,1)S(1)}, u32[]{:S(2)}, u32[]{:S(2)}) collective-permute-start(bf16[224,512]{1,0:T(8,128)(2,1)} %get-tuple-element.26.refs_0_), channel_id=1, source_target_pairs={{32,64},{64,32},{33,65},{65,33},{34,66},{66,34},{35,67},{67,35},{3... | collective-permute-start | bytes 688136 | tf_op jit(solution)/shard_map/ppermute | solution.py:28
  2.5 25.6 %collective-permute-start.4 = (bf16[224,512]{1,0:T(8,128)(2,1)}, bf16[224,512]{1,0:T(8,128)(2,1)S(1)}, u32[]{:S(2)}, u32[]{:S(2)}) collective-permute-start(bf16[224,512]{1,0:T(8,128)(2,1)} %get-tuple-element.26.refs_0_), channel_id=1, source_target_pairs={{0,32},{32,0},{64,96},{96,64},{1,33},{33,1},{65,97},{97,65},{2,34}... | collective-permute-start | bytes 688136 | tf_op jit(solution)/shard_map/ppermute | solution.py:24
  15.5 12.6 %collective-permute-start.1 = (bf16[224,256]{1,0:T(8,128)(2,1)}, bf16[224,256]{1,0:T(8,128)(2,1)S(1)}, u32[]{:S(2)}, u32[]{:S(2)}) collective-permute-start(bf16[224,256]{1,0:T(8,128)(2,1)} %get-tuple-element.29.refs_0_), channel_id=1, source_target_pairs={{0,8},{8,0},{1,9},{9,1},{2,10},{10,2},{3,11},{11,3},{4,12},{12,4},... | collective-permute-start | bytes 344072 | tf_op jit(solution)/shard_map/ppermute | solution.py:24
  18.6 9.4 %collective-permute-start.2 = (bf16[224,256]{1,0:T(8,128)(2,1)}, bf16[224,256]{1,0:T(8,128)(2,1)S(1)}, u32[]{:S(2)}, u32[]{:S(2)}) collective-permute-start(bf16[224,256]{1,0:T(8,128)(2,1)} %get-tuple-element.29.refs_0_), channel_id=1, source_target_pairs={{8,16},{16,8},{9,17},{17,9},{10,18},{18,10},{11,19},{19,11},{12,20... | collective-permute-start | bytes 344072 | tf_op jit(solution)/shard_map/ppermute | solution.py:282
  21.6 5.7 %collective-permute-start.3 = (bf16[1,32,384]{2,1,0:T(8,128)(2,1)}, bf16[1,32,384]{2,1,0:T(8,128)(2,1)S(1)}, u32[]{:S(2)}, u32[]{:S(2)}) collective-permute-start(bf16[1,32,384]{2,1,0:T(8,128)(2,1)} %get-tuple-element.28.refs_0_), channel_id=1, source_target_pairs={{0,256},{128,384},{256,0},{384,128},{1,257},{129,385},{257,1},{385... | collective-permute-start | bytes 73736 | tf_op jit(solution)/shard_map/ppermute | solution.py:24
  27.3 0.7 copy-start.1
  28.1 0.9 %copy-start = (bf16[224,512]{1,0:T(8,128)(2,1)S(1)}, bf16[224,512]{1,0:T(8,128)(2,1)}, u32[]{:S(2)}) copy-start(bf16[224,512]{1,0:T(8,128)(2,1)} %get-tuple-element.26.refs_0_) | copy-start | bytes 688132
  29.1 18.6 %collective-permute-start.6 = (bf16[672,512]{1,0:T(8,128)(2,1)S(1)}, bf16[672,512]{1,0:T(8,128)(2,1)S(1)}, u32[]{:S(2)}, u32[]{:S(2)}) collective-permute-start(bf16[672,512]{1,0:T(8,128)(2,1)S(1)} %shard_map.66.refs_3_), channel_id=1, source_target_pairs={{0,128},{128,0},{256,384},{384,256},{1,129},{129,1},{257,385},{385... | collective-permute-start | bytes 2064392 | tf_op jit(solution)/shard_map/ppermute | solution.py:24
  32.3 16.1 %collective-permute-start.5 = (bf16[672,512]{1,0:T(8,128)(2,1)S(1)}, bf16[672,512]{1,0:T(8,128)(2,1)S(1)}, u32[]{:S(2)}, u32[]{:S(2)}) collective-permute-start(bf16[672,512]{1,0:T(8,128)(2,1)S(1)} %shard_map.66.refs_3_), channel_id=1, source_target_pairs={{128,256},{256,128},{129,257},{257,129},{130,258},{258,130},{131,2... | collective-permute-start | bytes 2064392 | tf_op jit(solution)/shard_map/ppermute | solution.py:28
  33.0 6.5 %collective-permute-start.7 = (bf16[2,32,384]{2,1,0:T(8,128)(2,1)S(1)}, bf16[2,32,384]{2,1,0:T(8,128)(2,1)S(1)}, u32[]{:S(2)}, u32[]{:S(2)}) collective-permute-start(bf16[2,32,384]{2,1,0:T(8,128)(2,1)S(1)} %shard_map.65.refs_0_), channel_id=1, source_target_pairs={{0,32},{32,0},{64,96},{96,64},{1,33},{33,1},{65,97},{97,65},{2,34}... | collective-permute-start | bytes 147464 | tf_op jit(solution)/shard_map/ppermute | solution.py:24
  35.0 0.9 copy-start.3
  39.5 9.5 %collective-permute-start.8 = (bf16[4,32,384]{2,1,0:T(8,128)(2,1)S(1)}, bf16[4,32,384]{2,1,0:T(8,128)(2,1)S(1)}, u32[]{:S(2)}, u32[]{:S(2)}) collective-permute-start(bf16[4,32,384]{2,1,0:T(8,128)(2,1)S(1)} %shard_map.68.refs_0_), channel_id=1, source_target_pairs={{0,96},{32,64},{64,32},{96,0},{1,97},{33,65},{65,33},{97,1},{2,98}... | collective-permute-start | bytes 294920 | tf_op jit(solution)/shard_map/ppermute | solution.py:24
  49.1 12.2 %collective-permute-start.9 = (f32[2,136,256]{2,1,0:T(8,128)S(1)}, f32[2,136,256]{2,1,0:T(8,128)S(1)}, u32[]{:S(2)}, u32[]{:S(2)}) collective-permute-start(f32[2,136,256]{2,1,0:T(8,128)S(1)} %get-tuple-element.48), channel_id=1, source_target_pairs={{0,8},{8,0},{1,9},{9,1},{2,10},{10,2},{3,11},{11,3},{4,12},{12,4},... | collective-permute-start | bytes 835592 | tf_op jit(solution)/shard_map/ppermute | solution.py:24
  51.0 10.3 %collective-permute-start.10 = (f32[2,136,256]{2,1,0:T(8,128)S(1)}, f32[2,136,256]{2,1,0:T(8,128)S(1)}, u32[]{:S(2)}, u32[]{:S(2)}) collective-permute-start(f32[2,136,256]{2,1,0:T(8,128)S(1)} %get-tuple-element.47), channel_id=1, source_target_pairs={{8,16},{16,8},{9,17},{17,9},{10,18},{18,10},{11,19},{19,11},{12,20... | collective-permute-start | bytes 835592 | tf_op jit(solution)/shard_map/ppermute | solution.py:301
  54.8 12.6 %collective-permute-start.12 = (bf16[8,32,384]{2,1,0:T(8,128)(2,1)S(1)}, bf16[8,32,384]{2,1,0:T(8,128)(2,1)S(1)}, u32[]{:S(2)}, u32[]{:S(2)}) collective-permute-start(bf16[8,32,384]{2,1,0:T(8,128)(2,1)S(1)} %shard_map.74.refs_0_), channel_id=1, source_target_pairs={{0,128},{128,0},{256,384},{384,256},{1,129},{129,1},{257,385},{385... | collective-permute-start | bytes 589832 | tf_op jit(solution)/shard_map/ppermute | solution.py:24
  62.0 10.5 %collective-permute-start.11 = (bf16[224,256]{1,0:T(8,128)(2,1)S(1)}, bf16[224,256]{1,0:T(8,128)(2,1)S(1)}, u32[]{:S(2)}, u32[]{:S(2)}) collective-permute-start(bf16[224,256]{1,0:T(8,128)(2,1)S(1)} %shard_map.72), channel_id=1, source_target_pairs={{0,1},{1,0},{2,3},{3,2},{4,5},{5,4},{6,7},{7,6},{8,9},{9,8},{10,11... | collective-permute-start | bytes 344072 | tf_op jit(solution)/shard_map/ppermute | solution.py:24
  67.4 18.7 %collective-permute-start.13 = (bf16[16,32,384]{2,1,0:T(8,128)(2,1)S(1)}, bf16[16,32,384]{2,1,0:T(8,128)(2,1)S(1)}, u32[]{:S(2)}, u32[]{:S(2)}) collective-permute-start(bf16[16,32,384]{2,1,0:T(8,128)(2,1)S(1)} %shard_map.75.refs_0_), channel_id=1, source_target_pairs={{0,16},{16,0},{1,17},{17,1},{2,18},{18,2},{3,19},{19,3},{4,20},{20... | collective-permute-start | bytes 1179656 | tf_op jit(solution)/shard_map/ppermute | solution.py:24
  72.5 16.4 %copy-start.4 = (f32[384]{0:T(512)S(1)}, f32[384]{0:T(512)}, u32[]{:S(2)}) copy-start(f32[384]{0:T(512)} %param.11) | copy-start | bytes 4612
  86.2 4.6 %collective-permute-start.14 = (bf16[32,32,384]{2,1,0:T(8,128)(2,1)S(1)}, bf16[32,32,384]{2,1,0:T(8,128)(2,1)S(1)}, u32[]{:S(2)}, u32[]{:S(2)}) collective-permute-start(bf16[32,32,384]{2,1,0:T(8,128)(2,1)S(1)} %shard_map.76.mine_ref), channel_id=1, source_target_pairs={{0,8},{8,0},{1,9},{9,1},{2,10},{10,2},{3,11},{11,3},{4,12},{12,4},... | collective-permute-start | bytes 2359304 | tf_op jit(solution)/shard_map/ppermute | solution.py:24

commit v5 on v4

--- a/solution.py
+++ b/solution.py
@@ -78,6 +78,7 @@
         in_specs=[pl.BlockSpec(memory_space=pl.ANY)] * 4,
         out_specs=(vmem, vmem, vmem),
         scratch_shapes=[pltpu.SemaphoreType.DMA((4,))],
+        compiler_params=pltpu.CompilerParams(vmem_limit_bytes=VMEM_LIMIT),
     )(keys, values, queries, weight)
 
 

time: 94.9 us -> 96 us (1.012)
  waiting for transfers between devices: 14.8 us -> 13.2 us
  starting transfers between devices: 53.2 us -> 54.7 us
    ppermute x11, starting transfers between devices: 45.1 us -> 47.7 us  [swapped(): return lax.ppermute(value, axis, [(i, i ^ flip) for i in range(count)])]
    pallas_call x4, Pallas kernels: 3.42 us -> 5.67 us  [attend(): pl.pallas_call(functools.partial(attend_kernel, low, high, stage), out_sh...]
    ppermute x11, waiting for transfers between devices: 14.8 us -> 13.2 us  [swapped(): return lax.ppermute(value, axis, [(i, i ^ flip) for i in range(count)])]
    pallas_call x1, Pallas kernels: 1.8 us -> 0.23 us  [staged(): pl.pallas_call(staged_kernel, out_shape=(jax.ShapeDtypeStruct((rows, 2 *...]
    ppermute x1, starting transfers between devices: 3.69 us -> 2.62 us  [local(): from_face = lax.ppermute(given[:, :, LANES:], ('w', 'c'), facing)]
    unnamed x10 -> x12, local copies, waits for them, and re-layouts: 2.58 us -> 3.44 us
  transfers between devices with their start and end apart: 15 -> 15, of which waited for: 5 -> 5; matrix products, arithmetic and copies ran while one was open for 0% -> 0% of each run, Pallas kernels for 4% -> 7%
where the time goes in v5:
time: 96 us; the launch traced here: 94.9 us
  starting transfers between devices  54.7 us (57%)
  blocking collectives  13.3 us (14%)
  waiting for transfers between devices  13.2 us (14%)
  Pallas kernels  9.76 us (10%)
  local copies, waits for them, and re-layouts  3.56 us (4%)
    ppermute x11, starting transfers between devices, swapped(): return lax.ppermute(value, axis, [(i, i ^ flip) for i in range(count)])  47.7 us
    all_gather x1, blocking collectives, local(): lax.all_gather(joined(attended[None], across[None]), 'x', axis=0, tiled=F...  13.3 us
    ppermute x11, waiting for transfers between devices, swapped(): return lax.ppermute(value, axis, [(i, i ^ flip) for i in range(count)])  13.2 us
    pallas_call x4, Pallas kernels, attend(): pl.pallas_call(functools.partial(attend_kernel, low, high, stage), out_sh...  5.67 us
    unnamed x12, local copies, waits for them, and re-layouts  3.44 us
    ppermute x1, starting transfers between devices, local(): lax.ppermute(queries, ('w', 'c'), facing)  3 us
    ppermute x1, starting transfers between devices, local(): from_face = lax.ppermute(given[:, :, LANES:], ('w', 'c'), facing)  2.62 us
  transfers between devices with their start and end apart: 15, of which 5 were waited for; matrix products, arithmetic and copies ran while one was open for 0% of the time, Pallas kernels for 7%

profile of v5, /device:TPU:1, one launch (start us, length us, event | category | flops | bytes accessed | tf_op | source)
XLA Modules:
  0.0 94.9 jit_solution(14311671546700013992)
XLA Ops:
  0.0 0.0 copy-start
  0.0 0.9 copy-done
  0.9 0.0 copy-start.1
  0.9 0.9 copy-done.1
  1.8 0.0 copy-start.2
  1.8 0.9 copy-done.2
  2.7 0.0 copy-start.3
  2.7 0.7 copy-done.3
  3.4 0.0 copy-start.4
  3.4 0.2 shard_map.64
  3.7 0.7 collective-permute-start
  4.4 13.0 %collective-permute-start.4 = (bf16[224,512]{1,0:T(8,128)(2,1)S(1)}, bf16[224,512]{1,0:T(8,128)(2,1)S(1)}, u32[]{:S(2)}, u32[]{:S(2)}) collective-permute-start(bf16[224,512]{1,0:T(8,128)(2,1)S(1)} %get-tuple-element.26.refs_0_), channel_id=1, source_target_pairs={{0,32},{32,0},{64,96},{96,64},{1,33},{33,1},{65,97},{97,65},{2,34}... | collective-permute-start | bytes 688136 | tf_op jit(solution)/shard_map/ppermute | solution.py:24
  17.4 3.1 %collective-permute-start.1 = (bf16[224,256]{1,0:T(8,128)(2,1)S(1)}, bf16[224,256]{1,0:T(8,128)(2,1)S(1)}, u32[]{:S(2)}, u32[]{:S(2)}) collective-permute-start(bf16[224,256]{1,0:T(8,128)(2,1)S(1)} %get-tuple-element.29.refs_0_), channel_id=1, source_target_pairs={{0,8},{8,0},{1,9},{9,1},{2,10},{10,2},{3,11},{11,3},{4,12},{12,4},... | collective-permute-start | bytes 344072 | tf_op jit(solution)/shard_map/ppermute | solution.py:24
  20.5 3.0 %collective-permute-start.2 = (bf16[224,256]{1,0:T(8,128)(2,1)S(1)}, bf16[224,256]{1,0:T(8,128)(2,1)S(1)}, u32[]{:S(2)}, u32[]{:S(2)}) collective-permute-start(bf16[224,256]{1,0:T(8,128)(2,1)S(1)} %get-tuple-element.29.refs_0_), channel_id=1, source_target_pairs={{8,16},{16,8},{9,17},{17,9},{10,18},{18,10},{11,19},{19,11},{12,20... | collective-permute-start | bytes 344072 | tf_op jit(solution)/shard_map/ppermute | solution.py:283
  23.5 4.2 %collective-permute-start.3 = (bf16[1,32,384]{2,1,0:T(8,128)(2,1)S(1)}, bf16[1,32,384]{2,1,0:T(8,128)(2,1)S(1)}, u32[]{:S(2)}, u32[]{:S(2)}) collective-permute-start(bf16[1,32,384]{2,1,0:T(8,128)(2,1)S(1)} %get-tuple-element.28.refs_0_), channel_id=1, source_target_pairs={{0,256},{128,384},{256,0},{384,128},{1,257},{129,385},{257,1},{385... | collective-permute-start | bytes 73736 | tf_op jit(solution)/shard_map/ppermute | solution.py:24
  27.7 1.2 %collective-permute-done.3.refs_1_ = bf16[1,32,384]{2,1,0:T(8,128)(2,1)S(1)} collective-permute-done((bf16[1,32,384]{2,1,0:T(8,128)(2,1)S(1)}, bf16[1,32,384]{2,1,0:T(8,128)(2,1)S(1)}, u32[]{:S(2)}, u32[]{:S(2)}) %collective-permute-start.3) | collective-permute-done | bytes 24608 | tf_op jit(solution)/shard_map/ppermute | solution.py:24
  29.0 0.0 collective-permute-done.1.refs_1_
  29.0 0.0 collective-permute-done.2.refs_2_
  29.0 0.0 collective-permute-done.refs_2_
  29.0 0.0 collective-permute-done.4.refs_1_
  29.1 3.2 %collective-permute-start.6 = (bf16[672,512]{1,0:T(8,128)(2,1)S(1)}, bf16[672,512]{1,0:T(8,128)(2,1)S(1)}, u32[]{:S(2)}, u32[]{:S(2)}) collective-permute-start(bf16[672,512]{1,0:T(8,128)(2,1)S(1)} %shard_map.66.refs_3_), channel_id=1, source_target_pairs={{0,128},{128,0},{256,384},{384,256},{1,129},{129,1},{257,385},{385... | collective-permute-start | bytes 2064392 | tf_op jit(solution)/shard_map/ppermute | solution.py:24
  32.3 0.7 collective-permute-start.5
  33.0 2.5 %collective-permute-start.7 = (bf16[2,32,384]{2,1,0:T(8,128)(2,1)S(1)}, bf16[2,32,384]{2,1,0:T(8,128)(2,1)S(1)}, u32[]{:S(2)}, u32[]{:S(2)}) collective-permute-start(bf16[2,32,384]{2,1,0:T(8,128)(2,1)S(1)} %shard_map.65.refs_0_), channel_id=1, source_target_pairs={{0,32},{32,0},{64,96},{96,64},{1,33},{33,1},{65,97},{97,65},{2,34}... | collective-permute-start | bytes 147464 | tf_op jit(solution)/shard_map/ppermute | solution.py:24
  35.5 0.1 stack.23.pos_ref
  35.6 0.0 copy-done.4
  35.6 2.1 %shard_map.67 = (f32[2,136,768]{2,1,0:T(8,128)S(1)}, bf16[768,256]{1,0:T(8,128)(2,1)S(1)}) custom-call(s32[5]{0:T(128)S(1)} %stack.23.pos_ref, s32[2,3]{1,0:T(2,128)S(1)} %copy-done.4, bf16[224,256]{1,0:T(8,128)(2,1)S(1)} %get-tuple-element.29.refs_0_, bf16[224,256]{1,0:T(8,128)(2,1)S(1)} %collective-permute-done.1.refs_1_, ...), custom_call_target="tpu_custom_call" | custom-call | flops 462422016 | bytes 688128 | tf_op jit(solution)/shard_map/pallas_call | solution.py:178
  37.7 1.7 %collective-permute-done.7.refs_1_ = bf16[2,32,384]{2,1,0:T(8,128)(2,1)S(1)} collective-permute-done((bf16[2,32,384]{2,1,0:T(8,128)(2,1)S(1)}, bf16[2,32,384]{2,1,0:T(8,128)(2,1)S(1)}, u32[]{:S(2)}, u32[]{:S(2)}) %collective-permute-start.7) | collective-permute-done | bytes 49184 | tf_op jit(solution)/shard_map/ppermute | solution.py:24
  39.4 2.4 %collective-permute-start.8 = (bf16[4,32,384]{2,1,0:T(8,128)(2,1)S(1)}, bf16[4,32,384]{2,1,0:T(8,128)(2,1)S(1)}, u32[]{:S(2)}, u32[]{:S(2)}) collective-permute-start(bf16[4,32,384]{2,1,0:T(8,128)(2,1)S(1)} %shard_map.68.refs_0_), channel_id=1, source_target_pairs={{0,96},{32,64},{64,32},{96,0},{1,97},{33,65},{65,33},{97,1},{2,98}... | collective-permute-start | bytes 294920 | tf_op jit(solution)/shard_map/ppermute | solution.py:24
  41.7 6.0 %collective-permute-done.6.refs_1_ = bf16[672,512]{1,0:T(8,128)(2,1)S(1)} collective-permute-done((bf16[672,512]{1,0:T(8,128)(2,1)S(1)}, bf16[672,512]{1,0:T(8,128)(2,1)S(1)}, u32[]{:S(2)}, u32[]{:S(2)}) %collective-permute-start.6) | collective-permute-done | bytes 688160 | tf_op jit(solution)/shard_map/ppermute | solution.py:24
  47.7 2.4 %shard_map.69.refs_2_ = f32[2,136,768]{2,1,0:T(8,128)S(1)} custom-call(s32[5]{0:T(128)S(1)} %stack.23.pos_ref, s32[2,3]{1,0:T(2,128)S(1)} %copy-done.4, bf16[768,256]{1,0:T(8,128)(2,1)S(1)} %get-tuple-element.35.refs_0_, bf16[672,512]{1,0:T(8,128)(2,1)S(1)} %collective-permute-done.6.refs_1_, f32[2,136,768]{2,1,0:T(8,128)S(1)} %get-tuple-element.39.refs_2_), custom_call_target="tpu_custom_call" | custom-call | flops 462422016 | bytes 688128 | tf_op jit(solution)/shard_map/pallas_call | solution.py:178
  50.1 0.0 collective-permute-done.5.refs_1_
  50.1 0.6 shard_map.70
  50.7 0.0 collective-permute-done.8.refs_1_
  50.8 1.9 %collective-permute-start.9 = (f32[2,136,256]{2,1,0:T(8,128)S(1)}, f32[2,136,256]{2,1,0:T(8,128)S(1)}, u32[]{:S(2)}, u32[]{:S(2)}) collective-permute-start(f32[2,136,256]{2,1,0:T(8,128)S(1)} %get-tuple-element.48), channel_id=1, source_target_pairs={{0,8},{8,0},{1,9},{9,1},{2,10},{10,2},{3,11},{11,3},{4,12},{12,4},... | collective-permute-start | bytes 835592 | tf_op jit(solution)/shard_map/ppermute | solution.py:24
  52.7 2.6 %collective-permute-start.10 = (f32[2,136,256]{2,1,0:T(8,128)S(1)}, f32[2,136,256]{2,1,0:T(8,128)S(1)}, u32[]{:S(2)}, u32[]{:S(2)}) collective-permute-start(f32[2,136,256]{2,1,0:T(8,128)S(1)} %get-tuple-element.47), channel_id=1, source_target_pairs={{8,16},{16,8},{9,17},{17,9},{10,18},{18,10},{11,19},{19,11},{12,20... | collective-permute-start | bytes 835592 | tf_op jit(solution)/shard_map/ppermute | solution.py:302
  55.4 5.5 %collective-permute-start.12 = (bf16[8,32,384]{2,1,0:T(8,128)(2,1)S(1)}, bf16[8,32,384]{2,1,0:T(8,128)(2,1)S(1)}, u32[]{:S(2)}, u32[]{:S(2)}) collective-permute-start(bf16[8,32,384]{2,1,0:T(8,128)(2,1)S(1)} %shard_map.74.refs_0_), channel_id=1, source_target_pairs={{0,128},{128,0},{256,384},{384,256},{1,129},{129,1},{257,385},{385... | collective-permute-start | bytes 589832 | tf_op jit(solution)/shard_map/ppermute | solution.py:24
  60.9 0.6 shard_map.71.own_ref
  61.5 0.0 collective-permute-done.9.core_ref
  61.5 0.0 collective-permute-done.10.face_ref
  61.5 0.7 shard_map.72
  62.2 6.3 %collective-permute-start.11 = (bf16[224,256]{1,0:T(8,128)(2,1)S(1)}, bf16[224,256]{1,0:T(8,128)(2,1)S(1)}, u32[]{:S(2)}, u32[]{:S(2)}) collective-permute-start(bf16[224,256]{1,0:T(8,128)(2,1)S(1)} %shard_map.72), channel_id=1, source_target_pairs={{0,1},{1,0},{2,3},{3,2},{4,5},{5,4},{6,7},{7,6},{8,9},{9,8},{10,11... | collective-permute-start | bytes 344072 | tf_op jit(solution)/shard_map/ppermute | solution.py:24
  68.6 0.0 collective-permute-done.12.refs_1_
  68.6 1.9 %collective-permute-start.13 = (bf16[16,32,384]{2,1,0:T(8,128)(2,1)S(1)}, bf16[16,32,384]{2,1,0:T(8,128)(2,1)S(1)}, u32[]{:S(2)}, u32[]{:S(2)}) collective-permute-start(bf16[16,32,384]{2,1,0:T(8,128)(2,1)S(1)} %shard_map.75.refs_0_), channel_id=1, source_target_pairs={{0,16},{16,0},{1,17},{17,1},{2,18},{18,2},{3,19},{19,3},{4,20},{20... | collective-permute-start | bytes 1179656 | tf_op jit(solution)/shard_map/ppermute | solution.py:24
  70.6 2.4 %collective-permute-done.11 = bf16[224,256]{1,0:T(8,128)(2,1)S(1)} collective-permute-done((bf16[224,256]{1,0:T(8,128)(2,1)S(1)}, bf16[224,256]{1,0:T(8,128)(2,1)S(1)}, u32[]{:S(2)}, u32[]{:S(2)}) %collective-permute-start.11) | collective-permute-done | bytes 114720 | tf_op jit(solution)/shard_map/ppermute | solution.py:24
  73.0 0.0 copy-start.5
  73.0 13.3 %all-gather = bf16[8,224,256]{2,1,0:T(8,128)(2,1)S(1)} all-gather(bf16[2,224,256]{2,1,0:T(8,128)(2,1)S(1)} %shard_map.73), channel_id=2, replica_groups=mesh['t'=4,'u'=4,'w'=2,'c'=2,'x'=4,'h'=2] {'x'}, dimensions={0}, use_global_device_ids=true | all-gather | bytes 1146880 | tf_op jit(solution)/shard_map/all_gather | solution.py:311
  86.3 0.0 collective-permute-done.13.refs_1_
  86.3 0.1 shard_map.76.mine_ref
  86.4 3.6 %collective-permute-start.14 = (bf16[32,32,384]{2,1,0:T(8,128)(2,1)S(1)}, bf16[32,32,384]{2,1,0:T(8,128)(2,1)S(1)}, u32[]{:S(2)}, u32[]{:S(2)}) collective-permute-start(bf16[32,32,384]{2,1,0:T(8,128)(2,1)S(1)} %shard_map.76.mine_ref), channel_id=1, source_target_pairs={{0,8},{8,0},{1,9},{9,1},{2,10},{10,2},{3,11},{11,3},{4,12},{12,4},... | collective-permute-start | bytes 2359304 | tf_op jit(solution)/shard_map/ppermute | solution.py:24
  90.0 0.0 copy-done.5
  90.0 1.9 %collective-permute-done.14.other_ref = bf16[32,32,384]{2,1,0:T(8,128)(2,1)S(1)} collective-permute-done((bf16[32,32,384]{2,1,0:T(8,128)(2,1)S(1)}, bf16[32,32,384]{2,1,0:T(8,128)(2,1)S(1)}, u32[]{:S(2)}, u32[]{:S(2)}) %collective-permute-start.14) | collective-permute-done | bytes 786464 | tf_op jit(solution)/shard_map/ppermute | solution.py:24
  91.9 1.1 %shard_map.77.weight_ref = bf16[2048,384]{1,0:T(8,128)(2,1)S(1)} custom-call(s32[5]{0:T(128)S(1)} %stack.23.pos_ref, bf16[32,32,384]{2,1,0:T(8,128)(2,1)S(1)} %shard_map.76.mine_ref, bf16[32,32,384]{2,1,0:T(8,128)(2,1)S(1)} %collective-permute-done.14.other_ref), custom_call_target="tpu_custom_call" | custom-call | tf_op jit(solution)/shard_map/pallas_call | solution.py:236
  93.0 1.9 %shard_map.78 = bf16[224,384]{1,0:T(8,128)(2,1)} custom-call(s32[5]{0:T(128)S(1)} %stack.23.pos_ref, bf16[4,2,224,256]{3,2,1,0:T(8,128)(2,1)S(1)} %bitcast.8, bf16[2048,384]{1,0:T(8,128)(2,1)S(1)} %shard_map.77.weight_ref, f32[1,384]{1,0:T(1,128)S(1)} %broadcast_in_dim.11.gate_ref), custom_call_target="tpu_custom_call" | custom-call | tf_op jit(solution)/shard_map/pallas_call | solution.py:260
  (8 shorter events, 0.2 us)
Async XLA Ops:
  0.0 0.9 copy-start
  0.9 0.9 copy-start.1
  1.8 0.9 copy-start.2
  2.7 0.7 copy-start.3
  3.4 32.2 %copy-start.4 = (s32[2,3]{1,0:T(2,128)S(1)}, s32[2,3]{1,0:T(2,128)}, u32[]{:S(2)}) copy-start(s32[2,3]{1,0:T(2,128)} %ext_ref.7) | copy-start | bytes 76
  3.7 25.3 %collective-permute-start = (bf16[224,512]{1,0:T(8,128)(2,1)S(1)}, bf16[224,512]{1,0:T(8,128)(2,1)S(1)}, u32[]{:S(2)}, u32[]{:S(2)}) collective-permute-start(bf16[224,512]{1,0:T(8,128)(2,1)S(1)} %get-tuple-element.26.refs_0_), channel_id=1, source_target_pairs={{32,64},{64,32},{33,65},{65,33},{34,66},{66,34},{35,67},{67,35},{3... | collective-permute-start | bytes 688136 | tf_op jit(solution)/shard_map/ppermute | solution.py:28
  4.4 24.7 %collective-permute-start.4 = (bf16[224,512]{1,0:T(8,128)(2,1)S(1)}, bf16[224,512]{1,0:T(8,128)(2,1)S(1)}, u32[]{:S(2)}, u32[]{:S(2)}) collective-permute-start(bf16[224,512]{1,0:T(8,128)(2,1)S(1)} %get-tuple-element.26.refs_0_), channel_id=1, source_target_pairs={{0,32},{32,0},{64,96},{96,64},{1,33},{33,1},{65,97},{97,65},{2,34}... | collective-permute-start | bytes 688136 | tf_op jit(solution)/shard_map/ppermute | solution.py:24
  17.4 11.6 %collective-permute-start.1 = (bf16[224,256]{1,0:T(8,128)(2,1)S(1)}, bf16[224,256]{1,0:T(8,128)(2,1)S(1)}, u32[]{:S(2)}, u32[]{:S(2)}) collective-permute-start(bf16[224,256]{1,0:T(8,128)(2,1)S(1)} %get-tuple-element.29.refs_0_), channel_id=1, source_target_pairs={{0,8},{8,0},{1,9},{9,1},{2,10},{10,2},{3,11},{11,3},{4,12},{12,4},... | collective-permute-start | bytes 344072 | tf_op jit(solution)/shard_map/ppermute | solution.py:24
  20.5 8.5 %collective-permute-start.2 = (bf16[224,256]{1,0:T(8,128)(2,1)S(1)}, bf16[224,256]{1,0:T(8,128)(2,1)S(1)}, u32[]{:S(2)}, u32[]{:S(2)}) collective-permute-start(bf16[224,256]{1,0:T(8,128)(2,1)S(1)} %get-tuple-element.29.refs_0_), channel_id=1, source_target_pairs={{8,16},{16,8},{9,17},{17,9},{10,18},{18,10},{11,19},{19,11},{12,20... | collective-permute-start | bytes 344072 | tf_op jit(solution)/shard_map/ppermute | solution.py:283
  23.5 5.5 %collective-permute-start.3 = (bf16[1,32,384]{2,1,0:T(8,128)(2,1)S(1)}, bf16[1,32,384]{2,1,0:T(8,128)(2,1)S(1)}, u32[]{:S(2)}, u32[]{:S(2)}) collective-permute-start(bf16[1,32,384]{2,1,0:T(8,128)(2,1)S(1)} %get-tuple-element.28.refs_0_), channel_id=1, source_target_pairs={{0,256},{128,384},{256,0},{384,128},{1,257},{129,385},{257,1},{385... | collective-permute-start | bytes 73736 | tf_op jit(solution)/shard_map/ppermute | solution.py:24
  29.1 18.6 %collective-permute-start.6 = (bf16[672,512]{1,0:T(8,128)(2,1)S(1)}, bf16[672,512]{1,0:T(8,128)(2,1)S(1)}, u32[]{:S(2)}, u32[]{:S(2)}) collective-permute-start(bf16[672,512]{1,0:T(8,128)(2,1)S(1)} %shard_map.66.refs_3_), channel_id=1, source_target_pairs={{0,128},{128,0},{256,384},{384,256},{1,129},{129,1},{257,385},{385... | collective-permute-start | bytes 2064392 | tf_op jit(solution)/shard_map/ppermute | solution.py:24
  32.3 17.8 %collective-permute-start.5 = (bf16[672,512]{1,0:T(8,128)(2,1)S(1)}, bf16[672,512]{1,0:T(8,128)(2,1)S(1)}, u32[]{:S(2)}, u32[]{:S(2)}) collective-permute-start(bf16[672,512]{1,0:T(8,128)(2,1)S(1)} %shard_map.66.refs_3_), channel_id=1, source_target_pairs={{128,256},{256,128},{129,257},{257,129},{130,258},{258,130},{131,2... | collective-permute-start | bytes 2064392 | tf_op jit(solution)/shard_map/ppermute | solution.py:28
  33.0 6.4 %collective-permute-start.7 = (bf16[2,32,384]{2,1,0:T(8,128)(2,1)S(1)}, bf16[2,32,384]{2,1,0:T(8,128)(2,1)S(1)}, u32[]{:S(2)}, u32[]{:S(2)}) collective-permute-start(bf16[2,32,384]{2,1,0:T(8,128)(2,1)S(1)} %shard_map.65.refs_0_), channel_id=1, source_target_pairs={{0,32},{32,0},{64,96},{96,64},{1,33},{33,1},{65,97},{97,65},{2,34}... | collective-permute-start | bytes 147464 | tf_op jit(solution)/shard_map/ppermute | solution.py:24
  39.4 11.4 %collective-permute-start.8 = (bf16[4,32,384]{2,1,0:T(8,128)(2,1)S(1)}, bf16[4,32,384]{2,1,0:T(8,128)(2,1)S(1)}, u32[]{:S(2)}, u32[]{:S(2)}) collective-permute-start(bf16[4,32,384]{2,1,0:T(8,128)(2,1)S(1)} %shard_map.68.refs_0_), channel_id=1, source_target_pairs={{0,96},{32,64},{64,32},{96,0},{1,97},{33,65},{65,33},{97,1},{2,98}... | collective-permute-start | bytes 294920 | tf_op jit(solution)/shard_map/ppermute | solution.py:24
  50.8 10.7 %collective-permute-start.9 = (f32[2,136,256]{2,1,0:T(8,128)S(1)}, f32[2,136,256]{2,1,0:T(8,128)S(1)}, u32[]{:S(2)}, u32[]{:S(2)}) collective-permute-start(f32[2,136,256]{2,1,0:T(8,128)S(1)} %get-tuple-element.48), channel_id=1, source_target_pairs={{0,8},{8,0},{1,9},{9,1},{2,10},{10,2},{3,11},{11,3},{4,12},{12,4},... | collective-permute-start | bytes 835592 | tf_op jit(solution)/shard_map/ppermute | solution.py:24
  52.7 8.8 %collective-permute-start.10 = (f32[2,136,256]{2,1,0:T(8,128)S(1)}, f32[2,136,256]{2,1,0:T(8,128)S(1)}, u32[]{:S(2)}, u32[]{:S(2)}) collective-permute-start(f32[2,136,256]{2,1,0:T(8,128)S(1)} %get-tuple-element.47), channel_id=1, source_target_pairs={{8,16},{16,8},{9,17},{17,9},{10,18},{18,10},{11,19},{19,11},{12,20... | collective-permute-start | bytes 835592 | tf_op jit(solution)/shard_map/ppermute | solution.py:302
  55.4 13.2 %collective-permute-start.12 = (bf16[8,32,384]{2,1,0:T(8,128)(2,1)S(1)}, bf16[8,32,384]{2,1,0:T(8,128)(2,1)S(1)}, u32[]{:S(2)}, u32[]{:S(2)}) collective-permute-start(bf16[8,32,384]{2,1,0:T(8,128)(2,1)S(1)} %shard_map.74.refs_0_), channel_id=1, source_target_pairs={{0,128},{128,0},{256,384},{384,256},{1,129},{129,1},{257,385},{385... | collective-permute-start | bytes 589832 | tf_op jit(solution)/shard_map/ppermute | solution.py:24
  62.2 10.8 %collective-permute-start.11 = (bf16[224,256]{1,0:T(8,128)(2,1)S(1)}, bf16[224,256]{1,0:T(8,128)(2,1)S(1)}, u32[]{:S(2)}, u32[]{:S(2)}) collective-permute-start(bf16[224,256]{1,0:T(8,128)(2,1)S(1)} %shard_map.72), channel_id=1, source_target_pairs={{0,1},{1,0},{2,3},{3,2},{4,5},{5,4},{6,7},{7,6},{8,9},{9,8},{10,11... | collective-permute-start | bytes 344072 | tf_op jit(solution)/shard_map/ppermute | solution.py:24
  68.6 17.7 %collective-permute-start.13 = (bf16[16,32,384]{2,1,0:T(8,128)(2,1)S(1)}, bf16[16,32,384]{2,1,0:T(8,128)(2,1)S(1)}, u32[]{:S(2)}, u32[]{:S(2)}) collective-permute-start(bf16[16,32,384]{2,1,0:T(8,128)(2,1)S(1)} %shard_map.75.refs_0_), channel_id=1, source_target_pairs={{0,16},{16,0},{1,17},{17,1},{2,18},{18,2},{3,19},{19,3},{4,20},{20... | collective-permute-start | bytes 1179656 | tf_op jit(solution)/shard_map/ppermute | solution.py:24
  73.0 17.0 %copy-start.5 = (f32[384]{0:T(512)S(1)}, f32[384]{0:T(512)}, u32[]{:S(2)}) copy-start(f32[384]{0:T(512)} %param.11) | copy-start | bytes 4612
  86.4 5.5 %collective-permute-start.14 = (bf16[32,32,384]{2,1,0:T(8,128)(2,1)S(1)}, bf16[32,32,384]{2,1,0:T(8,128)(2,1)S(1)}, u32[]{:S(2)}, u32[]{:S(2)}) collective-permute-start(bf16[32,32,384]{2,1,0:T(8,128)(2,1)S(1)} %shard_map.76.mine_ref), channel_id=1, source_target_pairs={{0,8},{8,0},{1,9},{9,1},{2,10},{10,2},{3,11},{11,3},{4,12},{12,4},... | collective-permute-start | bytes 2359304 | tf_op jit(solution)/shard_map/ppermute | solution.py:24

commit v6 on v3

--- a/solution.py
+++ b/solution.py
@@ -67,6 +67,7 @@
         in_specs=[pl.BlockSpec(memory_space=pl.ANY)] * 2,
         out_specs=pl.BlockSpec(memory_space=pltpu.VMEM),
         scratch_shapes=[pltpu.SemaphoreType.DMA((2,))],
+        compiler_params=pltpu.CompilerParams(vmem_limit_bytes=VMEM_LIMIT),
     )(left, right)
 
 

time: 95.5 us -> 94.8 us (level)
  Pallas kernels: 9.79 us -> 7.84 us
  blocking collectives: 12.7 us -> 13.7 us
  starting transfers between devices: 53.6 us -> 54.6 us
    pallas_call x1, Pallas kernels: 1.68 us -> 0.04 us  [beside(): pl.pallas_call(beside_kernel, out_shape=jax.ShapeDtypeStruct((left.shape[...]
    ppermute x11, waiting for transfers between devices: 15.6 us -> 14.6 us  [swapped(): return lax.ppermute(value, axis, [(i, i ^ flip) for i in range(count)])]
    unnamed x10 -> x12, local copies, waits for them, and re-layouts: 1.68 us -> 2.54 us
where the time goes in v6:
time: 94.8 us; the launch traced here: 93.7 us
  starting transfers between devices  54.6 us (58%)
  waiting for transfers between devices  14.7 us (16%)
  blocking collectives  13.7 us (14%)
  Pallas kernels  7.84 us (8%)
  local copies, waits for them, and re-layouts  2.67 us (3%)
    ppermute x11, starting transfers between devices, swapped(): return lax.ppermute(value, axis, [(i, i ^ flip) for i in range(count)])  47 us
    ppermute x11, waiting for transfers between devices, swapped(): return lax.ppermute(value, axis, [(i, i ^ flip) for i in range(count)])  14.6 us
    all_gather x1, blocking collectives, local(): lax.all_gather(joined(attended[None], across[None]), 'x', axis=0, tiled=F...  13.7 us
    pallas_call x4, Pallas kernels, attend(): pl.pallas_call(functools.partial(attend_kernel, low, high, stage), out_sh...  3.94 us
    ppermute x1, starting transfers between devices, local(): from_face = lax.ppermute(given[:, :, LANES:], ('w', 'c'), facing)  3.03 us
    ppermute x1, starting transfers between devices, local(): lax.ppermute(queries, ('w', 'c'), facing)  3 us
    unnamed x12, local copies, waits for them, and re-layouts  2.54 us
  transfers between devices with their start and end apart: 15, of which 5 were waited for; matrix products, arithmetic and copies ran while one was open for 0% of the time, Pallas kernels for 5%

profile of v6, /device:TPU:1, one launch (start us, length us, event | category | flops | bytes accessed | tf_op | source)
XLA Modules:
  0.0 93.7 jit_solution(16913644590019863597)
XLA Ops:
  0.0 0.0 copy-start
  0.0 0.9 copy-done
  0.9 0.0 copy-start.1
  0.9 0.9 copy-done.1
  1.8 0.0 copy-start.3
  1.8 0.0 copy-start.4
  1.8 0.8 collective-permute-start
  2.7 13.0 %collective-permute-start.4 = (bf16[224,512]{1,0:T(8,128)(2,1)S(1)}, bf16[224,512]{1,0:T(8,128)(2,1)S(1)}, u32[]{:S(2)}, u32[]{:S(2)}) collective-permute-start(bf16[224,512]{1,0:T(8,128)(2,1)S(1)} %shard_map.64.refs_0_), channel_id=1, source_target_pairs={{0,32},{32,0},{64,96},{96,64},{1,33},{33,1},{65,97},{97,65},{2,34}... | collective-permute-start | bytes 688136 | tf_op jit(solution)/shard_map/ppermute | solution.py:24
  15.7 3.1 %collective-permute-start.1 = (bf16[224,256]{1,0:T(8,128)(2,1)}, bf16[224,256]{1,0:T(8,128)(2,1)S(1)}, u32[]{:S(2)}, u32[]{:S(2)}) collective-permute-start(bf16[224,256]{1,0:T(8,128)(2,1)} %refs_0_), channel_id=1, source_target_pairs={{0,8},{8,0},{1,9},{9,1},{2,10},{10,2},{3,11},{11,3},{4,12},{12,4},... | collective-permute-start | bytes 344072 | tf_op jit(solution)/shard_map/ppermute | solution.py:24
  18.8 3.0 %collective-permute-start.2 = (bf16[224,256]{1,0:T(8,128)(2,1)}, bf16[224,256]{1,0:T(8,128)(2,1)S(1)}, u32[]{:S(2)}, u32[]{:S(2)}) collective-permute-start(bf16[224,256]{1,0:T(8,128)(2,1)} %refs_0_), channel_id=1, source_target_pairs={{8,16},{16,8},{9,17},{17,9},{10,18},{18,10},{11,19},{19,11},{12,20... | collective-permute-start | bytes 344072 | tf_op jit(solution)/shard_map/ppermute | solution.py:272
  21.8 4.2 %collective-permute-start.3 = (bf16[1,32,384]{2,1,0:T(8,128)(2,1)}, bf16[1,32,384]{2,1,0:T(8,128)(2,1)S(1)}, u32[]{:S(2)}, u32[]{:S(2)}) collective-permute-start(bf16[1,32,384]{2,1,0:T(8,128)(2,1)} %bitcast.12), channel_id=1, source_target_pairs={{0,256},{128,384},{256,0},{384,128},{1,257},{129,385},{257,1},{385... | collective-permute-start | bytes 73736 | tf_op jit(solution)/shard_map/ppermute | solution.py:24
  26.0 1.5 %collective-permute-done.3.refs_1_ = bf16[1,32,384]{2,1,0:T(8,128)(2,1)S(1)} collective-permute-done((bf16[1,32,384]{2,1,0:T(8,128)(2,1)}, bf16[1,32,384]{2,1,0:T(8,128)(2,1)S(1)}, u32[]{:S(2)}, u32[]{:S(2)}) %collective-permute-start.3) | collective-permute-done | bytes 24608 | tf_op jit(solution)/shard_map/ppermute | solution.py:24
  27.5 0.0 copy-start.2
  27.5 0.7 copy-done.2
  28.2 0.0 collective-permute-done.1.refs_1_
  28.2 0.0 collective-permute-done.2.refs_2_
  28.3 0.0 collective-permute-done.refs_2_
  28.3 0.0 collective-permute-done.4.refs_1_
  28.3 3.2 %collective-permute-start.6 = (bf16[672,512]{1,0:T(8,128)(2,1)S(1)}, bf16[672,512]{1,0:T(8,128)(2,1)S(1)}, u32[]{:S(2)}, u32[]{:S(2)}) collective-permute-start(bf16[672,512]{1,0:T(8,128)(2,1)S(1)} %shard_map.66.refs_3_), channel_id=1, source_target_pairs={{0,128},{128,0},{256,384},{384,256},{1,129},{129,1},{257,385},{385... | collective-permute-start | bytes 2064392 | tf_op jit(solution)/shard_map/ppermute | solution.py:24
  31.5 0.7 collective-permute-start.5
  32.3 1.9 %collective-permute-start.7 = (bf16[2,32,384]{2,1,0:T(8,128)(2,1)S(1)}, bf16[2,32,384]{2,1,0:T(8,128)(2,1)S(1)}, u32[]{:S(2)}, u32[]{:S(2)}) collective-permute-start(bf16[2,32,384]{2,1,0:T(8,128)(2,1)S(1)} %shard_map.65.refs_0_), channel_id=1, source_target_pairs={{0,32},{32,0},{64,96},{96,64},{1,33},{33,1},{65,97},{97,65},{2,34}... | collective-permute-start | bytes 147464 | tf_op jit(solution)/shard_map/ppermute | solution.py:24
  34.2 0.1 stack.23.pos_ref
  34.3 0.0 copy-done.3
  34.3 0.0 copy-done.4
  34.3 1.6 %shard_map.67 = (f32[2,136,768]{2,1,0:T(8,128)S(1)}, bf16[768,256]{1,0:T(8,128)(2,1)S(1)}) custom-call(s32[5]{0:T(128)S(1)} %stack.23.pos_ref, s32[2,3]{1,0:T(2,128)S(1)} %copy-done.3, bf16[224,256]{1,0:T(8,128)(2,1)S(1)} %copy-done.4, bf16[224,256]{1,0:T(8,128)(2,1)S(1)} %collective-permute-done.1.refs_1_, ...), custom_call_target="tpu_custom_call" | custom-call | flops 462422016 | bytes 688128 | tf_op jit(solution)/shard_map/pallas_call | solution.py:167
  35.9 2.5 %collective-permute-done.7.refs_1_ = bf16[2,32,384]{2,1,0:T(8,128)(2,1)S(1)} collective-permute-done((bf16[2,32,384]{2,1,0:T(8,128)(2,1)S(1)}, bf16[2,32,384]{2,1,0:T(8,128)(2,1)S(1)}, u32[]{:S(2)}, u32[]{:S(2)}) %collective-permute-start.7) | collective-permute-done | bytes 49184 | tf_op jit(solution)/shard_map/ppermute | solution.py:24
  38.4 1.9 %collective-permute-start.8 = (bf16[4,32,384]{2,1,0:T(8,128)(2,1)S(1)}, bf16[4,32,384]{2,1,0:T(8,128)(2,1)S(1)}, u32[]{:S(2)}, u32[]{:S(2)}) collective-permute-start(bf16[4,32,384]{2,1,0:T(8,128)(2,1)S(1)} %shard_map.68.refs_0_), channel_id=1, source_target_pairs={{0,96},{32,64},{64,32},{96,0},{1,97},{33,65},{65,33},{97,1},{2,98}... | collective-permute-start | bytes 294920 | tf_op jit(solution)/shard_map/ppermute | solution.py:24
  40.4 6.6 %collective-permute-done.6.refs_1_ = bf16[672,512]{1,0:T(8,128)(2,1)S(1)} collective-permute-done((bf16[672,512]{1,0:T(8,128)(2,1)S(1)}, bf16[672,512]{1,0:T(8,128)(2,1)S(1)}, u32[]{:S(2)}, u32[]{:S(2)}) %collective-permute-start.6) | collective-permute-done | bytes 688160 | tf_op jit(solution)/shard_map/ppermute | solution.py:24
  47.0 1.1 %shard_map.69.refs_2_ = f32[2,136,768]{2,1,0:T(8,128)S(1)} custom-call(s32[5]{0:T(128)S(1)} %stack.23.pos_ref, s32[2,3]{1,0:T(2,128)S(1)} %copy-done.3, bf16[768,256]{1,0:T(8,128)(2,1)S(1)} %get-tuple-element.29.refs_0_, bf16[672,512]{1,0:T(8,128)(2,1)S(1)} %collective-permute-done.6.refs_1_, f32[2,136,768]{2,1,0:T(8,128)S(1)} %get-tuple-element.33.refs_2_), custom_call_target="tpu_custom_call" | custom-call | flops 462422016 | bytes 688128 | tf_op jit(solution)/shard_map/pallas_call | solution.py:167
  48.1 0.0 collective-permute-done.5.refs_1_
  48.1 0.6 shard_map.70
  48.7 0.0 collective-permute-done.8.refs_1_
  48.8 1.9 %collective-permute-start.9 = (f32[2,136,256]{2,1,0:T(8,128)S(1)}, f32[2,136,256]{2,1,0:T(8,128)S(1)}, u32[]{:S(2)}, u32[]{:S(2)}) collective-permute-start(f32[2,136,256]{2,1,0:T(8,128)S(1)} %get-tuple-element.42), channel_id=1, source_target_pairs={{0,8},{8,0},{1,9},{9,1},{2,10},{10,2},{3,11},{11,3},{4,12},{12,4},... | collective-permute-start | bytes 835592 | tf_op jit(solution)/shard_map/ppermute | solution.py:24
  50.7 3.0 %collective-permute-start.10 = (f32[2,136,256]{2,1,0:T(8,128)S(1)}, f32[2,136,256]{2,1,0:T(8,128)S(1)}, u32[]{:S(2)}, u32[]{:S(2)}) collective-permute-start(f32[2,136,256]{2,1,0:T(8,128)S(1)} %get-tuple-element.41), channel_id=1, source_target_pairs={{8,16},{16,8},{9,17},{17,9},{10,18},{18,10},{11,19},{19,11},{12,20... | collective-permute-start | bytes 835592 | tf_op jit(solution)/shard_map/ppermute | solution.py:292
  53.8 6.1 %collective-permute-start.12 = (bf16[8,32,384]{2,1,0:T(8,128)(2,1)S(1)}, bf16[8,32,384]{2,1,0:T(8,128)(2,1)S(1)}, u32[]{:S(2)}, u32[]{:S(2)}) collective-permute-start(bf16[8,32,384]{2,1,0:T(8,128)(2,1)S(1)} %shard_map.74.refs_0_), channel_id=1, source_target_pairs={{0,128},{128,0},{256,384},{384,256},{1,129},{129,1},{257,385},{385... | collective-permute-start | bytes 589832 | tf_op jit(solution)/shard_map/ppermute | solution.py:24
  59.9 0.6 shard_map.71.own_ref
  60.5 0.0 collective-permute-done.9.core_ref
  60.5 0.0 collective-permute-done.10.face_ref
  60.6 0.7 shard_map.72
  61.2 6.6 %collective-permute-start.11 = (bf16[224,256]{1,0:T(8,128)(2,1)S(1)}, bf16[224,256]{1,0:T(8,128)(2,1)S(1)}, u32[]{:S(2)}, u32[]{:S(2)}) collective-permute-start(bf16[224,256]{1,0:T(8,128)(2,1)S(1)} %shard_map.72), channel_id=1, source_target_pairs={{0,1},{1,0},{2,3},{3,2},{4,5},{5,4},{6,7},{7,6},{8,9},{9,8},{10,11... | collective-permute-start | bytes 344072 | tf_op jit(solution)/shard_map/ppermute | solution.py:24
  67.8 0.0 collective-permute-done.12.refs_1_
  67.9 1.9 %collective-permute-start.13 = (bf16[16,32,384]{2,1,0:T(8,128)(2,1)S(1)}, bf16[16,32,384]{2,1,0:T(8,128)(2,1)S(1)}, u32[]{:S(2)}, u32[]{:S(2)}) collective-permute-start(bf16[16,32,384]{2,1,0:T(8,128)(2,1)S(1)} %shard_map.75.refs_0_), channel_id=1, source_target_pairs={{0,16},{16,0},{1,17},{17,1},{2,18},{18,2},{3,19},{19,3},{4,20},{20... | collective-permute-start | bytes 1179656 | tf_op jit(solution)/shard_map/ppermute | solution.py:24
  69.8 2.2 %collective-permute-done.11 = bf16[224,256]{1,0:T(8,128)(2,1)S(1)} collective-permute-done((bf16[224,256]{1,0:T(8,128)(2,1)S(1)}, bf16[224,256]{1,0:T(8,128)(2,1)S(1)}, u32[]{:S(2)}, u32[]{:S(2)}) %collective-permute-start.11) | collective-permute-done | bytes 114720 | tf_op jit(solution)/shard_map/ppermute | solution.py:24
  72.0 0.0 copy-start.5
  72.0 13.7 %all-gather = bf16[8,224,256]{2,1,0:T(8,128)(2,1)S(1)} all-gather(bf16[2,224,256]{2,1,0:T(8,128)(2,1)S(1)} %shard_map.73), channel_id=2, replica_groups=mesh['t'=4,'u'=4,'w'=2,'c'=2,'x'=4,'h'=2] {'x'}, dimensions={0}, use_global_device_ids=true | all-gather | bytes 1146880 | tf_op jit(solution)/shard_map/all_gather | solution.py:301
  85.7 0.0 collective-permute-done.13.refs_1_
  85.7 0.1 shard_map.76.mine_ref
  85.8 3.1 %collective-permute-start.14 = (bf16[32,32,384]{2,1,0:T(8,128)(2,1)S(1)}, bf16[32,32,384]{2,1,0:T(8,128)(2,1)S(1)}, u32[]{:S(2)}, u32[]{:S(2)}) collective-permute-start(bf16[32,32,384]{2,1,0:T(8,128)(2,1)S(1)} %shard_map.76.mine_ref), channel_id=1, source_target_pairs={{0,8},{8,0},{1,9},{9,1},{2,10},{10,2},{3,11},{11,3},{4,12},{12,4},... | collective-permute-start | bytes 2359304 | tf_op jit(solution)/shard_map/ppermute | solution.py:24
  88.8 0.0 copy-done.5
  88.9 1.9 %collective-permute-done.14.other_ref = bf16[32,32,384]{2,1,0:T(8,128)(2,1)S(1)} collective-permute-done((bf16[32,32,384]{2,1,0:T(8,128)(2,1)S(1)}, bf16[32,32,384]{2,1,0:T(8,128)(2,1)S(1)}, u32[]{:S(2)}, u32[]{:S(2)}) %collective-permute-start.14) | collective-permute-done | bytes 786464 | tf_op jit(solution)/shard_map/ppermute | solution.py:24
  90.7 1.1 %shard_map.77.weight_ref = bf16[2048,384]{1,0:T(8,128)(2,1)S(1)} custom-call(s32[5]{0:T(128)S(1)} %stack.23.pos_ref, bf16[32,32,384]{2,1,0:T(8,128)(2,1)S(1)} %shard_map.76.mine_ref, bf16[32,32,384]{2,1,0:T(8,128)(2,1)S(1)} %collective-permute-done.14.other_ref), custom_call_target="tpu_custom_call" | custom-call | tf_op jit(solution)/shard_map/pallas_call | solution.py:225
  91.8 1.9 %shard_map.78 = bf16[224,384]{1,0:T(8,128)(2,1)} custom-call(s32[5]{0:T(128)S(1)} %stack.23.pos_ref, bf16[4,2,224,256]{3,2,1,0:T(8,128)(2,1)S(1)} %bitcast.9, bf16[2048,384]{1,0:T(8,128)(2,1)S(1)} %shard_map.77.weight_ref, f32[1,384]{1,0:T(1,128)S(1)} %broadcast_in_dim.15.gate_ref), custom_call_target="tpu_custom_call" | custom-call | tf_op jit(solution)/shard_map/pallas_call | solution.py:249
  (9 shorter events, 0.2 us)
Async XLA Ops:
  0.0 0.9 copy-start
  0.9 0.9 copy-start.1
  1.8 32.5 %copy-start.3 = (s32[2,3]{1,0:T(2,128)S(1)}, s32[2,3]{1,0:T(2,128)}, u32[]{:S(2)}) copy-start(s32[2,3]{1,0:T(2,128)} %ext_ref.7) | copy-start | bytes 76
  1.8 32.5 %copy-start.4 = (bf16[224,256]{1,0:T(8,128)(2,1)S(1)}, bf16[224,256]{1,0:T(8,128)(2,1)}, u32[]{:S(2)}) copy-start(bf16[224,256]{1,0:T(8,128)(2,1)} %refs_0_) | copy-start | bytes 344068
  1.8 26.4 %collective-permute-start = (bf16[224,512]{1,0:T(8,128)(2,1)S(1)}, bf16[224,512]{1,0:T(8,128)(2,1)S(1)}, u32[]{:S(2)}, u32[]{:S(2)}) collective-permute-start(bf16[224,512]{1,0:T(8,128)(2,1)S(1)} %shard_map.64.refs_0_), channel_id=1, source_target_pairs={{32,64},{64,32},{33,65},{65,33},{34,66},{66,34},{35,67},{67,35},{3... | collective-permute-start | bytes 688136 | tf_op jit(solution)/shard_map/ppermute | solution.py:28
  2.7 25.6 %collective-permute-start.4 = (bf16[224,512]{1,0:T(8,128)(2,1)S(1)}, bf16[224,512]{1,0:T(8,128)(2,1)S(1)}, u32[]{:S(2)}, u32[]{:S(2)}) collective-permute-start(bf16[224,512]{1,0:T(8,128)(2,1)S(1)} %shard_map.64.refs_0_), channel_id=1, source_target_pairs={{0,32},{32,0},{64,96},{96,64},{1,33},{33,1},{65,97},{97,65},{2,34}... | collective-permute-start | bytes 688136 | tf_op jit(solution)/shard_map/ppermute | solution.py:24
  15.7 12.6 %collective-permute-start.1 = (bf16[224,256]{1,0:T(8,128)(2,1)}, bf16[224,256]{1,0:T(8,128)(2,1)S(1)}, u32[]{:S(2)}, u32[]{:S(2)}) collective-permute-start(bf16[224,256]{1,0:T(8,128)(2,1)} %refs_0_), channel_id=1, source_target_pairs={{0,8},{8,0},{1,9},{9,1},{2,10},{10,2},{3,11},{11,3},{4,12},{12,4},... | collective-permute-start | bytes 344072 | tf_op jit(solution)/shard_map/ppermute | solution.py:24
  18.8 9.4 %collective-permute-start.2 = (bf16[224,256]{1,0:T(8,128)(2,1)}, bf16[224,256]{1,0:T(8,128)(2,1)S(1)}, u32[]{:S(2)}, u32[]{:S(2)}) collective-permute-start(bf16[224,256]{1,0:T(8,128)(2,1)} %refs_0_), channel_id=1, source_target_pairs={{8,16},{16,8},{9,17},{17,9},{10,18},{18,10},{11,19},{19,11},{12,20... | collective-permute-start | bytes 344072 | tf_op jit(solution)/shard_map/ppermute | solution.py:272
  21.8 5.7 %collective-permute-start.3 = (bf16[1,32,384]{2,1,0:T(8,128)(2,1)}, bf16[1,32,384]{2,1,0:T(8,128)(2,1)S(1)}, u32[]{:S(2)}, u32[]{:S(2)}) collective-permute-start(bf16[1,32,384]{2,1,0:T(8,128)(2,1)} %bitcast.12), channel_id=1, source_target_pairs={{0,256},{128,384},{256,0},{384,128},{1,257},{129,385},{257,1},{385... | collective-permute-start | bytes 73736 | tf_op jit(solution)/shard_map/ppermute | solution.py:24
  27.5 0.7 copy-start.2
  28.3 18.6 %collective-permute-start.6 = (bf16[672,512]{1,0:T(8,128)(2,1)S(1)}, bf16[672,512]{1,0:T(8,128)(2,1)S(1)}, u32[]{:S(2)}, u32[]{:S(2)}) collective-permute-start(bf16[672,512]{1,0:T(8,128)(2,1)S(1)} %shard_map.66.refs_3_), channel_id=1, source_target_pairs={{0,128},{128,0},{256,384},{384,256},{1,129},{129,1},{257,385},{385... | collective-permute-start | bytes 2064392 | tf_op jit(solution)/shard_map/ppermute | solution.py:24
  31.5 16.5 %collective-permute-start.5 = (bf16[672,512]{1,0:T(8,128)(2,1)S(1)}, bf16[672,512]{1,0:T(8,128)(2,1)S(1)}, u32[]{:S(2)}, u32[]{:S(2)}) collective-permute-start(bf16[672,512]{1,0:T(8,128)(2,1)S(1)} %shard_map.66.refs_3_), channel_id=1, source_target_pairs={{128,256},{256,128},{129,257},{257,129},{130,258},{258,130},{131,2... | collective-permute-start | bytes 2064392 | tf_op jit(solution)/shard_map/ppermute | solution.py:28
  32.3 6.2 %collective-permute-start.7 = (bf16[2,32,384]{2,1,0:T(8,128)(2,1)S(1)}, bf16[2,32,384]{2,1,0:T(8,128)(2,1)S(1)}, u32[]{:S(2)}, u32[]{:S(2)}) collective-permute-start(bf16[2,32,384]{2,1,0:T(8,128)(2,1)S(1)} %shard_map.65.refs_0_), channel_id=1, source_target_pairs={{0,32},{32,0},{64,96},{96,64},{1,33},{33,1},{65,97},{97,65},{2,34}... | collective-permute-start | bytes 147464 | tf_op jit(solution)/shard_map/ppermute | solution.py:24
  38.4 10.3 %collective-permute-start.8 = (bf16[4,32,384]{2,1,0:T(8,128)(2,1)S(1)}, bf16[4,32,384]{2,1,0:T(8,128)(2,1)S(1)}, u32[]{:S(2)}, u32[]{:S(2)}) collective-permute-start(bf16[4,32,384]{2,1,0:T(8,128)(2,1)S(1)} %shard_map.68.refs_0_), channel_id=1, source_target_pairs={{0,96},{32,64},{64,32},{96,0},{1,97},{33,65},{65,33},{97,1},{2,98}... | collective-permute-start | bytes 294920 | tf_op jit(solution)/shard_map/ppermute | solution.py:24
  48.8 11.8 %collective-permute-start.9 = (f32[2,136,256]{2,1,0:T(8,128)S(1)}, f32[2,136,256]{2,1,0:T(8,128)S(1)}, u32[]{:S(2)}, u32[]{:S(2)}) collective-permute-start(f32[2,136,256]{2,1,0:T(8,128)S(1)} %get-tuple-element.42), channel_id=1, source_target_pairs={{0,8},{8,0},{1,9},{9,1},{2,10},{10,2},{3,11},{11,3},{4,12},{12,4},... | collective-permute-start | bytes 835592 | tf_op jit(solution)/shard_map/ppermute | solution.py:24
  50.7 9.8 %collective-permute-start.10 = (f32[2,136,256]{2,1,0:T(8,128)S(1)}, f32[2,136,256]{2,1,0:T(8,128)S(1)}, u32[]{:S(2)}, u32[]{:S(2)}) collective-permute-start(f32[2,136,256]{2,1,0:T(8,128)S(1)} %get-tuple-element.41), channel_id=1, source_target_pairs={{8,16},{16,8},{9,17},{17,9},{10,18},{18,10},{11,19},{19,11},{12,20... | collective-permute-start | bytes 835592 | tf_op jit(solution)/shard_map/ppermute | solution.py:292
  53.8 14.1 %collective-permute-start.12 = (bf16[8,32,384]{2,1,0:T(8,128)(2,1)S(1)}, bf16[8,32,384]{2,1,0:T(8,128)(2,1)S(1)}, u32[]{:S(2)}, u32[]{:S(2)}) collective-permute-start(bf16[8,32,384]{2,1,0:T(8,128)(2,1)S(1)} %shard_map.74.refs_0_), channel_id=1, source_target_pairs={{0,128},{128,0},{256,384},{384,256},{1,129},{129,1},{257,385},{385... | collective-permute-start | bytes 589832 | tf_op jit(solution)/shard_map/ppermute | solution.py:24
  61.2 10.8 %collective-permute-start.11 = (bf16[224,256]{1,0:T(8,128)(2,1)S(1)}, bf16[224,256]{1,0:T(8,128)(2,1)S(1)}, u32[]{:S(2)}, u32[]{:S(2)}) collective-permute-start(bf16[224,256]{1,0:T(8,128)(2,1)S(1)} %shard_map.72), channel_id=1, source_target_pairs={{0,1},{1,0},{2,3},{3,2},{4,5},{5,4},{6,7},{7,6},{8,9},{9,8},{10,11... | collective-permute-start | bytes 344072 | tf_op jit(solution)/shard_map/ppermute | solution.py:24
  67.9 17.8 %collective-permute-start.13 = (bf16[16,32,384]{2,1,0:T(8,128)(2,1)S(1)}, bf16[16,32,384]{2,1,0:T(8,128)(2,1)S(1)}, u32[]{:S(2)}, u32[]{:S(2)}) collective-permute-start(bf16[16,32,384]{2,1,0:T(8,128)(2,1)S(1)} %shard_map.75.refs_0_), channel_id=1, source_target_pairs={{0,16},{16,0},{1,17},{17,1},{2,18},{18,2},{3,19},{19,3},{4,20},{20... | collective-permute-start | bytes 1179656 | tf_op jit(solution)/shard_map/ppermute | solution.py:24
  72.0 16.8 %copy-start.5 = (f32[384]{0:T(512)S(1)}, f32[384]{0:T(512)}, u32[]{:S(2)}) copy-start(f32[384]{0:T(512)} %param.11) | copy-start | bytes 4612
  85.8 5.0 %collective-permute-start.14 = (bf16[32,32,384]{2,1,0:T(8,128)(2,1)S(1)}, bf16[32,32,384]{2,1,0:T(8,128)(2,1)S(1)}, u32[]{:S(2)}, u32[]{:S(2)}) collective-permute-start(bf16[32,32,384]{2,1,0:T(8,128)(2,1)S(1)} %shard_map.76.mine_ref), channel_id=1, source_target_pairs={{0,8},{8,0},{1,9},{9,1},{2,10},{10,2},{3,11},{11,3},{4,12},{12,4},... | collective-permute-start | bytes 2359304 | tf_op jit(solution)/shard_map/ppermute | solution.py:24

commit v7 on v6

--- a/solution.py
+++ b/solution.py
@@ -220,20 +220,8 @@
         lax.fori_loop(0, mine_ref.shape[0], one_block, 0, unroll=4)
 
 
-def arranged_weight(pos, mine, other):
-    vmem = pl.BlockSpec(memory_space=pltpu.VMEM)
-    return pl.pallas_call(
-        arrange_kernel,
-        out_shape=jax.ShapeDtypeStruct(
-            (2 * mine.shape[0] * mine.shape[1], mine.shape[2]), mine.dtype
-        ),
-        in_specs=[pl.BlockSpec(memory_space=pltpu.SMEM), vmem, vmem],
-        out_specs=vmem,
-        compiler_params=pltpu.CompilerParams(vmem_limit_bytes=VMEM_LIMIT),
-    )(pos, mine, other)
-
-
-def project_kernel(groups, pos_ref, rows_ref, weight_ref, gate_ref, out_ref):
+def project_kernel(groups, pos_ref, rows_ref, mine_ref, other_ref, gate_ref, out_ref, weight_ref):
+    arrange_kernel(pos_ref, mine_ref, other_ref, weight_ref)
     depth = rows_ref.shape[3]
     total = jnp.zeros(out_ref.shape, jnp.float32)
     for x in range(groups):
@@ -244,15 +232,17 @@
     out_ref[...] = (total * gate_ref[...]).astype(jnp.bfloat16)
 
 
-def project(pos, rows, weight, gate):
+def project(pos, rows, mine, other, gate):
     vmem = pl.BlockSpec(memory_space=pltpu.VMEM)
+    depth, width = 2 * mine.shape[0] * mine.shape[1], mine.shape[2]
     return pl.pallas_call(
         functools.partial(project_kernel, rows.shape[0]),
-        out_shape=jax.ShapeDtypeStruct((rows.shape[2], weight.shape[1]), jnp.bfloat16),
-        in_specs=[pl.BlockSpec(memory_space=pltpu.SMEM), vmem, vmem, vmem],
+        out_shape=jax.ShapeDtypeStruct((rows.shape[2], width), jnp.bfloat16),
+        in_specs=[pl.BlockSpec(memory_space=pltpu.SMEM), vmem, vmem, vmem, vmem],
         out_specs=vmem,
-        compiler_params=pltpu.CompilerParams(vmem_limit_bytes=VMEM_LIMIT),
-    )(pos, rows, weight, gate)
+        scratch_shapes=[pltpu.VMEM((depth, width), mine.dtype)],
+        compiler_params=pltpu.CompilerParams(vmem_limit_bytes=VMEM_LIMIT),
+    )(pos, rows, mine, other, gate)
 
 
 def after(value, other):
@@ -300,8 +290,7 @@
     weight_w = swapped(weight, "w", 1)
     rows = lax.all_gather(joined(attended[None], across[None]), "x", axis=0, tiled=False)
     weight = joined(weight, after(weight_w, rows))
-    weight = arranged_weight(pos, weight, swapped(weight, "c", 1))
-    return project(pos, rows, weight, gate_scale[None, :])
+    return project(pos, rows, weight, swapped(weight, "c", 1), gate_scale[None, :])
 
 
 def solution(mesh):

time: 94.8 us -> 93.1 us (0.982)
  waiting for transfers between devices: 14.7 us -> 13.7 us
    ppermute x11, starting transfers between devices: 47 us -> 45.4 us  [swapped(): return lax.ppermute(value, axis, [(i, i ^ flip) for i in range(count)])]
    ppermute x1, starting transfers between devices: 3.03 us -> 4.43 us  [local(): from_face = lax.ppermute(given[:, :, LANES:], ('w', 'c'), facing)]
    pallas_call x1 -> x0, Pallas kernels: 1.11 us -> none  [arranged_weight(): pl.pallas_call(arrange_kernel, out_shape=jax.ShapeDtypeStruct((2 * mine.s...]
    ppermute x11, waiting for transfers between devices: 14.6 us -> 13.7 us  [swapped(): return lax.ppermute(value, axis, [(i, i ^ flip) for i in range(count)])]
where the time goes in v7:
time: 93.1 us; the launch traced here: 91.7 us
  starting transfers between devices  54.4 us (58%)
  waiting for transfers between devices  13.7 us (15%)
  blocking collectives  13.6 us (15%)
  Pallas kernels  7.2 us (8%)
  local copies, waits for them, and re-layouts  2.52 us (3%)
    ppermute x11, starting transfers between devices, swapped(): return lax.ppermute(value, axis, [(i, i ^ flip) for i in range(count)])  45.4 us
    ppermute x11, waiting for transfers between devices, swapped(): return lax.ppermute(value, axis, [(i, i ^ flip) for i in range(count)])  13.7 us
    all_gather x1, blocking collectives, local(): lax.all_gather(joined(attended[None], across[None]), 'x', axis=0, tiled=F...  13.6 us
    ppermute x1, starting transfers between devices, local(): from_face = lax.ppermute(given[:, :, LANES:], ('w', 'c'), facing)  4.43 us
    pallas_call x4, Pallas kernels, attend(): pl.pallas_call(functools.partial(attend_kernel, low, high, stage), out_sh...  3.84 us
    ppermute x1, starting transfers between devices, local(): lax.ppermute(queries, ('w', 'c'), facing)  3 us
    pallas_call x1, Pallas kernels, project(): pl.pallas_call(functools.partial(project_kernel, rows.shape[0]), out_shap...  2.43 us
    unnamed x12, local copies, waits for them, and re-layouts  2.4 us
  transfers between devices with their start and end apart: 15, of which 5 were waited for; matrix products, arithmetic and copies ran while one was open for 0% of the time, Pallas kernels for 5%

profile of v7, /device:TPU:1, one launch (start us, length us, event | category | flops | bytes accessed | tf_op | source)
XLA Modules:
  0.0 91.7 jit_solution(12142858516803485183)
XLA Ops:
  0.0 0.0 copy-start
  0.0 0.9 copy-done
  0.9 0.0 copy-start.1
  0.9 0.9 copy-done.1
  1.8 0.0 copy-start.4
  1.8 0.0 copy-start.2
  1.8 0.8 collective-permute-start
  2.7 13.0 %collective-permute-start.4 = (bf16[224,512]{1,0:T(8,128)(2,1)S(1)}, bf16[224,512]{1,0:T(8,128)(2,1)S(1)}, u32[]{:S(2)}, u32[]{:S(2)}) collective-permute-start(bf16[224,512]{1,0:T(8,128)(2,1)S(1)} %shard_map.64.refs_0_), channel_id=1, source_target_pairs={{0,32},{32,0},{64,96},{96,64},{1,33},{33,1},{65,97},{97,65},{2,34}... | collective-permute-start | bytes 688136 | tf_op jit(solution)/shard_map/ppermute | solution.py:24
  15.7 0.0 copy-done.4
  15.7 3.1 %collective-permute-start.1 = (bf16[224,256]{1,0:T(8,128)(2,1)S(1)}, bf16[224,256]{1,0:T(8,128)(2,1)S(1)}, u32[]{:S(2)}, u32[]{:S(2)}) collective-permute-start(bf16[224,256]{1,0:T(8,128)(2,1)S(1)} %copy-done.4), channel_id=1, source_target_pairs={{0,8},{8,0},{1,9},{9,1},{2,10},{10,2},{3,11},{11,3},{4,12},{12,4},... | collective-permute-start | bytes 344072 | tf_op jit(solution)/shard_map/ppermute | solution.py:24
  18.8 3.0 %collective-permute-start.2 = (bf16[224,256]{1,0:T(8,128)(2,1)S(1)}, bf16[224,256]{1,0:T(8,128)(2,1)S(1)}, u32[]{:S(2)}, u32[]{:S(2)}) collective-permute-start(bf16[224,256]{1,0:T(8,128)(2,1)S(1)} %copy-done.4), channel_id=1, source_target_pairs={{8,16},{16,8},{9,17},{17,9},{10,18},{18,10},{11,19},{19,11},{12,20... | collective-permute-start | bytes 344072 | tf_op jit(solution)/shard_map/ppermute | solution.py:262
  21.8 0.0 copy-done.2
  21.8 4.2 %collective-permute-start.3 = (bf16[1,32,384]{2,1,0:T(8,128)(2,1)S(1)}, bf16[1,32,384]{2,1,0:T(8,128)(2,1)S(1)}, u32[]{:S(2)}, u32[]{:S(2)}) collective-permute-start(bf16[1,32,384]{2,1,0:T(8,128)(2,1)S(1)} %bitcast.12), channel_id=1, source_target_pairs={{0,256},{128,384},{256,0},{384,128},{1,257},{129,385},{257,1},{385... | collective-permute-start | bytes 73736 | tf_op jit(solution)/shard_map/ppermute | solution.py:24
  26.1 1.2 %collective-permute-done.3.refs_1_ = bf16[1,32,384]{2,1,0:T(8,128)(2,1)S(1)} collective-permute-done((bf16[1,32,384]{2,1,0:T(8,128)(2,1)S(1)}, bf16[1,32,384]{2,1,0:T(8,128)(2,1)S(1)}, u32[]{:S(2)}, u32[]{:S(2)}) %collective-permute-start.3) | collective-permute-done | bytes 24608 | tf_op jit(solution)/shard_map/ppermute | solution.py:24
  27.3 0.0 collective-permute-done.1.refs_1_
  27.3 0.0 collective-permute-done.2.refs_2_
  27.3 0.0 collective-permute-done.refs_2_
  27.3 0.0 collective-permute-done.4.refs_1_
  27.4 3.2 %collective-permute-start.6 = (bf16[672,512]{1,0:T(8,128)(2,1)S(1)}, bf16[672,512]{1,0:T(8,128)(2,1)S(1)}, u32[]{:S(2)}, u32[]{:S(2)}) collective-permute-start(bf16[672,512]{1,0:T(8,128)(2,1)S(1)} %shard_map.66.refs_3_), channel_id=1, source_target_pairs={{0,128},{128,0},{256,384},{384,256},{1,129},{129,1},{257,385},{385... | collective-permute-start | bytes 2064392 | tf_op jit(solution)/shard_map/ppermute | solution.py:24
  30.6 0.7 collective-permute-start.5
  31.3 2.5 %collective-permute-start.7 = (bf16[2,32,384]{2,1,0:T(8,128)(2,1)S(1)}, bf16[2,32,384]{2,1,0:T(8,128)(2,1)S(1)}, u32[]{:S(2)}, u32[]{:S(2)}) collective-permute-start(bf16[2,32,384]{2,1,0:T(8,128)(2,1)S(1)} %shard_map.65.refs_0_), channel_id=1, source_target_pairs={{0,32},{32,0},{64,96},{96,64},{1,33},{33,1},{65,97},{97,65},{2,34}... | collective-permute-start | bytes 147464 | tf_op jit(solution)/shard_map/ppermute | solution.py:24
  33.8 0.0 copy-start.3
  33.8 0.1 stack.23.pos_ref
  33.9 0.6 copy-done.3
  34.5 1.9 %shard_map.67 = (f32[2,136,768]{2,1,0:T(8,128)S(1)}, bf16[768,256]{1,0:T(8,128)(2,1)S(1)}) custom-call(s32[5]{0:T(128)S(1)} %stack.23.pos_ref, s32[2,3]{1,0:T(2,128)S(1)} %copy-done.3, bf16[224,256]{1,0:T(8,128)(2,1)S(1)} %copy-done.4, bf16[224,256]{1,0:T(8,128)(2,1)S(1)} %collective-permute-done.1.refs_1_, ...), custom_call_target="tpu_custom_call" | custom-call | flops 462422016 | bytes 688128 | tf_op jit(solution)/shard_map/pallas_call | solution.py:167
  36.4 1.2 %collective-permute-done.7.refs_1_ = bf16[2,32,384]{2,1,0:T(8,128)(2,1)S(1)} collective-permute-done((bf16[2,32,384]{2,1,0:T(8,128)(2,1)S(1)}, bf16[2,32,384]{2,1,0:T(8,128)(2,1)S(1)}, u32[]{:S(2)}, u32[]{:S(2)}) %collective-permute-start.7) | collective-permute-done | bytes 49184 | tf_op jit(solution)/shard_map/ppermute | solution.py:24
  37.7 2.3 %collective-permute-start.8 = (bf16[4,32,384]{2,1,0:T(8,128)(2,1)S(1)}, bf16[4,32,384]{2,1,0:T(8,128)(2,1)S(1)}, u32[]{:S(2)}, u32[]{:S(2)}) collective-permute-start(bf16[4,32,384]{2,1,0:T(8,128)(2,1)S(1)} %shard_map.68.refs_0_), channel_id=1, source_target_pairs={{0,96},{32,64},{64,32},{96,0},{1,97},{33,65},{65,33},{97,1},{2,98}... | collective-permute-start | bytes 294920 | tf_op jit(solution)/shard_map/ppermute | solution.py:24
  40.0 6.0 %collective-permute-done.6.refs_1_ = bf16[672,512]{1,0:T(8,128)(2,1)S(1)} collective-permute-done((bf16[672,512]{1,0:T(8,128)(2,1)S(1)}, bf16[672,512]{1,0:T(8,128)(2,1)S(1)}, u32[]{:S(2)}, u32[]{:S(2)}) %collective-permute-start.6) | collective-permute-done | bytes 688160 | tf_op jit(solution)/shard_map/ppermute | solution.py:24
  46.0 0.7 shard_map.69.refs_2_
  46.7 0.0 collective-permute-done.5.refs_1_
  46.7 0.6 shard_map.70
  47.4 0.0 collective-permute-done.8.refs_1_
  47.4 1.9 %collective-permute-start.9 = (f32[2,136,256]{2,1,0:T(8,128)S(1)}, f32[2,136,256]{2,1,0:T(8,128)S(1)}, u32[]{:S(2)}, u32[]{:S(2)}) collective-permute-start(f32[2,136,256]{2,1,0:T(8,128)S(1)} %get-tuple-element.42), channel_id=1, source_target_pairs={{0,8},{8,0},{1,9},{9,1},{2,10},{10,2},{3,11},{11,3},{4,12},{12,4},... | collective-permute-start | bytes 835592 | tf_op jit(solution)/shard_map/ppermute | solution.py:24
  49.4 4.4 %collective-permute-start.10 = (f32[2,136,256]{2,1,0:T(8,128)S(1)}, f32[2,136,256]{2,1,0:T(8,128)S(1)}, u32[]{:S(2)}, u32[]{:S(2)}) collective-permute-start(f32[2,136,256]{2,1,0:T(8,128)S(1)} %get-tuple-element.41), channel_id=1, source_target_pairs={{8,16},{16,8},{9,17},{17,9},{10,18},{18,10},{11,19},{19,11},{12,20... | collective-permute-start | bytes 835592 | tf_op jit(solution)/shard_map/ppermute | solution.py:282
  53.8 5.7 %collective-permute-start.12 = (bf16[8,32,384]{2,1,0:T(8,128)(2,1)S(1)}, bf16[8,32,384]{2,1,0:T(8,128)(2,1)S(1)}, u32[]{:S(2)}, u32[]{:S(2)}) collective-permute-start(bf16[8,32,384]{2,1,0:T(8,128)(2,1)S(1)} %shard_map.74.refs_0_), channel_id=1, source_target_pairs={{0,128},{128,0},{256,384},{384,256},{1,129},{129,1},{257,385},{385... | collective-permute-start | bytes 589832 | tf_op jit(solution)/shard_map/ppermute | solution.py:24
  59.5 0.6 shard_map.71.own_ref
  60.2 0.0 collective-permute-done.9.core_ref
  60.2 0.0 collective-permute-done.10.face_ref
  60.2 0.7 shard_map.72
  60.9 5.2 %collective-permute-start.11 = (bf16[224,256]{1,0:T(8,128)(2,1)S(1)}, bf16[224,256]{1,0:T(8,128)(2,1)S(1)}, u32[]{:S(2)}, u32[]{:S(2)}) collective-permute-start(bf16[224,256]{1,0:T(8,128)(2,1)S(1)} %shard_map.72), channel_id=1, source_target_pairs={{0,1},{1,0},{2,3},{3,2},{4,5},{5,4},{6,7},{7,6},{8,9},{9,8},{10,11... | collective-permute-start | bytes 344072 | tf_op jit(solution)/shard_map/ppermute | solution.py:24
  66.1 0.0 collective-permute-done.12.refs_1_
  66.1 1.9 %collective-permute-start.13 = (bf16[16,32,384]{2,1,0:T(8,128)(2,1)S(1)}, bf16[16,32,384]{2,1,0:T(8,128)(2,1)S(1)}, u32[]{:S(2)}, u32[]{:S(2)}) collective-permute-start(bf16[16,32,384]{2,1,0:T(8,128)(2,1)S(1)} %shard_map.75.refs_0_), channel_id=1, source_target_pairs={{0,16},{16,0},{1,17},{17,1},{2,18},{18,2},{3,19},{19,3},{4,20},{20... | collective-permute-start | bytes 1179656 | tf_op jit(solution)/shard_map/ppermute | solution.py:24
  68.0 3.3 %collective-permute-done.11 = bf16[224,256]{1,0:T(8,128)(2,1)S(1)} collective-permute-done((bf16[224,256]{1,0:T(8,128)(2,1)S(1)}, bf16[224,256]{1,0:T(8,128)(2,1)S(1)}, u32[]{:S(2)}, u32[]{:S(2)}) %collective-permute-start.11) | collective-permute-done | bytes 114720 | tf_op jit(solution)/shard_map/ppermute | solution.py:24
  71.4 13.6 %all-gather = bf16[8,224,256]{2,1,0:T(8,128)(2,1)S(1)} all-gather(bf16[2,224,256]{2,1,0:T(8,128)(2,1)S(1)} %shard_map.73), channel_id=2, replica_groups=mesh['t'=4,'u'=4,'w'=2,'c'=2,'x'=4,'h'=2] {'x'}, dimensions={0}, use_global_device_ids=true | all-gather | bytes 1146880 | tf_op jit(solution)/shard_map/all_gather | solution.py:291
  85.0 0.0 collective-permute-done.13.refs_1_
  85.0 0.0 copy-start.5
  85.0 0.1 shard_map.76.mine_ref
  85.0 2.3 %collective-permute-start.14 = (bf16[32,32,384]{2,1,0:T(8,128)(2,1)S(1)}, bf16[32,32,384]{2,1,0:T(8,128)(2,1)S(1)}, u32[]{:S(2)}, u32[]{:S(2)}) collective-permute-start(bf16[32,32,384]{2,1,0:T(8,128)(2,1)S(1)} %shard_map.76.mine_ref), channel_id=1, source_target_pairs={{0,8},{8,0},{1,9},{9,1},{2,10},{10,2},{3,11},{11,3},{4,12},{12,4},... | collective-permute-start | bytes 2359304 | tf_op jit(solution)/shard_map/ppermute | solution.py:24
  87.4 0.0 copy-done.5
  87.4 1.9 %collective-permute-done.14.other_ref = bf16[32,32,384]{2,1,0:T(8,128)(2,1)S(1)} collective-permute-done((bf16[32,32,384]{2,1,0:T(8,128)(2,1)S(1)}, bf16[32,32,384]{2,1,0:T(8,128)(2,1)S(1)}, u32[]{:S(2)}, u32[]{:S(2)}) %collective-permute-start.14) | collective-permute-done | bytes 786464 | tf_op jit(solution)/shard_map/ppermute | solution.py:24
  89.2 2.4 %shard_map.77 = bf16[224,384]{1,0:T(8,128)(2,1)} custom-call(s32[5]{0:T(128)S(1)} %stack.23.pos_ref, bf16[4,2,224,256]{3,2,1,0:T(8,128)(2,1)S(1)} %bitcast.9, bf16[32,32,384]{2,1,0:T(8,128)(2,1)S(1)} %shard_map.76.mine_ref, bf16[32,32,384]{2,1,0:T(8,128)(2,1)S(1)} %collective-permute-done.14.other_ref, f32[1,384]{1,0:T(1,128)S(1)} %broadcast_in_dim.15.gate_ref), custom_call_target="tpu_custom_call" | custom-call | tf_op jit(solution)/shard_map/pallas_call | solution.py:238
  (9 shorter events, 0.2 us)
Async XLA Ops:
  0.0 0.9 copy-start
  0.9 0.9 copy-start.1
  1.8 13.9 %copy-start.4 = (bf16[224,256]{1,0:T(8,128)(2,1)S(1)}, bf16[224,256]{1,0:T(8,128)(2,1)}, u32[]{:S(2)}) copy-start(bf16[224,256]{1,0:T(8,128)(2,1)} %refs_0_) | copy-start | bytes 344068
  1.8 20.0 %copy-start.2 = (bf16[32,384]{1,0:T(8,128)(2,1)S(1)}, bf16[32,384]{1,0:T(8,128)(2,1)}, u32[]{:S(2)}) copy-start(bf16[32,384]{1,0:T(8,128)(2,1)} %param.10) | copy-start | bytes 73732
  1.8 25.5 %collective-permute-start = (bf16[224,512]{1,0:T(8,128)(2,1)S(1)}, bf16[224,512]{1,0:T(8,128)(2,1)S(1)}, u32[]{:S(2)}, u32[]{:S(2)}) collective-permute-start(bf16[224,512]{1,0:T(8,128)(2,1)S(1)} %shard_map.64.refs_0_), channel_id=1, source_target_pairs={{32,64},{64,32},{33,65},{65,33},{34,66},{66,34},{35,67},{67,35},{3... | collective-permute-start | bytes 688136 | tf_op jit(solution)/shard_map/ppermute | solution.py:28
  2.7 24.7 %collective-permute-start.4 = (bf16[224,512]{1,0:T(8,128)(2,1)S(1)}, bf16[224,512]{1,0:T(8,128)(2,1)S(1)}, u32[]{:S(2)}, u32[]{:S(2)}) collective-permute-start(bf16[224,512]{1,0:T(8,128)(2,1)S(1)} %shard_map.64.refs_0_), channel_id=1, source_target_pairs={{0,32},{32,0},{64,96},{96,64},{1,33},{33,1},{65,97},{97,65},{2,34}... | collective-permute-start | bytes 688136 | tf_op jit(solution)/shard_map/ppermute | solution.py:24
  15.7 11.6 %collective-permute-start.1 = (bf16[224,256]{1,0:T(8,128)(2,1)S(1)}, bf16[224,256]{1,0:T(8,128)(2,1)S(1)}, u32[]{:S(2)}, u32[]{:S(2)}) collective-permute-start(bf16[224,256]{1,0:T(8,128)(2,1)S(1)} %copy-done.4), channel_id=1, source_target_pairs={{0,8},{8,0},{1,9},{9,1},{2,10},{10,2},{3,11},{11,3},{4,12},{12,4},... | collective-permute-start | bytes 344072 | tf_op jit(solution)/shard_map/ppermute | solution.py:24
  18.8 8.5 %collective-permute-start.2 = (bf16[224,256]{1,0:T(8,128)(2,1)S(1)}, bf16[224,256]{1,0:T(8,128)(2,1)S(1)}, u32[]{:S(2)}, u32[]{:S(2)}) collective-permute-start(bf16[224,256]{1,0:T(8,128)(2,1)S(1)} %copy-done.4), channel_id=1, source_target_pairs={{8,16},{16,8},{9,17},{17,9},{10,18},{18,10},{11,19},{19,11},{12,20... | collective-permute-start | bytes 344072 | tf_op jit(solution)/shard_map/ppermute | solution.py:262
  21.8 5.5 %collective-permute-start.3 = (bf16[1,32,384]{2,1,0:T(8,128)(2,1)S(1)}, bf16[1,32,384]{2,1,0:T(8,128)(2,1)S(1)}, u32[]{:S(2)}, u32[]{:S(2)}) collective-permute-start(bf16[1,32,384]{2,1,0:T(8,128)(2,1)S(1)} %bitcast.12), channel_id=1, source_target_pairs={{0,256},{128,384},{256,0},{384,128},{1,257},{129,385},{257,1},{385... | collective-permute-start | bytes 73736 | tf_op jit(solution)/shard_map/ppermute | solution.py:24
  27.4 18.6 %collective-permute-start.6 = (bf16[672,512]{1,0:T(8,128)(2,1)S(1)}, bf16[672,512]{1,0:T(8,128)(2,1)S(1)}, u32[]{:S(2)}, u32[]{:S(2)}) collective-permute-start(bf16[672,512]{1,0:T(8,128)(2,1)S(1)} %shard_map.66.refs_3_), channel_id=1, source_target_pairs={{0,128},{128,0},{256,384},{384,256},{1,129},{129,1},{257,385},{385... | collective-permute-start | bytes 2064392 | tf_op jit(solution)/shard_map/ppermute | solution.py:24
  30.6 16.1 %collective-permute-start.5 = (bf16[672,512]{1,0:T(8,128)(2,1)S(1)}, bf16[672,512]{1,0:T(8,128)(2,1)S(1)}, u32[]{:S(2)}, u32[]{:S(2)}) collective-permute-start(bf16[672,512]{1,0:T(8,128)(2,1)S(1)} %shard_map.66.refs_3_), channel_id=1, source_target_pairs={{128,256},{256,128},{129,257},{257,129},{130,258},{258,130},{131,2... | collective-permute-start | bytes 2064392 | tf_op jit(solution)/shard_map/ppermute | solution.py:28
  31.3 6.4 %collective-permute-start.7 = (bf16[2,32,384]{2,1,0:T(8,128)(2,1)S(1)}, bf16[2,32,384]{2,1,0:T(8,128)(2,1)S(1)}, u32[]{:S(2)}, u32[]{:S(2)}) collective-permute-start(bf16[2,32,384]{2,1,0:T(8,128)(2,1)S(1)} %shard_map.65.refs_0_), channel_id=1, source_target_pairs={{0,32},{32,0},{64,96},{96,64},{1,33},{33,1},{65,97},{97,65},{2,34}... | collective-permute-start | bytes 147464 | tf_op jit(solution)/shard_map/ppermute | solution.py:24
  33.8 0.7 copy-start.3
  37.7 9.7 %collective-permute-start.8 = (bf16[4,32,384]{2,1,0:T(8,128)(2,1)S(1)}, bf16[4,32,384]{2,1,0:T(8,128)(2,1)S(1)}, u32[]{:S(2)}, u32[]{:S(2)}) collective-permute-start(bf16[4,32,384]{2,1,0:T(8,128)(2,1)S(1)} %shard_map.68.refs_0_), channel_id=1, source_target_pairs={{0,96},{32,64},{64,32},{96,0},{1,97},{33,65},{65,33},{97,1},{2,98}... | collective-permute-start | bytes 294920 | tf_op jit(solution)/shard_map/ppermute | solution.py:24
  47.4 12.7 %collective-permute-start.9 = (f32[2,136,256]{2,1,0:T(8,128)S(1)}, f32[2,136,256]{2,1,0:T(8,128)S(1)}, u32[]{:S(2)}, u32[]{:S(2)}) collective-permute-start(f32[2,136,256]{2,1,0:T(8,128)S(1)} %get-tuple-element.42), channel_id=1, source_target_pairs={{0,8},{8,0},{1,9},{9,1},{2,10},{10,2},{3,11},{11,3},{4,12},{12,4},... | collective-permute-start | bytes 835592 | tf_op jit(solution)/shard_map/ppermute | solution.py:24
  49.4 10.8 %collective-permute-start.10 = (f32[2,136,256]{2,1,0:T(8,128)S(1)}, f32[2,136,256]{2,1,0:T(8,128)S(1)}, u32[]{:S(2)}, u32[]{:S(2)}) collective-permute-start(f32[2,136,256]{2,1,0:T(8,128)S(1)} %get-tuple-element.41), channel_id=1, source_target_pairs={{8,16},{16,8},{9,17},{17,9},{10,18},{18,10},{11,19},{19,11},{12,20... | collective-permute-start | bytes 835592 | tf_op jit(solution)/shard_map/ppermute | solution.py:282
  53.8 12.2 %collective-permute-start.12 = (bf16[8,32,384]{2,1,0:T(8,128)(2,1)S(1)}, bf16[8,32,384]{2,1,0:T(8,128)(2,1)S(1)}, u32[]{:S(2)}, u32[]{:S(2)}) collective-permute-start(bf16[8,32,384]{2,1,0:T(8,128)(2,1)S(1)} %shard_map.74.refs_0_), channel_id=1, source_target_pairs={{0,128},{128,0},{256,384},{384,256},{1,129},{129,1},{257,385},{385... | collective-permute-start | bytes 589832 | tf_op jit(solution)/shard_map/ppermute | solution.py:24
  60.9 10.5 %collective-permute-start.11 = (bf16[224,256]{1,0:T(8,128)(2,1)S(1)}, bf16[224,256]{1,0:T(8,128)(2,1)S(1)}, u32[]{:S(2)}, u32[]{:S(2)}) collective-permute-start(bf16[224,256]{1,0:T(8,128)(2,1)S(1)} %shard_map.72), channel_id=1, source_target_pairs={{0,1},{1,0},{2,3},{3,2},{4,5},{5,4},{6,7},{7,6},{8,9},{9,8},{10,11... | collective-permute-start | bytes 344072 | tf_op jit(solution)/shard_map/ppermute | solution.py:24
  66.1 18.9 %collective-permute-start.13 = (bf16[16,32,384]{2,1,0:T(8,128)(2,1)S(1)}, bf16[16,32,384]{2,1,0:T(8,128)(2,1)S(1)}, u32[]{:S(2)}, u32[]{:S(2)}) collective-permute-start(bf16[16,32,384]{2,1,0:T(8,128)(2,1)S(1)} %shard_map.75.refs_0_), channel_id=1, source_target_pairs={{0,16},{16,0},{1,17},{17,1},{2,18},{18,2},{3,19},{19,3},{4,20},{20... | collective-permute-start | bytes 1179656 | tf_op jit(solution)/shard_map/ppermute | solution.py:24
  85.0 2.4 %copy-start.5 = (f32[384]{0:T(512)S(1)}, f32[384]{0:T(512)}, u32[]{:S(2)}) copy-start(f32[384]{0:T(512)} %param.11) | copy-start | bytes 4612
  85.0 4.2 %collective-permute-start.14 = (bf16[32,32,384]{2,1,0:T(8,128)(2,1)S(1)}, bf16[32,32,384]{2,1,0:T(8,128)(2,1)S(1)}, u32[]{:S(2)}, u32[]{:S(2)}) collective-permute-start(bf16[32,32,384]{2,1,0:T(8,128)(2,1)S(1)} %shard_map.76.mine_ref), channel_id=1, source_target_pairs={{0,8},{8,0},{1,9},{9,1},{2,10},{10,2},{3,11},{11,3},{4,12},{12,4},... | collective-permute-start | bytes 2359304 | tf_op jit(solution)/shard_map/ppermute | solution.py:24
